TPU v7x, 32 devices: a whole 2x2x4 slice. The times are simulated.
32 devices in a mesh: ctx: 8 (over z, x), blk: 4 (over y, core).
Axes of the slice: x: 2, y: 2, z: 4, core: 2. Of those that a mesh axis runs over, the one named last changes fastest.
Arguments:
- layer_in: bfloat16 [16, 4096, 256], P('ctx', 'blk'), may hold values from -6 to 6
- matrices: bfloat16 [3072, 256], P(('ctx', 'blk')), may hold values from -2 to 2
- vectors: bfloat16 [2304], P(('ctx', 'blk')), may hold values from -2 to 2
- out_grad: bfloat16 [16, 4096, 256], P('ctx', 'blk'), may hold values from -6 to 6
Outputs:
- layer_out: bfloat16 [16, 4096, 256], P('ctx', 'blk')
- layer_grad: bfloat16 [16, 4096, 256], P('ctx', 'blk')
- matrices_grad: float32 [3072, 256], P(('ctx', 'blk'))
- vectors_grad: float32 [2304], P(('ctx', 'blk'))
All inputs are finite; a program needn't handle non-finite values.
Results may differ from a plain program's by a relative error of at most 0.015.
Values may be sent and summed in bfloat16 or wider, within the bound.
A program may use at most 128 MiB of HBM per device.

v0:
```python
import math

import jax
import jax.numpy as jnp
from jax import lax
from jax.sharding import PartitionSpec as P

HEADS = 4
HEAD_DIM = 64


EPSILON = 1e-05


def normalize(inputs):
    centre = jnp.mean(inputs, -1, keepdims=True)
    shifted = inputs - centre
    inverse = lax.rsqrt(jnp.mean(shifted * shifted, -1, keepdims=True) + EPSILON)
    return (shifted * inverse, inverse)


def normalize_back(grad_hat, normed, inverse):
    return inverse * (
        grad_hat
        - jnp.mean(grad_hat, -1, keepdims=True)
        - normed * jnp.mean(grad_hat * normed, -1, keepdims=True)
    )


def per_head(matrix):
    return matrix.reshape(matrix.shape[0], HEADS, matrix.shape[1] // HEADS)


def block_rows(length):
    return math.gcd(length, 512)


def score_terms(head_queries, head_grads, key_block, value_block, top_rows, total_rows, delta_rows):
    inv_root = 1.0 / math.sqrt(HEAD_DIM)
    scores = (
        jnp.einsum("qhd,khd->hqk", head_queries, key_block, preferred_element_type=jnp.float32)
        * inv_root
    )
    expo = jnp.exp(scores - top_rows[..., None])
    probs = expo / total_rows[..., None]
    dprobs = jnp.einsum("qhd,khd->hqk", head_grads, value_block, preferred_element_type=jnp.float32)
    grad_scores = (probs * (dprobs - delta_rows[..., None])).astype(jnp.bfloat16)
    return (grad_scores, expo.astype(jnp.bfloat16))


def scaled_grads(head_grads, total_rows):
    return head_grads.astype(jnp.float32) / total_rows.T[..., None]


def attend_context(queries, key_rows, value_rows):
    local_rows = queries.shape[0]
    head_queries = per_head(queries)
    head_width = head_queries.shape[2]
    inv_root = 1.0 / math.sqrt(HEAD_DIM)
    initial = (
        jnp.zeros((HEADS, local_rows, head_width), jnp.float32),
        jnp.full((HEADS, local_rows), -1e30, jnp.float32),
        jnp.zeros((HEADS, local_rows), jnp.float32),
    )
    running = initial
    key_piece = lax.all_gather(key_rows, "blk", axis=0, tiled=True)
    value_piece = lax.all_gather(value_rows, "blk", axis=0, tiled=True)
    length = key_piece.shape[0]
    block_width = block_rows(length)
    key_blocks = key_piece.reshape(length // block_width, block_width, HEADS, head_width)
    value_blocks = value_piece.reshape(length // block_width, block_width, HEADS, head_width)

    def absorb_block(states, blocks):
        summed, highest, totals = states
        key_block, value_block = blocks
        scores = (
            jnp.einsum("qhd,khd->hqk", head_queries, key_block, preferred_element_type=jnp.float32)
            * inv_root
        )
        new_top = jnp.maximum(highest, jnp.max(scores, -1))
        factor = jnp.exp(highest - new_top)
        weights = jnp.exp(scores - new_top[..., None])
        totals = totals * factor + jnp.sum(weights, -1)
        summed = summed * factor[..., None] + jnp.einsum(
            "hqk,khd->hqd",
            weights.astype(jnp.bfloat16),
            value_block,
            preferred_element_type=jnp.float32,
        )
        return ((summed, new_top, totals), None)

    running, unused = lax.scan(absorb_block, running, (key_blocks, value_blocks))
    summed, highest, totals = running
    attended = (summed / totals[..., None]).transpose(1, 0, 2).reshape(local_rows, -1)
    return (attended, highest, totals)


def back_scatter_keys(queries, key_rows, value_rows, grad_att, top_own, total_own, delta):
    local_rows, width = queries.shape
    inv_root = 1.0 / math.sqrt(HEAD_DIM)
    all_keys, all_values = (
        lax.all_gather(key_rows, "blk", axis=0, tiled=True),
        lax.all_gather(value_rows, "blk", axis=0, tiled=True),
    )
    length = all_keys.shape[0]
    block_width = block_rows(length)
    head_queries = per_head(queries)
    head_grads = per_head(grad_att)
    scaled = scaled_grads(head_grads, total_own)
    head_width = head_queries.shape[2]
    key_blocks = all_keys.reshape(length // block_width, block_width, HEADS, head_width)
    value_blocks = all_values.reshape(length // block_width, block_width, HEADS, head_width)

    def step_keys(grad_query, blocks):
        key_block, value_block = blocks
        grad_scores, expo_low = score_terms(
            head_queries, head_grads, key_block, value_block, top_own, total_own, delta
        )
        grad_query = (
            grad_query
            + jnp.einsum("hqk,khd->qhd", grad_scores, key_block, preferred_element_type=jnp.float32)
            * inv_root
        )
        grad_key = (
            jnp.einsum(
                "hqk,qhd->khd", grad_scores, head_queries, preferred_element_type=jnp.float32
            )
            * inv_root
        )
        grad_value = jnp.einsum(
            "hqk,qhd->khd", expo_low, scaled, preferred_element_type=jnp.float32
        )
        return (
            grad_query,
            jnp.concatenate(
                [grad_key.reshape(block_width, width), grad_value.reshape(block_width, width)], 1
            ),
        )

    start_query = jnp.zeros((local_rows, HEADS, head_width), jnp.float32)
    grad_query, key_terms = lax.scan(step_keys, start_query, (key_blocks, value_blocks))
    owned = lax.psum_scatter(
        key_terms.reshape(length, 2 * width).astype(jnp.bfloat16),
        "blk",
        scatter_dimension=0,
        tiled=True,
    ).astype(jnp.float32)
    return (grad_query.reshape(local_rows, width), owned[:, :width], owned[:, width:])


def per_device(layer_in, matrices, vectors, out_grad):
    mat_all, vec_all = (
        lax.all_gather(matrices, ("ctx", "blk"), axis=0, tiled=True),
        lax.all_gather(vectors, ("ctx", "blk"), axis=0, tiled=True),
    )
    vec_all = vec_all.astype(jnp.float32)
    seq_count, local_rows, width = layer_in.shape
    hidden_width = vec_all.shape[0] - 5 * width
    row_count = seq_count * local_rows
    gain_in = vec_all[:width]
    bias_in = vec_all[width : 2 * width]
    gain_mid = vec_all[2 * width : 3 * width]
    bias_mid = vec_all[3 * width : 4 * width]
    up_bias = vec_all[4 * width : 4 * width + hidden_width]
    down_bias = vec_all[4 * width + hidden_width :]
    w_input = mat_all[: 3 * width].reshape(3, width, width)
    w_output = mat_all[3 * width : 4 * width]
    up_rows = mat_all[4 * width : 4 * width + hidden_width]
    down_rows = mat_all[4 * width + hidden_width :]
    contract_rows = (((0,), (0,)), ((), ()))
    contract_cols = (((1,), (1,)), ((), ()))
    inputs = layer_in.reshape(row_count, width).astype(jnp.float32)
    normed_in, inverse_in = normalize(inputs)
    ln_in = (normed_in * gain_in + bias_in).astype(jnp.bfloat16)
    projected = jnp.einsum(
        "rd,kde->kre", ln_in, w_input, preferred_element_type=jnp.float32
    ).astype(jnp.bfloat16)
    query_seq = projected[0].reshape(seq_count, local_rows, width)
    key_seq = projected[1].reshape(seq_count, local_rows, width)
    value_seq = projected[2].reshape(seq_count, local_rows, width)

    def forward_one(unused, triple):
        return (None, attend_context(triple[0], triple[1], triple[2]))

    unused, (attended, top_rows, total_rows) = lax.scan(
        forward_one, None, (query_seq, key_seq, value_seq)
    )
    attended_low = attended.reshape(row_count, width).astype(jnp.bfloat16)
    middle = inputs + jnp.dot(attended_low, w_output, preferred_element_type=jnp.float32)
    normed_mid, inverse_mid = normalize(middle)
    ln_mid = (normed_mid * gain_mid + bias_mid).astype(jnp.bfloat16)
    upper = (
        lax.dot_general(ln_mid, up_rows, contract_cols, preferred_element_type=jnp.float32)
        + up_bias
    )
    activated, gelu_back = jax.vjp(lambda value: jax.nn.gelu(value, approximate=False), upper)
    hidden = activated.astype(jnp.bfloat16)
    result = middle + jnp.dot(hidden, down_rows, preferred_element_type=jnp.float32) + down_bias
    layer_out = result.astype(jnp.bfloat16).reshape(seq_count, local_rows, width)
    grad_rows = out_grad.reshape(row_count, width)
    grad_outf = grad_rows.astype(jnp.float32)
    grad_hidden = lax.dot_general(
        grad_rows, down_rows, contract_cols, preferred_element_type=jnp.float32
    )
    grad_down = lax.dot_general(
        hidden, grad_rows, contract_rows, preferred_element_type=jnp.float32
    )
    grad_down_bias = jnp.sum(grad_outf, 0)
    grad_upper = gelu_back(grad_hidden)[0].astype(jnp.bfloat16)
    grad_up_bias = jnp.sum(grad_upper.astype(jnp.float32), 0)
    grad_up = lax.dot_general(grad_upper, ln_mid, contract_rows, preferred_element_type=jnp.float32)
    grad_ln_mid = jnp.dot(grad_upper, up_rows, preferred_element_type=jnp.float32)
    grad_gain_mid = jnp.sum(grad_ln_mid * normed_mid, 0)
    grad_bias_mid = jnp.sum(grad_ln_mid, 0)
    grad_middle = grad_outf + normalize_back(grad_ln_mid * gain_mid, normed_mid, inverse_mid)
    grad_branch = grad_middle.astype(jnp.bfloat16)
    grad_wout = lax.dot_general(
        attended_low, grad_branch, contract_rows, preferred_element_type=jnp.float32
    )
    grad_att = lax.dot_general(
        grad_branch, w_output, contract_cols, preferred_element_type=jnp.float32
    ).astype(jnp.bfloat16)
    grad_att_seq = grad_att.reshape(seq_count, local_rows, width)
    head_shape = (seq_count, local_rows, HEADS, width // HEADS)
    delta = jnp.sum(
        grad_att_seq.astype(jnp.float32).reshape(head_shape) * attended.reshape(head_shape), -1
    ).transpose(0, 2, 1)

    def backward_one(unused, group):
        return (
            None,
            back_scatter_keys(group[0], group[1], group[2], group[3], group[4], group[5], group[6]),
        )

    unused, (grad_query, grad_key, grad_value) = lax.scan(
        backward_one,
        None,
        (query_seq, key_seq, value_seq, grad_att_seq, top_rows, total_rows, delta),
    )
    grad_projected = (
        jnp.stack([grad_query, grad_key, grad_value])
        .reshape(3, row_count, width)
        .astype(jnp.bfloat16)
    )
    grad_winput = jnp.einsum(
        "rd,kre->kde", ln_in, grad_projected, preferred_element_type=jnp.float32
    )
    grad_ln_in = jnp.einsum(
        "kre,kde->rd", grad_projected, w_input, preferred_element_type=jnp.float32
    )
    grad_gain_in = jnp.sum(grad_ln_in * normed_in, 0)
    grad_bias_in = jnp.sum(grad_ln_in, 0)
    grad_inputs = grad_middle + normalize_back(grad_ln_in * gain_in, normed_in, inverse_in)
    layer_grad = grad_inputs.astype(jnp.bfloat16).reshape(seq_count, local_rows, width)
    grad_mats = jnp.concatenate(
        [grad_winput.reshape(3 * width, width), grad_wout, grad_up, grad_down], 0
    )
    grad_vecs = jnp.concatenate(
        [grad_gain_in, grad_bias_in, grad_gain_mid, grad_bias_mid, grad_up_bias, grad_down_bias], 0
    )
    matrices_grad, vectors_grad = (
        lax.psum_scatter(grad_mats, ("ctx", "blk"), scatter_dimension=0, tiled=True),
        lax.psum_scatter(grad_vecs, ("ctx", "blk"), scatter_dimension=0, tiled=True),
    )
    return (layer_out, layer_grad, matrices_grad, vectors_grad)


def solution(mesh):
    placed = (
        P("ctx", "blk", None),
        P(("ctx", "blk"), None),
        P(("ctx", "blk")),
        P("ctx", "blk", None),
    )
    return jax.shard_map(
        per_device,
        mesh=mesh,
        in_specs=placed,
        out_specs=(
            P("ctx", "blk", None),
            P("ctx", "blk", None),
            P(("ctx", "blk"), None),
            P(("ctx", "blk")),
        ),
        check_vma=False,
    )
```

profile of v0, /device:TPU:0, one launch (start us, length us, event | category | flops | bytes accessed | tf_op | source)
XLA Modules:
  0.0 867.0 jit_solution(9020172836738128541)
XLA Ops:
  8.8 42.3 %all-reduce = bf16[2304]{0:T(1024)(128)(2,1)S(1)} all-reduce(bf16[2304]{0:T(1024)(128)(2,1)S(1)} %dynamic-update-slice), channel_id=1, replica_groups=mesh['ctx'=8,'blk'=4] {'ctx','blk'}, use_global_device_ids=true, to_apply=%add | all-reduce | flops 2304 | bytes 9216
  59.9 8.8 %all-gather.22.cloned.1.call-done = bf16[3072,256]{1,0:T(8,128)(2,1)} async-done(((bf16[96,256]{1,0:T(8,128)(2,1)}), bf16[3072,256]{1,0:T(8,128)(2,1)}) %all-gather.22.cloned.1.call-update) | async-done | bytes 1572880 | tf_op jit(solution)/shard_map/all_gather | solution.py:153
  78.1 212.6 %while.63 = (s32[]{:T(128)}, f32[2,1024,256]{1,2,0:T(8,128)}, f32[2,4,1024]{2,1,0:T(4,128)S(1)}, f32[2,4,1024]{2,1,0:T(4,128)S(1)}, bf16[2,1024,256]{1,2,0:T(8,1...) while((s32[]{:T(128)}, f32[2,1024,256]{1,2,0:T(8,128)}, ...), condition=%wide.region_7.8_spmd.clone, body=%wide.region_2.7_spmd.sunk.clone | while | flops 554717184 | bytes 68501904 | solution.py:185
  82.0 20.0 %all-gather.26.cloned.1.call-done = bf16[1,4096,256]{1,2,0:T(8,128)(2,1)} async-done(((bf16[1,1024,256]{1,2,0:T(8,128)(2,1)}), bf16[1,4096,256]{1,2,0:T(8,128)(2,1)}) %all-gather.26.cloned.1.call-update) | async-done | bytes 2097168 | tf_op jit(solution)/shard_map/while/body/eval_jaxpr/all_gather | solution.py:67
  106.5 20.3 %all-gather.24.cloned.1.call-done = bf16[1,4096,256]{1,2,0:T(8,128)(2,1)} async-done(((bf16[1,1024,256]{1,2,0:T(8,128)(2,1)}), bf16[1,4096,256]{1,2,0:T(8,128)(2,1)}) %all-gather.24.cloned.1.call-update) | async-done | bytes 2097168 | tf_op jit(solution)/shard_map/while/body/eval_jaxpr/all_gather | solution.py:66
  131.2 51.4 %while.62 = (s32[]{:T(128)}, f32[4,1024,64]{1,2,0:T(8,128)S(1)}, f32[4,1024]{1,0:T(4,128)S(1)}, f32[4,1024]{1,0:T(4,128)S(1)}, bf16[8,512,4,64]{1,3,2,0:T(8,128)...) while((s32[]{:T(128)}, f32[4,1024,64]{1,2,0:T(8,128)S(1)}, ...), condition=%wide.region_6.6_spmd.clone, body=%wide.region_3.5_spmd.clone.sunk | while | flops 554455040 | bytes 28573816 | solution.py:92
  134.9 2.7 fusion.132
  141.4 2.7 fusion.132
  187.9 20.7 %all-gather.26.cloned.1.call-done = bf16[1,4096,256]{1,2,0:T(8,128)(2,1)} async-done(((bf16[1,1024,256]{1,2,0:T(8,128)(2,1)}), bf16[1,4096,256]{1,2,0:T(8,128)(2,1)}) %all-gather.26.cloned.1.call-update) | async-done | bytes 2097168 | tf_op jit(solution)/shard_map/while/body/eval_jaxpr/all_gather | solution.py:67
  213.1 20.1 %all-gather.24.cloned.1.call-done = bf16[1,4096,256]{1,2,0:T(8,128)(2,1)} async-done(((bf16[1,1024,256]{1,2,0:T(8,128)(2,1)}), bf16[1,4096,256]{1,2,0:T(8,128)(2,1)}) %all-gather.24.cloned.1.call-update) | async-done | bytes 2097168 | tf_op jit(solution)/shard_map/while/body/eval_jaxpr/all_gather | solution.py:66
  237.7 51.4 %while.62 = (s32[]{:T(128)}, f32[4,1024,64]{1,2,0:T(8,128)S(1)}, f32[4,1024]{1,0:T(4,128)S(1)}, f32[4,1024]{1,0:T(4,128)S(1)}, bf16[8,512,4,64]{1,3,2,0:T(8,128)...) while((s32[]{:T(128)}, f32[4,1024,64]{1,2,0:T(8,128)S(1)}, ...), condition=%wide.region_6.6_spmd.clone, body=%wide.region_3.5_spmd.clone.sunk | while | flops 554455040 | bytes 28573816 | solution.py:92
  247.9 2.7 fusion.132
  295.1 20.7 %multiply_convert_fusion.1 = (bf16[2048,1024]{1,0:T(8,128)(2,1)S(1)}, f32[2048,1024]{1,0:T(8,128)S(1)}, f32[2048,1024]{1,0:T(8,128)}) fusion(f32[1024]{0:T(1024)S(1)} %copy-done.23, bf16[3072,256]{1,0:T(8,128)(2,1)S(1)} %copy-done.15, f32[2048,256]{1,0:T(8,128)S(1)} %get-tuple-element.462, f32[256]{0:T(256)S(1)} %copy-done.26, f32[256]{0:T(256)S(1)} %copy-done.24, ...), kind=kOutput, calls=%fused_computation.71 | convolution fusion | flops 1214775296 | bytes 23615488 | tf_op jit(solution)/shard_map/dot_general | solution.py:193
  315.8 9.2 %convert_reduce_fusion = (f32[1024]{0:T(1024)}, bf16[2048,1024]{1,0:T(8,128)(2,1)S(1)}) fusion(f32[2048,1024]{1,0:T(8,128)S(1)} %get-tuple-element.438, bf16[2048,256]{1,0:T(8,128)(2,1)S(1)} %bitcast.283, bf16[3072,256]{1,0:T(8,128)(2,1)S(1)} %copy-done.15, f32[2048,1024]{1,0:T(8,128)} %get-tuple-element.463, f32[1024]{0:T(1024)S(1)} %copy-done.23), kind=kOutput, calls=%fused_computation.69 | convolution fusion | flops 1109392384 | bytes 22552576 | tf_op jit(solution)/shard_map/dot_general | solution.py:202
  325.0 3.0 fusion.67
  340.0 4.0 reshape.186
  344.1 4.6 multiply_reduce_fusion.3
  348.8 400.1 %while.65 = (s32[]{:T(128)}, bf16[2,1024,256]{1,2,0:T(8,128)(2,1)}, bf16[2,1024,256]{2,1,0:T(8,128)(2,1)}, bf16[2,1024,256]{2,1,0:T(8,128)(2,1)}, bf16[2,1024,25...) while((s32[]{:T(128)}, bf16[2,1024,256]{1,2,0:T(8,128)(2,1)}, ...), condition=%wide.region_17.18_spmd.clone, body=%wide.region_13.17_spmd.sunk.clone | while | flops 1363935232 | bytes 120029784 | solution.py:235
  355.9 18.1 %all-gather.30.cloned.1.call-done = bf16[1,4096,256]{1,2,0:T(8,128)(2,1)} async-done(((bf16[1,1024,256]{1,2,0:T(8,128)(2,1)}), bf16[1,4096,256]{1,2,0:T(8,128)(2,1)}) %all-gather.30.cloned.1.call-update) | async-done | bytes 2097168 | tf_op jit(solution)/shard_map/while/body/eval_jaxpr/all_gather | solution.py:103
  378.4 19.7 %all-gather.28.cloned.1.call-done = bf16[1,4096,256]{1,2,0:T(8,128)(2,1)} async-done(((bf16[1,1024,256]{1,2,0:T(8,128)(2,1)}), bf16[1,4096,256]{1,2,0:T(8,128)(2,1)}) %all-gather.28.cloned.1.call-update) | async-done | bytes 2097168 | tf_op jit(solution)/shard_map/while/body/eval_jaxpr/all_gather | solution.py:102
  402.7 92.9 %while.64 = (s32[]{:T(128)}, f32[1024,4,64]{0,2,1:T(8,128)S(1)}, bf16[8,512,512]{1,2,0:T(8,128)(2,1)}, bf16[8,512,4,64]{1,3,2,0:T(8,128)(2,1)}, bf16[1024,4,64]{...) while((s32[]{:T(128)}, f32[1024,4,64]{0,2,1:T(8,128)S(1)}, ...), condition=%wide.region_15.15_spmd.clone, body=%wide.region_14.14_spmd.clone.sunk | while | flops 1363148800 | bytes 44368028 | solution.py:141
  406.5 3.6 multiply_convert_fusion.3
  418.1 3.6 multiply_convert_fusion.3
  429.7 3.6 multiply_convert_fusion.3
  441.3 3.6 multiply_convert_fusion.3
  452.9 3.6 multiply_convert_fusion.3
  464.6 3.6 multiply_convert_fusion.3
  476.2 3.6 multiply_convert_fusion.3
  487.8 3.6 multiply_convert_fusion.3
  495.5 6.5 copy.124
  503.0 43.7 %reduce-scatter.5.cloned.1.call-done = bf16[1024,512]{1,0:T(8,128)(2,1)} async-done(((bf16[4096,512]{1,0:T(8,128)(2,1)}), bf16[1024,512]{1,0:T(8,128)(2,1)}) %reduce-scatter.5.cloned.1.call-update) | async-done | bytes 1048592 | tf_op jit(solution)/shard_map/while/body/eval_jaxpr/reduce_scatter | solution.py:142
  555.9 18.1 %all-gather.30.cloned.1.call-done = bf16[1,4096,256]{1,2,0:T(8,128)(2,1)} async-done(((bf16[1,1024,256]{1,2,0:T(8,128)(2,1)}), bf16[1,4096,256]{1,2,0:T(8,128)(2,1)}) %all-gather.30.cloned.1.call-update) | async-done | bytes 2097168 | tf_op jit(solution)/shard_map/while/body/eval_jaxpr/all_gather | solution.py:103
  578.5 19.5 %all-gather.28.cloned.1.call-done = bf16[1,4096,256]{1,2,0:T(8,128)(2,1)} async-done(((bf16[1,1024,256]{1,2,0:T(8,128)(2,1)}), bf16[1,4096,256]{1,2,0:T(8,128)(2,1)}) %all-gather.28.cloned.1.call-update) | async-done | bytes 2097168 | tf_op jit(solution)/shard_map/while/body/eval_jaxpr/all_gather | solution.py:102
  602.6 92.9 %while.64 = (s32[]{:T(128)}, f32[1024,4,64]{0,2,1:T(8,128)S(1)}, bf16[8,512,512]{1,2,0:T(8,128)(2,1)}, bf16[8,512,4,64]{1,3,2,0:T(8,128)(2,1)}, bf16[1024,4,64]{...) while((s32[]{:T(128)}, f32[1024,4,64]{0,2,1:T(8,128)S(1)}, ...), condition=%wide.region_15.15_spmd.clone, body=%wide.region_14.14_spmd.clone.sunk | while | flops 1363148800 | bytes 44368028 | solution.py:141
  606.4 3.6 multiply_convert_fusion.3
  618.0 3.6 multiply_convert_fusion.3
  629.6 3.6 multiply_convert_fusion.3
  641.2 3.6 multiply_convert_fusion.3
  652.9 3.6 multiply_convert_fusion.3
  664.5 3.6 multiply_convert_fusion.3
  676.1 3.6 multiply_convert_fusion.3
  687.7 3.6 multiply_convert_fusion.3
  695.5 6.5 copy.124
  702.9 43.8 %reduce-scatter.5.cloned.1.call-done = bf16[1024,512]{1,0:T(8,128)(2,1)} async-done(((bf16[4096,512]{1,0:T(8,128)(2,1)}), bf16[1024,512]{1,0:T(8,128)(2,1)}) %reduce-scatter.5.cloned.1.call-update) | async-done | bytes 1048592 | tf_op jit(solution)/shard_map/while/body/eval_jaxpr/reduce_scatter | solution.py:142
  750.6 4.1 multiply_reduce_fusion.1
  758.7 39.5 %all-reduce.1 = f32[2304]{0:T(1024)S(1)} all-reduce(f32[2304]{0:T(1024)S(1)} %constant_dynamic-update-slice_fusion.1), channel_id=8, replica_groups=mesh['ctx'=8,'blk'=4] {'ctx','blk'}, use_global_device_ids=true, to_apply=%region_27.28.clone | all-reduce | flops 2304 | bytes 18432
  798.8 4.7 fusion.48
  805.6 54.4 %reduce-scatter.3.cloned.1.call-done = f32[96,256]{1,0:T(8,128)} async-done(((f32[3072,256]{1,0:T(8,128)}), f32[96,256]{1,0:T(8,128)}) %reduce-scatter.3.cloned.1.call-update) | async-done | bytes 98320 | tf_op jit(solution)/shard_map/reduce_scatter | solution.py:262
  (375 shorter events, 332.0 us)
Async XLA Ops:
  7.2 61.5 %all-gather.22.cloned.1.call-start = ((), (), s32[]{:S(2)}) async-start(), calls=%async_computation.2 | async-start | bytes 1622016 | tf_op jit(solution)/shard_map/all_gather | solution.py:153
  58.1 13.3 %copy-start.18 = (f32[256]{0:T(256)}, f32[256]{0:T(256)S(1)}, u32[]{:S(2)}) copy-start(f32[256]{0:T(256)S(1)} %get-tuple-element.459) | copy-start | bytes 3076
  58.1 13.3 %copy-start.20 = (f32[256]{0:T(256)}, f32[256]{0:T(256)S(1)}, u32[]{:S(2)}) copy-start(f32[256]{0:T(256)S(1)} %get-tuple-element.460) | copy-start | bytes 3076
  69.7 0.7 copy-start.9
  78.1 23.9 %all-gather.26.cloned.1.call-start = ((), (), s32[]{:S(2)}) async-start(), calls=%async_computation.5 | async-start | bytes 2621440 | tf_op jit(solution)/shard_map/while/body/eval_jaxpr/all_gather | solution.py:67
  80.0 46.8 %all-gather.24.cloned.1.call-start = ((), (), s32[]{:S(2)}) async-start(), calls=%async_computation.4 | async-start | bytes 2621440 | tf_op jit(solution)/shard_map/while/body/eval_jaxpr/all_gather | solution.py:66
  183.9 24.7 %all-gather.26.cloned.1.call-start = ((), (), s32[]{:S(2)}) async-start(), calls=%async_computation.5 | async-start | bytes 2621440 | tf_op jit(solution)/shard_map/while/body/eval_jaxpr/all_gather | solution.py:67
  185.9 47.4 %all-gather.24.cloned.1.call-start = ((), (), s32[]{:S(2)}) async-start(), calls=%async_computation.4 | async-start | bytes 2621440 | tf_op jit(solution)/shard_map/while/body/eval_jaxpr/all_gather | solution.py:66
  290.6 4.4 copy-start.23
  290.7 4.4 copy-start.24
  290.7 4.4 copy-start.26
  292.5 2.7 copy-start.15
  294.4 38.4 %copy-start.5 = (f32[2048,256]{1,0:T(8,128)}, f32[2048,256]{1,0:T(8,128)S(1)}, u32[]{:S(2)}) copy-start(f32[2048,256]{1,0:T(8,128)S(1)} %get-tuple-element.462) | copy-start | bytes 6291460
  295.1 20.7 %copy-start.7 = (bf16[2,1024,256]{2,1,0:T(8,128)(2,1)S(1)}, bf16[2,1024,256]{2,1,0:T(8,128)(2,1)}, u32[]{:S(2)}) copy-start(bf16[2,1024,256]{2,1,0:T(8,128)(2,1)} %param.15) | copy-start | bytes 3145732
  315.8 12.2 %copy-start.31 = (bf16[2048,1024]{1,0:T(8,128)(2,1)}, bf16[2048,1024]{1,0:T(8,128)(2,1)S(1)}, u32[]{:S(2)}) copy-start(bf16[2048,1024]{1,0:T(8,128)(2,1)S(1)} %get-tuple-element.437) | copy-start | bytes 12582916
  334.6 1.4 copy-start.2
  348.7 401.9 %copy-start.10 = (bf16[768,256]{1,0:T(8,128)(2,1)S(1)}, bf16[768,256]{1,0:T(8,128)(2,1)}, u32[]{:S(2)}) copy-start(bf16[768,256]{1,0:T(8,128)(2,1)} %copy-done.9) | copy-start | bytes 1179652
  348.7 401.9 %copy-start.16 = (f32[1,8,2,128]{3,1,2,0:T(8,128)S(1)}, f32[1,8,2,128]{3,1,2,0:T(8,128)}, u32[]{:S(2)}) copy-start(f32[1,8,2,128]{3,1,2,0:T(8,128)} %copy.90) | copy-start | bytes 24580
  348.7 401.9 %copy-start.17 = (f32[1,8,2,128]{3,1,2,0:T(8,128)S(1)}, f32[1,8,2,128]{3,1,2,0:T(8,128)}, u32[]{:S(2)}) copy-start(f32[1,8,2,128]{3,1,2,0:T(8,128)} %copy.91) | copy-start | bytes 24580
  348.7 401.9 %copy-start.19 = (f32[256]{0:T(256)S(1)}, f32[256]{0:T(256)}, u32[]{:S(2)}) copy-start(f32[256]{0:T(256)} %copy-done.18) | copy-start | bytes 3076
  348.7 401.9 %copy-start.21 = (f32[256]{0:T(256)S(1)}, f32[256]{0:T(256)}, u32[]{:S(2)}) copy-start(f32[256]{0:T(256)} %copy-done.20) | copy-start | bytes 3076
  348.9 4.4 copy-start
  348.9 25.0 %all-gather.30.cloned.1.call-start = ((), (), s32[]{:S(2)}) async-start(), calls=%async_computation.7 | async-start | bytes 2621440 | tf_op jit(solution)/shard_map/while/body/eval_jaxpr/all_gather | solution.py:103
  351.2 46.9 %all-gather.28.cloned.1.call-start = ((), (), s32[]{:S(2)}) async-start(), calls=%async_computation.6 | async-start | bytes 2621440 | tf_op jit(solution)/shard_map/while/body/eval_jaxpr/all_gather | solution.py:102
  353.2 193.5 %reduce-scatter.5.cloned.1.call-start = ((), (), s32[]{:S(2)}) async-start(), calls=%async_computation.8 | async-start | bytes 5242880 | tf_op jit(solution)/shard_map/while/body/eval_jaxpr/reduce_scatter | solution.py:142
  502.0 47.0 %copy-start.1 = (bf16[2,1024,256]{1,2,0:T(8,128)(2,1)S(1)}, bf16[2,1024,256]{1,2,0:T(8,128)(2,1)}, u32[]{:S(2)}) copy-start(bf16[2,1024,256]{1,2,0:T(8,128)(2,1)} %copy-done) | copy-start | bytes 3145732 | tf_op jit(solution)/shard_map/while
  549.0 4.4 copy-start
  549.0 25.0 %all-gather.30.cloned.1.call-start = ((), (), s32[]{:S(2)}) async-start(), calls=%async_computation.7 | async-start | bytes 2621440 | tf_op jit(solution)/shard_map/while/body/eval_jaxpr/all_gather | solution.py:103
  551.3 46.8 %all-gather.28.cloned.1.call-start = ((), (), s32[]{:S(2)}) async-start(), calls=%async_computation.6 | async-start | bytes 2621440 | tf_op jit(solution)/shard_map/while/body/eval_jaxpr/all_gather | solution.py:102
  553.3 193.4 %reduce-scatter.5.cloned.1.call-start = ((), (), s32[]{:S(2)}) async-start(), calls=%async_computation.8 | async-start | bytes 5242880 | tf_op jit(solution)/shard_map/while/body/eval_jaxpr/reduce_scatter | solution.py:142
  702.0 46.9 %copy-start.1 = (bf16[2,1024,256]{1,2,0:T(8,128)(2,1)S(1)}, bf16[2,1024,256]{1,2,0:T(8,128)(2,1)}, u32[]{:S(2)}) copy-start(bf16[2,1024,256]{1,2,0:T(8,128)(2,1)} %copy-done) | copy-start | bytes 3145732 | tf_op jit(solution)/shard_map/while
  748.9 111.1 %reduce-scatter.3.cloned.1.call-start = ((), (), s32[]{:S(2)}) async-start(), calls=%async_computation.3 | async-start | bytes 3244032 | tf_op jit(solution)/shard_map/reduce_scatter | solution.py:262
  750.6 4.2 copy-start.29
  750.6 4.1 copy-start.30
  754.8 1.2 copy-start.12
  754.8 1.5 copy-start.13
  754.8 1.6 copy-start.14
  756.4 1.9 copy-start.8
  756.4 2.2 copy-start.28
  756.4 2.3 copy-start.27
  756.4 2.3 copy-start.22
  756.4 42.4 %copy-start.6 = (f32[2048,256]{1,0:T(8,128)S(1)}, f32[2048,256]{1,0:T(8,128)}, u32[]{:S(2)}) copy-start(f32[2048,256]{1,0:T(8,128)} %copy-done.5) | copy-start | bytes 6291460
  756.4 42.4 %copy-start.25 = (f32[256]{0:T(256)S(1)}, f32[256]{0:T(256)}, u32[]{:S(2)}) copy-start(f32[256]{0:T(256)} %get-tuple-element.456) | copy-start | bytes 3076
  798.8 4.7 copy-start.3
  798.8 4.7 copy-start.4
  798.8 4.7 copy-start.11
Sparse Core Ops, SparseCore 0:
  10.9 57.7 all-gather.21
  80.5 21.4 all-gather.25
  104.1 22.5 all-gather.23
  186.0 22.5 all-gather.25
  210.6 22.5 all-gather.23
  351.3 22.5 all-gather.29
  375.5 22.5 all-gather.27
  502.2 44.4 reduce-scatter.4
  551.4 22.5 all-gather.29
  575.4 22.5 all-gather.27
  702.1 44.4 reduce-scatter.4
  758.4 101.5 reduce-scatter.2
where the time goes:
time: 880 us; the launch traced here: 867 us
  waiting for transfers between devices  308 us (35%)
  matrix products  304 us (35%)
  local copies, waits for them, and re-layouts  101 us (11%)
  blocking collectives  81.8 us (9%)
  other arithmetic  54.5 us (6%)
  between operations  14.8 us (2%)
    reduce_scatter x2, waiting for transfers between devices, back_scatter_keys(): lax.psum_scatter(key_terms.reshape(length, 2 * width).astype(jnp.bfloat16...  87.5 us
    unnamed x2, blocking collectives  81.8 us
    dot_general x16, matrix products, score_terms(): jnp.einsum('qhd,khd->hqk', head_grads, value_block, preferred_element_typ...  57.8 us
    reduce_scatter x1, waiting for transfers between devices, per_device(): lax.psum_scatter(grad_mats, ('ctx', 'blk'), scatter_dimension=0, tiled=True)  54.4 us
    dot_general x16, matrix products, absorb_block(): jnp.einsum('hqk,khd->hqd', weights.astype(jnp.bfloat16), value_block, pre...  43 us
    all_gather x2, waiting for transfers between devices, attend_context(): value_piece = lax.all_gather(value_rows, 'blk', axis=0, tiled=True)  40.7 us
    all_gather x2, waiting for transfers between devices, attend_context(): key_piece = lax.all_gather(key_rows, 'blk', axis=0, tiled=True)  40.4 us
    all_gather x2, waiting for transfers between devices, back_scatter_keys(): lax.all_gather(key_rows, 'blk', axis=0, tiled=True)  39.2 us
  transfers between devices with their start and end apart: 12, of which 12 were waited for; matrix products, arithmetic and copies ran while one was open for 6% of the time, Pallas kernels for 0%

commit v1 on v0

v1 whole, which is shorter than its diff:
```python
import functools
import math

import jax
import jax.numpy as jnp
from jax import lax
from jax.experimental import pallas as pl
from jax.experimental.pallas import tpu as pltpu
from jax.sharding import PartitionSpec as P

HEADS = 4
EPSILON = 1e-05
LOG2E = math.log2(math.e)
LN2 = math.log(2.0)
AUG = 80
SAFE_BOUND = 90.0
BF = jnp.bfloat16
F32 = jnp.float32
NT = (((1,), (1,)), ((), ()))
TN = (((0,), (0,)), ((), ()))


def dot(a, b):
    return jnp.dot(a, b, preferred_element_type=F32)


def dot_nt(a, b):
    return lax.dot_general(a, b, NT, preferred_element_type=F32)


def dot_tn(a, b):
    return lax.dot_general(a, b, TN, preferred_element_type=F32)


def params(**kw):
    return pltpu.CompilerParams(vmem_limit_bytes=60 << 20, **kw)


def whole(*shape):
    return pl.BlockSpec(shape, lambda *_: (0,) * len(shape))


def normalize(inputs):
    centre = jnp.mean(inputs, -1, keepdims=True)
    shifted = inputs - centre
    inverse = lax.rsqrt(jnp.mean(shifted * shifted, -1, keepdims=True) + EPSILON)
    return shifted * inverse, inverse


def normalize_back(grad_hat, normed, inverse):
    return inverse * (
        grad_hat
        - jnp.mean(grad_hat, -1, keepdims=True)
        - normed * jnp.mean(grad_hat * normed, -1, keepdims=True)
    )


def prep_kernel(own_steps, x_ref, w_ref, vec_ref, ln_ref, qt_ref, kn_ref, kta_ref, vta_ref, wt, wkp):
    width = x_ref.shape[1]
    head = width // HEADS
    step = pl.program_id(0)

    @pl.when(step == 0)
    def _():
        for index in range(3):
            piece = w_ref[index * width : (index + 1) * width, :].astype(F32)
            wt[index * width : (index + 1) * width, :] = piece.T.astype(BF)
        wk = w_ref[width : 2 * width, :].astype(F32)
        for h in range(HEADS):
            wide = jnp.concatenate([wk[:, h * head : (h + 1) * head], jnp.zeros((width, 128 - head), F32)], 1)
            wkp[:, h * 128 : (h + 1) * 128] = wide.astype(BF)

    normed, _ = normalize(x_ref[...].astype(F32))
    ln = (normed * vec_ref[0:1, :] + vec_ref[1:2, :]).astype(BF)
    ln_ref[...] = ln
    rows = ln.shape[0]
    extra = (lax.broadcasted_iota(jnp.int32, (AUG - head, rows), 0) < 3).astype(F32).astype(BF)

    kt = dot_nt(wt[width : 2 * width, :], ln).astype(BF)
    vt = dot_nt(wt[2 * width : 3 * width, :], ln).astype(BF)
    kn = dot(ln, wkp[...]).astype(BF)
    for h in range(HEADS):
        kta_ref[h, :head, :] = kt[h * head : (h + 1) * head, :]
        kta_ref[h, head:, :] = extra
        vta_ref[h, :head, :] = vt[h * head : (h + 1) * head, :]
        vta_ref[h, head:, :] = extra
        kn_ref[h] = kn[:, h * 128 : (h + 1) * 128]

    @pl.when(step < own_steps)
    def _():
        qt = dot_nt(wt[0:width, :], ln) * (LOG2E / math.sqrt(head))
        for h in range(HEADS):
            qt_ref[h] = qt[h * head : (h + 1) * head, :].astype(BF)


def prep(rows_all, own, w_input, vec):
    total, width = rows_all.shape
    head = width // HEADS
    block = min(512, own)
    steps, own_steps = total // block, own // block
    last = own_steps - 1
    return pl.pallas_call(
        functools.partial(prep_kernel, own_steps),
        grid=(steps,),
        in_specs=[
            pl.BlockSpec((block, width), lambda i: (i, 0)),
            whole(3 * width, width),
            whole(*vec.shape),
        ],
        out_specs=[
            pl.BlockSpec((block, width), lambda i: (i, 0)),
            pl.BlockSpec((HEADS, head, block), lambda i: (0, 0, jnp.minimum(i, last))),
            pl.BlockSpec((HEADS, block, 128), lambda i: (0, i, 0)),
            pl.BlockSpec((HEADS, AUG, block), lambda i: (0, 0, i)),
            pl.BlockSpec((HEADS, AUG, block), lambda i: (0, 0, i)),
        ],
        out_shape=[
            jax.ShapeDtypeStruct((total, width), BF),
            jax.ShapeDtypeStruct((HEADS, head, own), BF),
            jax.ShapeDtypeStruct((HEADS, total, 128), BF),
            jax.ShapeDtypeStruct((HEADS, AUG, total), BF),
            jax.ShapeDtypeStruct((HEADS, AUG, total), BF),
        ],
        scratch_shapes=[pltpu.VMEM((3 * width, width), BF), pltpu.VMEM((width, HEADS * 128), BF)],
        compiler_params=params(),
        name="project",
    )(rows_all, w_input, vec)


def attend_kernel(qt_ref, kn_ref, kta_ref, vta_ref, att_ref, lse_ref):
    head, own = qt_ref.shape[1:]
    total = kn_ref.shape[1]
    tq = min(1024, own)
    tk = min(256, total)
    count = total // tk

    def longest(rows):
        rows = rows.astype(F32)
        return jnp.max(jnp.sum(rows * rows, 0, keepdims=True))

    bound = longest(qt_ref[0]) * longest(kta_ref[0, :head, :])

    def finish(where, summed, top):
        totals = summed[head : head + 1, :]
        att_ref[0, :, where] = summed[:head, :] / totals
        level = jnp.log2(totals)
        lse_ref[0, :, where] = jnp.broadcast_to(level if top is None else level + top, (8, tq))

    def scores(queries, j):
        return dot(kn_ref[0, j * tk : (j + 1) * tk, :head], queries)

    @pl.when(bound <= SAFE_BOUND * SAFE_BOUND)
    def _():
        @pl.loop(0, own // tq)
        def _(i):
            where = pl.ds(pl.multiple_of(i * tq, tq), tq)
            queries = qt_ref[0, :, where]
            summed = jnp.zeros((AUG, tq), F32)
            now = scores(queries, 0)
            for j in range(count):
                expo = jnp.exp2(now).astype(BF)
                if j + 1 < count:
                    now = scores(queries, j + 1)
                summed = summed + dot(vta_ref[0, :, j * tk : (j + 1) * tk], expo)
            finish(where, summed, None)

    @pl.when(jnp.logical_not(bound <= SAFE_BOUND * SAFE_BOUND))
    def _():
        @pl.loop(0, own // tq)
        def _(i):
            where = pl.ds(pl.multiple_of(i * tq, tq), tq)
            queries = qt_ref[0, :, where]

            def absorb(j, carry):
                summed, top = carry
                part = pl.ds(pl.multiple_of(j * tk, tk), tk)
                now = dot(kn_ref[0, part, :head], queries)
                higher = jnp.maximum(top, jnp.max(now, 0, keepdims=True))
                expo = jnp.exp2(now - higher).astype(BF)
                summed = summed * jnp.exp2(top - higher) + dot(vta_ref[0, :, part], expo)
                return summed, higher

            start = (jnp.zeros((AUG, tq), F32), jnp.full((1, tq), -1e30, F32))
            summed, top = lax.fori_loop(0, count, absorb, start)
            finish(where, summed, top)


def attend(qt, kn, kta, vta):
    _, head, own = qt.shape
    total = kn.shape[1]
    per_head = lambda *shape: pl.BlockSpec((1, *shape), lambda h: (h, 0, 0))
    return pl.pallas_call(
        attend_kernel,
        grid=(HEADS,),
        in_specs=[per_head(head, own), per_head(total, 128), per_head(AUG, total), per_head(AUG, total)],
        out_specs=[per_head(head, own), per_head(8, own)],
        out_shape=[
            jax.ShapeDtypeStruct((HEADS, head, own), F32),
            jax.ShapeDtypeStruct((HEADS, 8, own), F32),
        ],
        compiler_params=params(),
        name="attend",
    )(qt, kn, kta, vta)


def gelu_both(value):
    square = value * value
    density = jnp.exp(-0.5 * square)
    place = pl.reciprocal(1.0 + (0.3275911 / math.sqrt(2.0)) * jnp.abs(value), approx=True)
    series = 1.061405429 * place - 1.453152027
    series = series * place + 1.421413741
    series = series * place - 0.284496736
    series = series * place + 0.254829592
    tail = 0.5 * series * place * density
    below = jnp.where(value >= 0.0, 1.0 - tail, tail)
    return value * below, below + value * density * (1.0 / math.sqrt(2.0 * math.pi))


def split_rows(level, count):
    high = level.astype(BF).astype(F32)
    middle = (level - high).astype(BF).astype(F32)
    low = level - high - middle
    place = lax.broadcasted_iota(jnp.int32, (count, level.shape[1]), 0)
    rows = jnp.where(place == 0, high, jnp.where(place == 1, middle, jnp.where(place == 2, low, 0.0)))
    return rows


def middle_kernel(
    x_ref, g_ref, att_ref, lse_ref, qt_ref, w_ref, vec_ref,
    out_ref, gmid_ref, qa_ref, doa_ref, dot_ref, gwo_ref, gup_ref, gdown_ref, gvec_ref,
):
    width = x_ref.shape[1]
    head = width // HEADS
    rows = x_ref.shape[0]
    hidden_width = (w_ref.shape[0] - width) // 2
    wo = w_ref[:width, :]
    up = w_ref[width : width + hidden_width, :]
    down = w_ref[width + hidden_width :, :]
    pieces = hidden_width // width
    up_bias = jnp.concatenate([vec_ref[4 + p : 5 + p, :] for p in range(pieces)], 1)
    down_bias = vec_ref[4 + pieces : 5 + pieces, :]
    gain, bias = vec_ref[2:3, :], vec_ref[3:4, :]

    @pl.when(pl.program_id(0) == 0)
    def _():
        gwo_ref[...] = jnp.zeros_like(gwo_ref)
        gup_ref[...] = jnp.zeros_like(gup_ref)
        gdown_ref[...] = jnp.zeros_like(gdown_ref)
        gvec_ref[...] = jnp.zeros_like(gvec_ref)

    att = att_ref[...].reshape(width, rows)
    att_low = att.astype(BF)
    grad = g_ref[...]
    gradf = grad.astype(F32)
    middle = x_ref[...].astype(F32) + dot_tn(att_low, wo)
    normed, inverse = normalize(middle)
    ln_mid = (normed * gain + bias).astype(BF)
    upper = dot_nt(ln_mid, up) + up_bias
    grad_hidden = dot_nt(grad, down)
    activated, slope = gelu_both(upper)
    hidden = activated.astype(BF)
    grad_upper = (grad_hidden * slope).astype(BF)
    out_ref[...] = (middle + dot(hidden, down) + down_bias).astype(BF)
    gdown_ref[...] += dot_tn(grad, hidden)
    gup_ref[...] += dot_tn(ln_mid, grad_upper)
    grad_ln = dot(grad_upper, up)
    total_up = jnp.sum(grad_upper.astype(F32), 0, keepdims=True)
    gvec_ref[2:3, :] += jnp.sum(grad_ln * normed, 0, keepdims=True)
    gvec_ref[3:4, :] += jnp.sum(grad_ln, 0, keepdims=True)
    for p in range(pieces):
        gvec_ref[4 + p : 5 + p, :] += total_up[:, p * width : (p + 1) * width]
    gvec_ref[4 + pieces : 5 + pieces, :] += jnp.sum(gradf, 0, keepdims=True)
    grad_mid = gradf + normalize_back(grad_ln * gain, normed, inverse)
    gmid_ref[...] = grad_mid
    branch = grad_mid.astype(BF)
    gwo_ref[...] += dot(att_low, branch)
    grad_att = dot_nt(wo, branch).astype(BF)
    spare = jnp.zeros((128 - AUG, rows), F32)
    for h in range(HEADS):
        mine = slice(h * head, (h + 1) * head)
        grad_head = grad_att[mine, :]
        dot_ref[h] = grad_head
        delta = jnp.sum(grad_head.astype(F32) * att[mine, :], 0, keepdims=True)
        wide = jnp.concatenate([grad_head.astype(F32), split_rows(-delta, AUG - head), spare], 0)
        doa_ref[h] = wide.T.astype(BF)
        level = lse_ref[h, 0:1, :]
        wide = jnp.concatenate([qt_ref[h].astype(F32), split_rows(-level, AUG - head), spare], 0)
        qa_ref[h] = wide.T.astype(BF)


def between(x, grad, att, lse, qt, weights, vec):
    own, width = x.shape
    head = width // HEADS
    hidden_width = (weights.shape[0] - width) // 2
    block = min(512, own)
    rows = lambda i: (i, 0)
    lanes = lambda i: (0, 0, i)
    tall = lambda i: (0, i, 0)
    return pl.pallas_call(
        middle_kernel,
        grid=(own // block,),
        in_specs=[
            pl.BlockSpec((block, width), rows),
            pl.BlockSpec((block, width), rows),
            pl.BlockSpec((HEADS, head, block), lanes),
            pl.BlockSpec((HEADS, 8, block), lanes),
            pl.BlockSpec((HEADS, head, block), lanes),
            whole(*weights.shape),
            whole(*vec.shape),
        ],
        out_specs=[
            pl.BlockSpec((block, width), rows),
            pl.BlockSpec((block, width), rows),
            pl.BlockSpec((HEADS, block, 128), tall),
            pl.BlockSpec((HEADS, block, 128), tall),
            pl.BlockSpec((HEADS, head, block), lanes),
            whole(width, width),
            whole(width, hidden_width),
            whole(width, hidden_width),
            whole(16, width),
        ],
        out_shape=[
            jax.ShapeDtypeStruct((own, width), BF),
            jax.ShapeDtypeStruct((own, width), F32),
            jax.ShapeDtypeStruct((HEADS, own, 128), BF),
            jax.ShapeDtypeStruct((HEADS, own, 128), BF),
            jax.ShapeDtypeStruct((HEADS, head, own), BF),
            jax.ShapeDtypeStruct((width, width), F32),
            jax.ShapeDtypeStruct((width, hidden_width), F32),
            jax.ShapeDtypeStruct((width, hidden_width), F32),
            jax.ShapeDtypeStruct((16, width), F32),
        ],
        compiler_params=params(),
        name="between",
    )(x, grad, att, lse, qt, weights, vec)


def attend_back_kernel(qa_ref, doa_ref, qt_ref, dot_ref, kta_ref, vta_ref, kn_ref, dq_ref, dk_ref, dv_ref, dk_sum, dv_sum):
    head, own = qt_ref.shape[1:]
    total = kn_ref.shape[1]
    tq = min(1024, own)
    tk = min(512, total)
    count = total // tk
    dk_sum[...] = jnp.zeros_like(dk_sum)
    dv_sum[...] = jnp.zeros_like(dv_sum)

    @pl.loop(0, own // tq)
    def _(i):
        where = pl.ds(pl.multiple_of(i * tq, tq), tq)
        queries, grads = qa_ref[0, where, :AUG], doa_ref[0, where, :AUG]
        queries_t, grads_t = qt_ref[0, :, where], dot_ref[0, :, where]

        def pair(j):
            part = slice(j * tk, (j + 1) * tk)
            return dot(queries, kta_ref[0, :, part]), dot(grads, vta_ref[0, :, part])

        grad_query = jnp.zeros((tq, 128), F32)
        level, change = pair(0)
        for j in range(count):
            part = slice(j * tk, (j + 1) * tk)
            probs = jnp.exp2(level)
            probs_low = probs.astype(BF)
            grad_scores = (probs * change).astype(BF)
            if j + 1 < count:
                level, change = pair(j + 1)
            dv_sum[:, part] += dot(grads_t, probs_low)
            dk_sum[:, part] += dot(queries_t, grad_scores)
            grad_query = grad_query + dot(grad_scores, kn_ref[0, part, :])
        dq_ref[0, where, :] = (grad_query * (1.0 / math.sqrt(head))).astype(BF)

    dk_ref[0] = (dk_sum[...] * LN2).astype(BF)
    dv_ref[0] = dv_sum[...].astype(BF)


def attend_back(qa, doa, qt, dot_t, kta, vta, kn):
    _, head, own = qt.shape
    total = kn.shape[1]
    per_head = lambda *shape: pl.BlockSpec((1, *shape), lambda h: (h, 0, 0))
    return pl.pallas_call(
        attend_back_kernel,
        grid=(HEADS,),
        in_specs=[
            per_head(own, 128), per_head(own, 128), per_head(head, own), per_head(head, own),
            per_head(AUG, total), per_head(AUG, total), per_head(total, 128),
        ],
        out_specs=[per_head(own, 128), per_head(head, total), per_head(head, total)],
        out_shape=[
            jax.ShapeDtypeStruct((HEADS, own, 128), BF),
            jax.ShapeDtypeStruct((HEADS, head, total), BF),
            jax.ShapeDtypeStruct((HEADS, head, total), BF),
        ],
        scratch_shapes=[pltpu.VMEM((head, total), F32), pltpu.VMEM((head, total), F32)],
        compiler_params=params(),
        name="attend_back",
    )(qa, doa, qt, dot_t, kta, vta, kn)


def unproject_kernel(own_steps, dq_ref, dk_ref, dv_ref, ln_ref, w_ref, gw_ref, part_ref, gq, gk, gv):
    width = ln_ref.shape[1]
    head = width // HEADS
    rows = ln_ref.shape[0]
    step = pl.program_id(0)

    @pl.when(step == 0)
    def _():
        gq[...] = jnp.zeros_like(gq)
        gk[...] = jnp.zeros_like(gk)
        gv[...] = jnp.zeros_like(gv)

    ln = ln_ref[...]
    dk = dk_ref[...].reshape(width, rows)
    dv = dv_ref[...].reshape(width, rows)
    gk[...] += dot(dk, ln)
    gv[...] += dot(dv, ln)
    part_ref[...] = (dot(w_ref[width : 2 * width, :], dk) + dot(w_ref[2 * width : 3 * width, :], dv)).astype(BF)

    @pl.when(step < own_steps)
    def _():
        dq = jnp.concatenate([dq_ref[h] for h in range(HEADS)], 1)
        gq[...] += dot_tn(ln, dq)

    @pl.when(step == pl.num_programs(0) - 1)
    def _():
        for h in range(HEADS):
            gw_ref[:width, h * head : (h + 1) * head] = gq[:, h * 128 : h * 128 + head]
        gw_ref[width : 2 * width, :] = gk[...].T
        gw_ref[2 * width :, :] = gv[...].T


def unproject(dq, dk, dv, ln, w_input):
    total, width = ln.shape
    _, own, _ = dq.shape
    head = width // HEADS
    block = min(512, own)
    own_steps = own // block
    last = own_steps - 1
    return pl.pallas_call(
        functools.partial(unproject_kernel, own_steps),
        grid=(total // block,),
        in_specs=[
            pl.BlockSpec((HEADS, block, 128), lambda i: (0, jnp.minimum(i, last), 0)),
            pl.BlockSpec((HEADS, head, block), lambda i: (0, 0, i)),
            pl.BlockSpec((HEADS, head, block), lambda i: (0, 0, i)),
            pl.BlockSpec((block, width), lambda i: (i, 0)),
            whole(3 * width, width),
        ],
        out_specs=[whole(3 * width, width), pl.BlockSpec((width, block), lambda i: (0, i))],
        out_shape=[
            jax.ShapeDtypeStruct((3 * width, width), F32),
            jax.ShapeDtypeStruct((width, total), BF),
        ],
        scratch_shapes=[
            pltpu.VMEM((width, HEADS * 128), F32), pltpu.VMEM((width, width), F32), pltpu.VMEM((width, width), F32),
        ],
        compiler_params=params(),
        name="unproject",
    )(dq, dk, dv, ln, w_input)


def finish_kernel(x_ref, gmid_ref, dq_ref, part_ref, other_ref, w_ref, vec_ref, out_ref, gvec_ref, wqt):
    width = x_ref.shape[1]
    head = width // HEADS

    @pl.when(pl.program_id(0) == 0)
    def _():
        gvec_ref[...] = jnp.zeros_like(gvec_ref)
        turned = w_ref[...].astype(F32).T
        for h in range(HEADS):
            wqt[h * 128 : h * 128 + head, :] = turned[h * head : (h + 1) * head, :].astype(BF)
            wqt[h * 128 + head : (h + 1) * 128, :] = jnp.zeros((128 - head, width), BF)

    dq = jnp.concatenate([dq_ref[h] for h in range(HEADS)], 1)
    from_rows = part_ref[...].astype(F32) + other_ref[...].astype(F32)
    grad_ln = dot(dq, wqt[...]) + from_rows.T
    normed, inverse = normalize(x_ref[...].astype(F32))
    gvec_ref[0:1, :] += jnp.sum(grad_ln * normed, 0, keepdims=True)
    gvec_ref[1:2, :] += jnp.sum(grad_ln, 0, keepdims=True)
    out_ref[...] = (gmid_ref[...] + normalize_back(grad_ln * vec_ref[0:1, :], normed, inverse)).astype(BF)


def finish(x, gmid, dq, part, other, w_query, vec):
    own, width = x.shape
    block = min(512, own)
    rows = lambda i: (i, 0)
    lanes = lambda i: (0, i)
    return pl.pallas_call(
        finish_kernel,
        grid=(own // block,),
        in_specs=[
            pl.BlockSpec((block, width), rows),
            pl.BlockSpec((block, width), rows),
            pl.BlockSpec((HEADS, block, 128), lambda i: (0, i, 0)),
            pl.BlockSpec((width, block), lanes),
            pl.BlockSpec((width, block), lanes),
            whole(width, width),
            whole(*vec.shape),
        ],
        out_specs=[pl.BlockSpec((block, width), rows), whole(8, width)],
        out_shape=[jax.ShapeDtypeStruct((own, width), BF), jax.ShapeDtypeStruct((8, width), F32)],
        scratch_shapes=[pltpu.VMEM((HEADS * 128, width), BF)],
        compiler_params=params(),
        name="finish",
    )(x, gmid, dq, part, other, w_query, vec)


def per_device(blk_size, layer_in, matrices, vectors, out_grad):
    seq_count, local_rows, width = layer_in.shape
    group = blk_size // seq_count
    blk = lax.axis_index("blk")
    mine = blk // group
    far = [(b, (b + group) % blk_size) for b in range(blk_size)]
    near = [(b, b ^ 1) for b in range(blk_size)]

    def swap(pair):
        kept = lax.dynamic_index_in_dim(pair, mine, 0, keepdims=False)
        sent = lax.dynamic_index_in_dim(pair, 1 - mine, 0, keepdims=False)
        return jnp.concatenate([kept, lax.ppermute(sent, "blk", far)], 0)

    def unswap(rows):
        kept, sent = rows[:local_rows], rows[local_rows:]
        got = lax.ppermute(sent, "blk", far)
        return jnp.where(mine == 0, jnp.stack([kept, got]), jnp.stack([got, kept]))

    x = swap(layer_in)
    grad = swap(out_grad)
    rows_all = jnp.concatenate([x, lax.ppermute(x, "blk", near)], 0)
    mats = lax.all_gather(matrices, ("ctx", "blk"), axis=0, tiled=True)
    vec = lax.all_gather(vectors, ("ctx", "blk"), axis=0, tiled=True).astype(F32).reshape(-1, width)
    vec = jnp.pad(vec, ((0, 16 - vec.shape[0]), (0, 0)))
    own = x.shape[0]
    ln, qt, kn, kta, vta = prep(rows_all, own, mats[: 3 * width], vec)
    att, lse = attend(qt, kn, kta, vta)
    out, gmid, qa, doa, dot_t, gwo, gup, gdown, gvec = between(x, grad, att, lse, qt, mats[3 * width :], vec)
    layer_out = unswap(out)
    dq, dk, dv = attend_back(qa, doa, qt, dot_t, kta, vta, kn)
    gw, part = unproject(dq, dk, dv, ln, mats[: 3 * width])
    other = lax.ppermute(part[:, own:], "blk", near)
    grad_rows, gvec_in = finish(x, gmid, dq, part[:, :own], other, mats[:width], vec)
    layer_grad = unswap(grad_rows)
    grad_mats = jnp.concatenate([gw, gwo, gup.T, gdown.T], 0)
    grad_vecs = jnp.concatenate([gvec_in[:2], gvec[2:9]], 0).reshape(-1)
    matrices_grad = lax.psum_scatter(grad_mats, ("ctx", "blk"), scatter_dimension=0, tiled=True)
    vectors_grad = lax.psum_scatter(grad_vecs, ("ctx", "blk"), scatter_dimension=0, tiled=True)
    return layer_out, layer_grad, matrices_grad, vectors_grad


def solution(mesh):
    rows = P("ctx", "blk", None)
    flat = P(("ctx", "blk"))
    return jax.shard_map(
        functools.partial(per_device, mesh.shape["blk"]),
        mesh=mesh,
        in_specs=(rows, flat, flat, rows),
        out_specs=(rows, rows, flat, flat),
        check_vma=False,
    )
```

time: 880 us -> 356 us (0.40); the launches traced: 867 us -> 355 us
  matrix products: 304 us -> 0 us
  waiting for transfers between devices: 308 us -> 51.7 us
  Pallas kernels: 0 us -> 163 us
  local copies, waits for them, and re-layouts: 101 us -> 18.7 us
  other arithmetic: 54.5 us -> 9.73 us
    dot_general x124 -> x0, matrix products: 304 us -> none  [the longest x16 57.8 us: score_terms(): jnp.einsum('qhd,khd->hqk', head_grads, value_block, preferred_element_typ...]
    all_gather x9 -> x1, waiting for transfers between devices: 165 us -> 0.01 us  [per_device(): mats = lax.all_gather(matrices, ('ctx', 'blk'), axis=0, tiled=True)]
    pallas_call x0 -> x6, Pallas kernels: none -> 163 us  [the longest x1 80.8 us: attend_back(): pl.pallas_call(attend_back_kernel, grid=(HEADS,), in_specs=[per_head(own,...]
    reduce_scatter x3 -> x0, waiting for transfers between devices: 142 us -> none  [the longest x2 87.5 us: back_scatter_keys(): lax.psum_scatter(key_terms.reshape(length, 2 * width).astype(jnp.bfloat16...]
    while x44 -> x0, local copies, waits for them, and re-layouts: 42.9 us -> none
    unnamed x2 -> x3, waiting for transfers between devices: 0.7 us -> 38 us
    reduce_sum x21 -> x0, other arithmetic: 31.3 us -> none  [the longest x16 22.3 us: absorb_block(): totals = totals * factor + jnp.sum(weights, -1)]
    dynamic_slice x20 -> x0, local copies, waits for them, and re-layouts: 20.6 us -> none  [the longest x16 20.5 us: per_device(): lax.scan(forward_one, None, (query_seq, key_seq, value_seq))]
  transfers between devices with their start and end apart: 12 -> 8, of which waited for: 12 -> 3; matrix products, arithmetic and copies ran while one was open for 6% -> 4% of each run, Pallas kernels for 0% -> 2%
where the time goes in v1:
time: 356 us; the launch traced here: 355 us
  Pallas kernels  163 us (46%)
  blocking collectives  90.3 us (25%)
  waiting for transfers between devices  51.7 us (15%)
  local copies, waits for them, and re-layouts  18.7 us (5%)
  between operations  14.2 us (4%)
  other arithmetic  9.73 us (3%)
  starting transfers between devices  8.21 us (2%)
    unnamed x2, blocking collectives  90.3 us
    pallas_call x1, Pallas kernels, attend_back(): pl.pallas_call(attend_back_kernel, grid=(HEADS,), in_specs=[per_head(own,...  80.8 us
    unnamed x3, waiting for transfers between devices  38 us
    pallas_call x1, Pallas kernels, attend(): pl.pallas_call(attend_kernel, grid=(HEADS,), in_specs=[per_head(head, own...  32.6 us
    pallas_call x1, Pallas kernels, between(): pl.pallas_call(middle_kernel, grid=(own // block,), in_specs=[pl.BlockSpe...  22.4 us
    ppermute x2, waiting for transfers between devices, swap(): return jnp.concatenate([kept, lax.ppermute(sent, 'blk', far)], 0)  11.9 us
    pallas_call x1, Pallas kernels, prep(): pl.pallas_call(functools.partial(prep_kernel, own_steps), grid=(steps,),...  10.7 us
    pallas_call x1, Pallas kernels, unproject(): pl.pallas_call(functools.partial(unproject_kernel, own_steps), grid=(tota...  10 us
  transfers between devices with their start and end apart: 8, of which 3 were waited for; matrix products, arithmetic and copies ran while one was open for 4% of the time, Pallas kernels for 2%

profile of v1, /device:TPU:0, one launch (start us, length us, event | category | flops | bytes accessed | tf_op | source)
XLA Modules:
  0.0 355.4 jit_solution(10565354962261053871)
XLA Ops:
  7.2 0.0 all-gather.2.cloned.1.call-start
  7.2 0.7 all-gather.2.cloned.1.call-update
  7.9 0.0 reduce-scatter.4.cloned.1.call-start
  8.0 1.4 dynamic-slice_bitcast_fusion.3
  9.3 3.0 collective-permute-start
  12.4 11.9 %collective-permute-done = bf16[1024,256]{1,0:T(8,128)(2,1)S(1)} collective-permute-done((bf16[1024,256]{1,0:T(8,128)(2,1)S(1)}, bf16[1024,256]{1,0:T(8,128)(2,1)S(1)}, u32[]{:S(2)}, u32[]{:S(2)}) %collective-permute-start) | collective-permute-done | bytes 524320 | tf_op jit(solution)/shard_map/ppermute | solution.py:517
  24.3 0.1 pad_maximum_fusion.2.x_ref
  24.4 0.0 copy-start
  24.4 0.1 collective-permute-start.2
  24.5 0.1 dynamic-slice_bitcast_fusion.1
  24.6 2.2 collective-permute-start.1
  26.7 0.2 dynamic-update-slice
  26.9 48.0 %all-reduce.1 = bf16[2304]{0:T(1024)(128)(2,1)S(1)} all-reduce(bf16[2304]{0:T(1024)(128)(2,1)S(1)} %dynamic-update-slice), channel_id=1, replica_groups=mesh['ctx'=8,'blk'=4] {'ctx','blk'}, use_global_device_ids=true, to_apply=%add.1 | all-reduce | flops 2304 | bytes 9216
  74.9 0.6 pad_convert_fusion.vec_ref
  75.5 0.0 collective-permute-done.1
  75.5 2.1 pad_maximum_fusion.3.g_ref
  77.6 0.0 collective-permute-done.2
  77.6 2.7 pad_maximum_fusion.1.x_ref
  80.3 1.8 slice.45.w_ref
  82.0 10.7 %project.1 = (bf16[4096,256]{1,0:T(8,128)(2,1)}, bf16[4,64,2048]{2,1,0:T(8,128)(2,1)}, bf16[4,4096,128]{2,1,0:T(8,128)(2,1)}, bf16[4,80,4096]{2,1,0:T(8,128)(2,1)}, bf16[4,80,4096]{2,1,0:T(8,128)(2,1)}) custom-call(bf16[4096,256]{1,0:T(8,128)(2,1)} %pad_maximum_fusion.1.x_ref, bf16[768,256]{1,0:T(8,128)(2,1)} %slice.45.w_ref, f32[16,256]{1,0:T(8,128)} %pad_convert_fusion.vec_ref), custom_call_target="tpu_custom_call" | custom-call | tf_op jit(solution)/shard_map/project/pallas_call | solution.py:102
  92.7 32.6 %attend.1 = (f32[4,64,2048]{2,1,0:T(8,128)}, f32[4,8,2048]{2,1,0:T(8,128)}) custom-call(bf16[4,64,2048]{2,1,0:T(8,128)(2,1)} %get-tuple-element.27.qt_ref, bf16[4,4096,128]{2,1,0:T(8,128)(2,1)} %get-tuple-element.28.kn_ref, bf16[4,80,4096]{2,1,0:T(8,128)(2,1)} %get-tuple-element.29.kta_ref, bf16[4,80,4096]{2,1,0:T(8,128)(2,1)} %get-tuple-element.30.vta_ref), custom_call_target="tpu_custom_call" | custom-call | tf_op jit(solution)/shard_map/attend/pallas_call | solution.py:192
  125.4 1.1 slice.46.w_ref
  126.5 22.4 %between.1 = (bf16[2048,256]{1,0:T(8,128)(2,1)}, f32[2048,256]{1,0:T(8,128)}, bf16[4,2048,128]{2,1,0:T(8,128)(2,1)}, bf16[4,2048,128]{2,1,0:T(8,128)(2,1)}, bf16...) custom-call(bf16[2048,256]{1,0:T(8,128)(2,1)} %copy-done, ...), custom_call_target="tpu_custom_call" | custom-call | tf_op jit(solution)/shard_map/between/pallas_call | solution.py:299
  148.9 1.1 copy.12
  149.9 80.8 %attend_back.1 = (bf16[4,2048,128]{2,1,0:T(8,128)(2,1)}, bf16[4,64,4096]{2,1,0:T(8,128)(2,1)}, bf16[4,64,4096]{2,1,0:T(8,128)(2,1)}) custom-call(bf16[4,2048,128]{2,1,0:T(8,128)(2,1)} %get-tuple-element.35.qa_ref, bf16[4,2048,128]{2,1,0:T(8,128)(2,1)} %get-tuple-element.36.doa_ref, bf16[4,64,2048]{2,1,0:T(8,128)(2,1)} %get-tuple-element.27.qt_ref, ...), custom_call_target="tpu_custom_call" | custom-call | tf_op jit(solution)/shard_map/attend_back/pallas_call | solution.py:379
  230.8 10.0 %unproject.1 = (f32[768,256]{1,0:T(8,128)}, bf16[256,4096]{1,0:T(8,128)(2,1)}) custom-call(bf16[4,2048,128]{2,1,0:T(8,128)(2,1)} %get-tuple-element.38.dq_ref, bf16[4,64,4096]{2,1,0:T(8,128)(2,1)} %get-tuple-element.39.dk_ref, bf16[4,64,4096]{2,1,0:T(8,128)(2,1)} %get-tuple-element.40.dv_ref, bf16[4096,256]{1,0:T(8,128)(2,1)} %get-tuple-element.41.ln_ref, ...), custom_call_target="tpu_custom_call" | custom-call | tf_op jit(solution)/shard_map/unproject/pallas_call | solution.py:437
  240.8 2.3 copy.11
  243.1 2.0 pad_maximum_fusion
  245.2 2.3 copy.14
  247.5 0.0 reduce-scatter.4.cloned.1.call-update
  247.5 1.6 copy-done.1
  249.1 1.1 fusion
  250.2 0.5 copy-done.4
  250.7 0.1 slice_bitcast_fusion.1
  250.8 2.3 collective-permute-start.3
  253.1 1.6 slice.47.w_ref
  254.7 1.0 copy-done.3
  255.7 5.9 %finish.1 = (bf16[2048,256]{1,0:T(8,128)(2,1)}, f32[8,256]{1,0:T(8,128)}) custom-call(bf16[2048,256]{1,0:T(8,128)(2,1)} %copy-done, f32[2048,256]{1,0:T(8,128)} %get-tuple-element.34.gmid_ref, bf16[4,2048,128]{2,1,0:T(8,128)(2,1)} %get-tuple-element.38.dq_ref, bf16[256,2048]{1,0:T(8,128)(2,1)} %get-tuple-element.59.part_ref, bf16[256,2048]{1,0:T(8,128)(2,1)} %copy-done.3, ...), custom_call_target="tpu_custom_call" | custom-call | tf_op jit(solution)/shard_map/finish/pallas_call | solution.py:486
  261.6 1.3 slice_bitcast_fusion
  262.9 0.5 collective-permute-start.5
  263.5 1.8 collective-permute-done.3
  265.2 1.1 maximum_select_fusion
  266.4 0.7 slice.43
  267.1 42.4 %all-reduce.2 = f32[2304]{0:T(1024)S(1)} all-reduce(f32[2304]{0:T(1024)S(1)} %reshape.16), channel_id=3, replica_groups=mesh['ctx'=8,'blk'=4] {'ctx','blk'}, use_global_device_ids=true, to_apply=%region_1.2.clone | all-reduce | flops 2304 | bytes 18432
  309.5 0.6 dynamic-slice
  310.1 0.0 collective-permute-done.5
  310.1 1.1 maximum_select_fusion.1
  311.2 37.3 %reduce-scatter.4.cloned.1.call-done = f32[96,256]{1,0:T(8,128)} async-done(((f32[3072,256]{1,0:T(8,128)}), f32[96,256]{1,0:T(8,128)}) %reduce-scatter.4.cloned.1.call-update) | async-done | bytes 98320
  (20 shorter events, 0.1 us)
Async XLA Ops:
  7.2 73.1 %all-gather.2.cloned.1.call-start = ((), (), s32[]{:S(2)}) async-start(), calls=%async_computation.1 | async-start | bytes 1622016 | tf_op jit(solution)/shard_map/all_gather | solution.py:527
  7.9 340.6 %reduce-scatter.4.cloned.1.call-start = ((), (), s32[]{:S(2)}) async-start(), calls=%async_computation.2 | async-start | bytes 3244032
  8.0 16.5 %copy-start.5 = (bf16[2,1024,256]{2,1,0:T(8,128)(2,1)S(1)}, bf16[2,1024,256]{2,1,0:T(8,128)(2,1)}, u32[]{:S(2)}) copy-start(bf16[2,1024,256]{2,1,0:T(8,128)(2,1)} %param.7) | copy-start | bytes 3145732
  9.3 15.0 %collective-permute-start = (bf16[1024,256]{1,0:T(8,128)(2,1)S(1)}, bf16[1024,256]{1,0:T(8,128)(2,1)S(1)}, u32[]{:S(2)}, u32[]{:S(2)}) collective-permute-start(bf16[1024,256]{1,0:T(8,128)(2,1)S(1)} %get-tuple-element.67), channel_id=1, source_target_pairs={{0,2},{1,3},{2,0},{3,1},{4,6},{5,7},{6,4},{7,5},{8,10},{9,11},{10,... | collective-permute-start | bytes 1572872 | tf_op jit(solution)/shard_map/ppermute | solution.py:517
  24.3 2.4 copy-start.7
  24.4 53.2 %copy-start = (bf16[2048,256]{1,0:T(8,128)(2,1)}, bf16[2048,256]{1,0:T(8,128)(2,1)S(1)}, u32[]{:S(2)}) copy-start(bf16[2048,256]{1,0:T(8,128)(2,1)S(1)} %pad_maximum_fusion.2.x_ref) | copy-start | bytes 3145732
  24.4 53.2 %collective-permute-start.2 = (bf16[2048,256]{1,0:T(8,128)(2,1)S(1)}, bf16[2048,256]{1,0:T(8,128)(2,1)}, u32[]{:S(2)}, u32[]{:S(2)}) collective-permute-start(bf16[2048,256]{1,0:T(8,128)(2,1)S(1)} %pad_maximum_fusion.2.x_ref), channel_id=1, source_target_pairs={{0,1},{1,0},{2,3},{3,2},{4,5},{5,4},{6,7},{7,6},{8,9},{9,8},{10,11... | collective-permute-start | bytes 3145736 | tf_op jit(solution)/shard_map/ppermute | solution.py:526
  24.6 51.0 %collective-permute-start.1 = (bf16[1024,256]{1,0:T(8,128)(2,1)S(1)}, bf16[1024,256]{1,0:T(8,128)(2,1)}, u32[]{:S(2)}, u32[]{:S(2)}) collective-permute-start(bf16[1024,256]{1,0:T(8,128)(2,1)S(1)} %get-tuple-element.65), channel_id=1, source_target_pairs={{0,2},{1,3},{2,0},{3,1},{4,6},{5,7},{6,4},{7,5},{8,10},{9,11},{10,... | collective-permute-start | bytes 1572872 | tf_op jit(solution)/shard_map/ppermute | solution.py:517
  92.7 32.6 %copy-start.2 = (bf16[3072,256]{1,0:T(8,128)(2,1)S(1)}, bf16[3072,256]{1,0:T(8,128)(2,1)}, u32[]{:S(2)}) copy-start(bf16[3072,256]{1,0:T(8,128)(2,1)} %all-gather.2.cloned.1.call-done) | copy-start | bytes 4718596
  247.5 1.6 copy-start.1
  249.1 1.6 copy-start.4
  250.2 4.5 %collective-permute-start.4 = (bf16[256,2048]{1,0:T(8,128)(2,1)S(1)}, bf16[256,2048]{1,0:T(8,128)(2,1)S(1)}, u32[]{:S(2)}, u32[]{:S(2)}) collective-permute-start(bf16[256,2048]{1,0:T(8,128)(2,1)S(1)} %get-tuple-element.58), channel_id=1, source_target_pairs={{0,1},{1,0},{2,3},{3,2},{4,5},{5,4},{6,7},{7,6},{8,9},{9,8},{10,11... | collective-permute-start | bytes 3145736 | tf_op jit(solution)/shard_map/ppermute | solution.py:537
  250.8 14.5 %collective-permute-start.3 = (bf16[1024,256]{1,0:T(8,128)(2,1)S(1)}, bf16[1024,256]{1,0:T(8,128)(2,1)S(1)}, u32[]{:S(2)}, u32[]{:S(2)}) collective-permute-start(bf16[1024,256]{1,0:T(8,128)(2,1)S(1)} %get-tuple-element.63), channel_id=1, source_target_pairs={{0,2},{1,3},{2,0},{3,1},{4,6},{5,7},{6,4},{7,5},{8,10},{9,11},{10,... | collective-permute-start | bytes 1572872 | tf_op jit(solution)/shard_map/ppermute | solution.py:521
  254.7 1.0 copy-start.3
  261.6 1.8 copy-start.6
  262.9 47.1 %collective-permute-start.5 = (bf16[1024,256]{1,0:T(8,128)(2,1)S(1)}, bf16[1024,256]{1,0:T(8,128)(2,1)S(1)}, u32[]{:S(2)}, u32[]{:S(2)}) collective-permute-start(bf16[1024,256]{1,0:T(8,128)(2,1)S(1)} %get-tuple-element.61), channel_id=1, source_target_pairs={{0,2},{1,3},{2,0},{3,1},{4,6},{5,7},{6,4},{7,5},{8,10},{9,11},{10,... | collective-permute-start | bytes 1572872 | tf_op jit(solution)/shard_map/ppermute | solution.py:521
Sparse Core Ops, SparseCore 0:
  10.9 57.7 all-gather.1
  247.7 100.8 reduce-scatter.3

commit v2 on v1

--- a/solution.py
+++ b/solution.py
@@ -53,6 +53,129 @@
         - jnp.mean(grad_hat, -1, keepdims=True)
         - normed * jnp.mean(grad_hat * normed, -1, keepdims=True)
     )
+
+
+MESH = pl.DeviceIdType.MESH
+
+
+def send(source, target, sent, received, device):
+    copy = pltpu.make_async_remote_copy(
+        src_ref=source, dst_ref=target, send_sem=sent, recv_sem=received, device_id=device, device_id_type=MESH
+    )
+    copy.start()
+    return copy
+
+
+def greet(devices):
+    barrier = pltpu.get_barrier_semaphore()
+    for device in devices:
+        pl.semaphore_signal(barrier, inc=1, device_id=device, device_id_type=MESH)
+    pl.semaphore_wait(barrier, len(devices))
+
+
+def partners(blk_size):
+    ctx, blk = lax.axis_index("ctx"), lax.axis_index("blk")
+    half = blk_size // 2
+    return ctx, blk, blk + 1 - 2 * lax.rem(blk, 2), lax.rem(blk + half, blk_size), lax.div(blk, half)
+
+
+def exchange_kernel(
+    ctx_size, blk_size, x_ref, w_ref, rows_ref, all_ref,
+    far_sent, far_got, near_sent, near_got, relay_sent, relay_got, own_sem,
+    first_sent, first_got, second_sent, second_got, third_sent, third_got, keep_sem,
+):
+    ctx, blk, near, far, mine = partners(blk_size)
+    length = x_ref.shape[1]
+    owners = all_ref.shape[0] // blk_size
+    chunks = far_sent.shape[0]
+    size = length // chunks
+    others = [lax.rem(ctx + step, ctx_size) for step in range(1, ctx_size)]
+    greet([(ctx, near), (ctx, far)] + [(other, blk) for other in others])
+
+    @pl.when(ctx < owners)
+    def _():
+        keep = pltpu.make_async_copy(w_ref, all_ref.at[ctx * blk_size + blk], keep_sem)
+        keep.start()
+        for step, other in enumerate(others):
+            send(w_ref, all_ref.at[ctx * blk_size + blk], first_sent.at[step], first_got.at[ctx], (other, blk))
+
+    far_copies = []
+    for c in range(chunks):
+        part = pl.ds(c * size, size)
+        far_copies.append(
+            send(x_ref.at[1 - mine, part], rows_ref.at[pl.ds(length + c * size, size)], far_sent.at[c], far_got.at[c], (ctx, far))
+        )
+    near_copy = send(x_ref.at[mine], rows_ref.at[pl.ds(2 * length, length)], near_sent, near_got, (ctx, near))
+    own_copy = pltpu.make_async_copy(x_ref.at[mine], rows_ref.at[pl.ds(0, length)], own_sem)
+    own_copy.start()
+
+    @pl.when(ctx < owners)
+    def _():
+        pltpu.make_async_copy(w_ref, all_ref.at[ctx * blk_size + blk], keep_sem).wait()
+
+    def copy_of(slot, sent, got, device):
+        return pltpu.make_async_remote_copy(
+            src_ref=all_ref.at[slot], dst_ref=all_ref.at[slot], send_sem=sent, recv_sem=got,
+            device_id=device, device_id_type=MESH,
+        )
+
+    for o in range(owners):
+        @pl.when(ctx != o)
+        def _():
+            copy_of(o * blk_size + blk, first_sent.at[0], first_got.at[o], (ctx, near)).wait_recv()
+
+        copy_of(o * blk_size + blk, second_sent.at[o], second_got.at[o], (ctx, far)).start()
+        copy_of(o * blk_size + blk, third_sent.at[o], third_got.at[o], (ctx, near)).start()
+    relays = []
+    for c in range(chunks):
+        far_copies[c].wait_recv()
+        here = rows_ref.at[pl.ds(length + c * size, size)]
+        there = rows_ref.at[pl.ds(3 * length + c * size, size)]
+        relays.append(send(here, there, relay_sent.at[c], relay_got.at[c], (ctx, near)))
+    for o in range(owners):
+        copy_of(o * blk_size + far, second_sent.at[o], second_got.at[o], (ctx, far)).wait_recv()
+        copy_of(o * blk_size + far, third_sent.at[owners + o], third_got.at[owners + o], (ctx, near)).start()
+
+    for o in range(owners):
+        copy_of(o * blk_size + blk, second_sent.at[o], second_got.at[o], (ctx, far)).wait_send()
+        for turn in range(2):
+            copy_of(o * blk_size + blk, third_sent.at[turn * owners + o], third_got.at[turn * owners + o], (ctx, near)).wait()
+    for c in range(chunks):
+        far_copies[c].wait_send()
+        relays[c].wait()
+    near_copy.wait()
+    own_copy.wait()
+
+    @pl.when(ctx < owners)
+    def _():
+        for step, other in enumerate(others):
+            pltpu.make_async_remote_copy(
+                src_ref=w_ref, dst_ref=all_ref.at[ctx * blk_size + blk], send_sem=first_sent.at[step],
+                recv_sem=first_got.at[ctx], device_id=(other, blk), device_id_type=MESH,
+            ).wait_send()
+
+
+def exchange(ctx_size, blk_size, layer_in, block, owners):
+    seq_count, length, width = layer_in.shape
+    chunks = 4 if length % 64 == 0 else 1
+    dma = pltpu.SemaphoreType.DMA
+    place = pl.BlockSpec(memory_space=pl.ANY)
+    return pl.pallas_call(
+        functools.partial(exchange_kernel, ctx_size, blk_size),
+        in_specs=[place] * 2,
+        out_specs=[place] * 2,
+        out_shape=[
+            jax.ShapeDtypeStruct((4 * length, width), BF),
+            jax.ShapeDtypeStruct((owners * blk_size, *block.shape), BF),
+        ],
+        scratch_shapes=[
+            dma((chunks,)), dma((chunks,)), dma, dma, dma((chunks,)), dma((chunks,)), dma,
+            dma((ctx_size - 1,)) if ctx_size > 1 else dma((1,)), dma((owners,)), dma((owners,)), dma((owners,)),
+            dma((2 * owners,)), dma((2 * owners,)), dma,
+        ],
+        compiler_params=params(collective_id=1, has_side_effects=True),
+        name="exchange",
+    )(layer_in, block)
 
 
 def prep_kernel(own_steps, x_ref, w_ref, vec_ref, ln_ref, qt_ref, kn_ref, kta_ref, vta_ref, wt, wkp):
@@ -289,7 +412,7 @@
 
 
 def between(x, grad, att, lse, qt, weights, vec):
-    own, width = x.shape
+    own, width = grad.shape
     head = width // HEADS
     hidden_width = (weights.shape[0] - width) // 2
     block = min(512, own)
@@ -395,7 +518,7 @@
     )(qa, doa, qt, dot_t, kta, vta, kn)
 
 
-def unproject_kernel(own_steps, dq_ref, dk_ref, dv_ref, ln_ref, w_ref, gw_ref, part_ref, gq, gk, gv):
+def unproject_kernel(own_steps, places, dq_ref, dk_ref, dv_ref, ln_ref, w_ref, gw_ref, part_ref, gq, gk, gv):
     width = ln_ref.shape[1]
     head = width // HEADS
     rows = ln_ref.shape[0]
@@ -421,21 +544,29 @@
 
     @pl.when(step == pl.num_programs(0) - 1)
     def _():
-        for h in range(HEADS):
-            gw_ref[:width, h * head : (h + 1) * head] = gq[:, h * 128 : h * 128 + head]
-        gw_ref[width : 2 * width, :] = gk[...].T
-        gw_ref[2 * width :, :] = gv[...].T
-
-
-def unproject(dq, dk, dv, ln, w_input):
+        narrow = jnp.concatenate([gq[:, h * 128 : h * 128 + head] for h in range(HEADS)], 1)
+        grads = jnp.concatenate([narrow, gk[...].T, gv[...].T], 0)
+        blk_size, owners, per = places
+        filler = jnp.zeros((gw_ref.shape[2] - per, width), F32)
+        for slot in range(blk_size * owners):
+            o, k = slot // blk_size, slot % blk_size
+            piece = grads[slot * per : (slot + 1) * per, :]
+            if filler.shape[0]:
+                piece = jnp.concatenate([piece, filler], 0)
+            gw_ref[k, o] = piece.astype(BF)
+
+
+def unproject(dq, dk, dv, ln, w_input, places):
     total, width = ln.shape
     _, own, _ = dq.shape
     head = width // HEADS
-    block = min(512, own)
+    block = min(1024, own)
     own_steps = own // block
     last = own_steps - 1
+    blk_size, owners, per = places
+    slots = (blk_size, owners, -(-per // 16) * 16, width)
     return pl.pallas_call(
-        functools.partial(unproject_kernel, own_steps),
+        functools.partial(unproject_kernel, own_steps, places),
         grid=(total // block,),
         in_specs=[
             pl.BlockSpec((HEADS, block, 128), lambda i: (0, jnp.minimum(i, last), 0)),
@@ -444,9 +575,9 @@
             pl.BlockSpec((block, width), lambda i: (i, 0)),
             whole(3 * width, width),
         ],
-        out_specs=[whole(3 * width, width), pl.BlockSpec((width, block), lambda i: (0, i))],
+        out_specs=[whole(*slots), pl.BlockSpec((width, block), lambda i: (0, i))],
         out_shape=[
-            jax.ShapeDtypeStruct((3 * width, width), F32),
+            jax.ShapeDtypeStruct(slots, BF),
             jax.ShapeDtypeStruct((width, total), BF),
         ],
         scratch_shapes=[
@@ -457,90 +588,277 @@
     )(dq, dk, dv, ln, w_input)
 
 
-def finish_kernel(x_ref, gmid_ref, dq_ref, part_ref, other_ref, w_ref, vec_ref, out_ref, gvec_ref, wqt):
-    width = x_ref.shape[1]
+def finish_kernel(
+    ctx_size, blk_size, x_hbm, gmid_hbm, dq_hbm, part_hbm, gw_hbm, w_ref, vec_ref,
+    grad_ref, gw_ref, gvec_ref,
+    x, gmid, dq, part, other, gw_own, gw_first, gw_pass, gw_second, gw_sum, gw_third, gw_fourth,
+    made, vec_own, vec_near, vec_pair, vec_far, vec_four, vec_group, vec_all, vec_every, wqt,
+    load_sem, part_sent, part_got, first_sent, first_got, second_sent, second_got, third_sent, third_got,
+    fourth_sent, fourth_got, out_sent, out_got, keep_sem, vn_sent, vn_got, vf_sent, vf_got, vg_sent, vg_got,
+    va_sent, va_got,
+):
+    ctx, blk, near, far, mine = partners(blk_size)
+    width = x.shape[1]
     head = width // HEADS
-
-    @pl.when(pl.program_id(0) == 0)
-    def _():
-        gvec_ref[...] = jnp.zeros_like(gvec_ref)
-        turned = w_ref[...].astype(F32).T
-        for h in range(HEADS):
-            wqt[h * 128 : h * 128 + head, :] = turned[h * head : (h + 1) * head, :].astype(BF)
-            wqt[h * 128 + head : (h + 1) * 128, :] = jnp.zeros((128 - head, width), BF)
-
-    dq = jnp.concatenate([dq_ref[h] for h in range(HEADS)], 1)
-    from_rows = part_ref[...].astype(F32) + other_ref[...].astype(F32)
-    grad_ln = dot(dq, wqt[...]) + from_rows.T
-    normed, inverse = normalize(x_ref[...].astype(F32))
-    gvec_ref[0:1, :] += jnp.sum(grad_ln * normed, 0, keepdims=True)
-    gvec_ref[1:2, :] += jnp.sum(grad_ln, 0, keepdims=True)
-    out_ref[...] = (gmid_ref[...] + normalize_back(grad_ln * vec_ref[0:1, :], normed, inverse)).astype(BF)
-
-
-def finish(x, gmid, dq, part, other, w_query, vec):
-    own, width = x.shape
-    block = min(512, own)
-    rows = lambda i: (i, 0)
-    lanes = lambda i: (0, i)
+    own = x.shape[0]
+    length = own // 2
+    owners = gw_hbm.shape[1]
+    groups = ctx_size // owners
+    core = lax.rem(blk, 2)
+    group, place = lax.div(ctx, owners), lax.rem(ctx, owners)
+    peers = [lax.rem(place + step, owners) for step in range(1, owners)]
+    peer_devices = [(group * owners + peer, blk) for peer in peers]
+    others = [lax.rem(group + step, groups) for step in range(1, groups)]
+    other_devices = [(other_group * owners + place, blk) for other_group in others]
+    greet([(ctx, near), (ctx, far)] + peer_devices + other_devices)
+
+    first = [send(gw_hbm.at[2 * y + 1 - core], gw_first.at[y], first_sent.at[y], first_got.at[y], (ctx, near)) for y in range(2)]
+    halves = []
+    for half in (1, 0):
+        there = pl.ds(half * length, length)
+        halves.append(
+            send(part_hbm.at[:, pl.ds(own + half * length, length)], other.at[:, there], part_sent.at[half], part_got.at[half], (ctx, near))
+        )
+    loads = [
+        pltpu.make_async_copy(gw_hbm.at[2 * y + core], gw_own.at[y], load_sem.at[y]) for y in range(2)
+    ]
+    for half in (1, 0):
+        rows = pl.ds(half * length, length)
+        base = 2 + 4 * half
+        loads += [
+            pltpu.make_async_copy(x_hbm.at[rows], x.at[rows], load_sem.at[base]),
+            pltpu.make_async_copy(gmid_hbm.at[rows], gmid.at[rows], load_sem.at[base + 1]),
+            pltpu.make_async_copy(dq_hbm.at[:, rows], dq.at[:, rows], load_sem.at[base + 2]),
+            pltpu.make_async_copy(part_hbm.at[:, rows], part.at[:, rows], load_sem.at[base + 3]),
+        ]
+    for load in loads:
+        load.start()
+
+    turned = w_ref[...].astype(F32).T
+    for h in range(HEADS):
+        wqt[h * 128 : h * 128 + head, :] = turned[h * head : (h + 1) * head, :].astype(BF)
+        wqt[h * 128 + head : (h + 1) * 128, :] = jnp.zeros((128 - head, width), BF)
+
+    gain = vec_ref[0:1, :]
+    size = min(512, length)
+    state = [jnp.zeros((1, width), F32), jnp.zeros((1, width), F32)]
+
+    def rows_back(low):
+        rows = slice(low, low + size)
+        from_q = dot(jnp.concatenate([dq[h, rows, :] for h in range(HEADS)], 1), wqt[...])
+        grad_ln = from_q + (part[:, rows].astype(F32) + other[:, rows].astype(F32)).T
+        normed, inverse = normalize(x[rows, :].astype(F32))
+        state[0] = state[0] + jnp.sum(grad_ln * normed, 0, keepdims=True)
+        state[1] = state[1] + jnp.sum(grad_ln, 0, keepdims=True)
+        made[rows, :] = (gmid[rows, :] + normalize_back(grad_ln * gain, normed, inverse)).astype(BF)
+
+    sums = (2, owners) + gw_hbm.shape[2:]
+
+    for y in range(2):
+        loads[y].wait()
+        first[y].wait_recv()
+    for y in range(2):
+        gw_pass[y] = (gw_own[y].astype(F32) + gw_first[y].astype(F32)).astype(BF)
+    second = send(gw_pass.at[1 - mine], gw_second, second_sent, second_got, (ctx, far))
+
+    for load in loads[2:6]:
+        load.wait()
+    halves[0].wait_recv()
+    outs = []
+    chunk = 0
+    for low in range(length, own, size):
+        rows_back(low)
+        outs.append(
+            send(
+                made.at[pl.ds(low, size)], grad_ref.at[mine, pl.ds(low - length, size)],
+                out_sent.at[chunk], out_got.at[chunk], (ctx, far),
+            )
+        )
+        chunk += 1
+
+    second.wait_recv()
+    gw_sum[...] = (gw_pass[mine].astype(F32) + gw_second[...].astype(F32)).astype(BF)
+    third = [
+        send(gw_sum.at[peer], gw_third.at[place], third_sent.at[step], third_got.at[place], peer_devices[step])
+        for step, peer in enumerate(peers)
+    ]
+
+    for load in loads[6:]:
+        load.wait()
+    halves[1].wait_recv()
+    keeps = []
+    for low in range(0, length, size):
+        rows_back(low)
+        keeps.append(
+            pltpu.make_async_copy(made.at[pl.ds(low, size)], grad_ref.at[mine, pl.ds(low, size)], keep_sem.at[low // size])
+        )
+        keeps[-1].start()
+
+    row = lax.broadcasted_iota(jnp.int32, (8, width), 0)
+    vec_own[...] = jnp.where(row == 0, state[0], jnp.where(row == 1, state[1], 0.0))
+    to_near = send(vec_own, vec_near, vn_sent, vn_got, (ctx, near))
+
+    def from_peer(slot, holder, got, which):
+        return pltpu.make_async_remote_copy(
+            src_ref=holder.at[slot], dst_ref=holder.at[slot], send_sem=got.at[slot], recv_sem=got.at[slot],
+            device_id=(ctx, near), device_id_type=MESH,
+        )
+
+    total = gw_sum[place].astype(F32)
+    for slot in range(owners):
+        @pl.when(place != slot)
+        def _():
+            from_peer(slot, gw_third, third_got, None).wait_recv()
+
+        total = total + jnp.where(place != slot, gw_third[slot].astype(F32), 0.0)
+    gw_ref[...] = total
+    gw_own[0, 0] = total.astype(BF)
+    if groups > 1:
+        @pl.when(group > 0)
+        def _():
+            send(gw_own.at[0, 0], gw_fourth.at[group - 1], fourth_sent, fourth_got.at[group - 1], (place, blk))
+
+    to_near.wait_recv()
+    vec_pair[...] = vec_own[...] + vec_near[...]
+    to_far = send(vec_pair, vec_far, vf_sent, vf_got, (ctx, far))
+    to_far.wait_recv()
+    vec_four[...] = vec_pair[...] + vec_far[...]
+    to_peers = [
+        send(vec_four, vec_group.at[place], vg_sent.at[step], vg_got.at[place], device)
+        for step, device in enumerate(peer_devices)
+    ]
+    vec_total = vec_four[...]
+    for slot in range(owners):
+        @pl.when(place != slot)
+        def _():
+            from_peer(slot, vec_group, vg_got, None).wait_recv()
+
+        vec_total = vec_total + jnp.where(place != slot, vec_group[slot], 0.0)
+    vec_all[...] = vec_total
+    to_others = [
+        send(vec_all, vec_every.at[group], va_sent.at[step], va_got.at[group], device)
+        for step, device in enumerate(other_devices)
+    ]
+    for slot in range(groups):
+        @pl.when(group != slot)
+        def _():
+            from_peer(slot, vec_every, va_got, None).wait_recv()
+
+        vec_total = vec_total + jnp.where(group != slot, vec_every[slot], 0.0)
+    gvec_ref[...] = vec_total
+
+    if groups > 1:
+        @pl.when(group == 0)
+        def _():
+            total = gw_ref[...]
+            for slot in range(groups - 1):
+                from_peer(slot, gw_fourth, fourth_got, None).wait_recv()
+                total = total + gw_fourth[slot].astype(F32)
+            gw_ref[...] = total
+
+        @pl.when(group > 0)
+        def _():
+            pltpu.make_async_remote_copy(
+                src_ref=gw_own.at[0, 0], dst_ref=gw_fourth.at[group - 1], send_sem=fourth_sent,
+                recv_sem=fourth_got.at[group - 1], device_id=(place, blk), device_id_type=MESH,
+            ).wait_send()
+
+    for copy in first + halves + [second] + third + [to_near, to_far] + to_peers + to_others:
+        copy.wait_send()
+    for copy in outs:
+        copy.wait()
+    for copy in keeps:
+        copy.wait()
+
+
+def finish(ctx_size, blk_size, rows_all, gmid, dq, part, gw, w_query, vec):
+    own, width = gmid.shape
+    length = own // 2
+    _, owners, per, _ = gw.shape
+    groups = ctx_size // owners
+    dma = pltpu.SemaphoreType.DMA
+    place = pl.BlockSpec(memory_space=pl.ANY)
+    vmem = pl.BlockSpec(memory_space=pltpu.VMEM)
+    chunks = length // min(512, length)
+    low = lambda *shape: pltpu.VMEM(shape, BF)
+    single = lambda *shape: pltpu.VMEM(shape, F32)
     return pl.pallas_call(
-        finish_kernel,
-        grid=(own // block,),
-        in_specs=[
-            pl.BlockSpec((block, width), rows),
-            pl.BlockSpec((block, width), rows),
-            pl.BlockSpec((HEADS, block, 128), lambda i: (0, i, 0)),
-            pl.BlockSpec((width, block), lanes),
-            pl.BlockSpec((width, block), lanes),
-            whole(width, width),
-            whole(*vec.shape),
-        ],
-        out_specs=[pl.BlockSpec((block, width), rows), whole(8, width)],
-        out_shape=[jax.ShapeDtypeStruct((own, width), BF), jax.ShapeDtypeStruct((8, width), F32)],
-        scratch_shapes=[pltpu.VMEM((HEADS * 128, width), BF)],
-        compiler_params=params(),
+        functools.partial(finish_kernel, ctx_size, blk_size),
+        in_specs=[place] * 5 + [vmem] * 2,
+        out_specs=[place, vmem, vmem],
+        out_shape=[
+            jax.ShapeDtypeStruct((2, length, width), BF),
+            jax.ShapeDtypeStruct((per, width), F32),
+            jax.ShapeDtypeStruct((8, width), F32),
+        ],
+        scratch_shapes=[
+            low(own, width), single(own, width), low(HEADS, own, 128), low(width, own), low(width, own),
+            low(2, owners, per, width), low(2, owners, per, width), low(2, owners, per, width),
+            low(owners, per, width), low(owners, per, width), low(owners, per, width), low(max(groups - 1, 1), per, width),
+            low(own, width), single(8, width), single(8, width), single(8, width), single(8, width), single(8, width),
+            single(owners, 8, width), single(8, width), single(groups, 8, width), low(HEADS * 128, width),
+            dma((10,)), dma((2,)), dma((2,)), dma((2,)), dma((2,)), dma, dma, dma((max(owners - 1, 1),)), dma((owners,)),
+            dma, dma((max(groups - 1, 1),)), dma((chunks,)), dma((chunks,)), dma((chunks,)), dma, dma, dma, dma,
+            dma((max(owners - 1, 1),)), dma((owners,)), dma((max(groups - 1, 1),)), dma((groups,)),
+        ],
+        compiler_params=params(collective_id=2, has_side_effects=True),
         name="finish",
-    )(x, gmid, dq, part, other, w_query, vec)
-
-
-def per_device(blk_size, layer_in, matrices, vectors, out_grad):
+    )(rows_all, gmid, dq, part, gw, w_query, vec)
+
+
+def per_device(ctx_size, blk_size, layer_in, matrices, vectors, out_grad):
     seq_count, local_rows, width = layer_in.shape
-    group = blk_size // seq_count
-    blk = lax.axis_index("blk")
-    mine = blk // group
-    far = [(b, (b + group) % blk_size) for b in range(blk_size)]
-    near = [(b, b ^ 1) for b in range(blk_size)]
-
-    def swap(pair):
-        kept = lax.dynamic_index_in_dim(pair, mine, 0, keepdims=False)
-        sent = lax.dynamic_index_in_dim(pair, 1 - mine, 0, keepdims=False)
-        return jnp.concatenate([kept, lax.ppermute(sent, "blk", far)], 0)
-
-    def unswap(rows):
-        kept, sent = rows[:local_rows], rows[local_rows:]
-        got = lax.ppermute(sent, "blk", far)
-        return jnp.where(mine == 0, jnp.stack([kept, got]), jnp.stack([got, kept]))
-
-    x = swap(layer_in)
-    grad = swap(out_grad)
-    rows_all = jnp.concatenate([x, lax.ppermute(x, "blk", near)], 0)
-    mats = lax.all_gather(matrices, ("ctx", "blk"), axis=0, tiled=True)
-    vec = lax.all_gather(vectors, ("ctx", "blk"), axis=0, tiled=True).astype(F32).reshape(-1, width)
+    per, entries = matrices.shape[0], vectors.shape[0]
+    slots = -(-per // 16) * 16
+    devices = ctx_size * blk_size
+    flat = lax.axis_index("ctx") * blk_size + lax.axis_index("blk")
+    mine = lax.axis_index("blk") // (blk_size // seq_count)
+    far = [(b, (b + blk_size // 2) % blk_size) for b in range(blk_size)]
+    in_rows = 3 * width
+    owners = max(-(-in_rows // (per * blk_size)), -(-2 * width // (entries * blk_size)))
+
+    block = jnp.concatenate(
+        [
+            jnp.pad(matrices, ((0, slots - per), (0, 0))),
+            jnp.pad(vectors.reshape(1, entries), ((0, 15), (0, width - entries))),
+        ],
+        0,
+    )
+    rows_all, first = exchange(ctx_size, blk_size, layer_in, block, owners)
+    w_input = first[:, :per].reshape(-1, width)[:in_rows]
+    vec_in = first[:, slots, :entries].reshape(-1)[: 2 * width].reshape(2, width).astype(F32)
+    vec_in = jnp.pad(vec_in, ((0, 6), (0, 0)))
+
+    every = lax.all_gather(block, ("ctx", "blk"), axis=0)
+    weights = every[:, :per].reshape(-1, width)[in_rows:]
+    vec = every[:, slots, :entries].reshape(-1, width).astype(F32)
     vec = jnp.pad(vec, ((0, 16 - vec.shape[0]), (0, 0)))
-    own = x.shape[0]
-    ln, qt, kn, kta, vta = prep(rows_all, own, mats[: 3 * width], vec)
+
+    kept = lax.dynamic_index_in_dim(out_grad, mine, 0, keepdims=False)
+    sent = lax.dynamic_index_in_dim(out_grad, 1 - mine, 0, keepdims=False)
+    grad = jnp.concatenate([kept, lax.ppermute(sent, "blk", far)], 0)
+
+    own = 2 * local_rows
+    ln, qt, kn, kta, vta = prep(rows_all, own, w_input, vec_in)
     att, lse = attend(qt, kn, kta, vta)
-    out, gmid, qa, doa, dot_t, gwo, gup, gdown, gvec = between(x, grad, att, lse, qt, mats[3 * width :], vec)
-    layer_out = unswap(out)
+    out, gmid, qa, doa, dot_t, gwo, gup, gdown, gvec = between(rows_all, grad, att, lse, qt, weights, vec)
+
+    got = lax.ppermute(out[local_rows:], "blk", far)
+    layer_out = jnp.where(mine == 0, jnp.stack([out[:local_rows], got]), jnp.stack([got, out[:local_rows]]))
+
+    late = jnp.concatenate([jnp.zeros((in_rows, width), F32), gwo, gup.T, gdown.T], 0).reshape(devices, per, width)
+    count = entries * devices // width
+    late_vec = jnp.concatenate([jnp.zeros((2, width), F32), gvec[2:count]], 0).reshape(devices, 1, entries)
+    late_vec = jnp.pad(late_vec, ((0, 0), (0, 7), (0, width - entries)))
+    late = jnp.pad(late, ((0, 0), (0, -per % 8), (0, 0)))
+    summed = lax.psum_scatter(jnp.concatenate([late, late_vec], 1), ("ctx", "blk"), scatter_dimension=0, tiled=False)
+
     dq, dk, dv = attend_back(qa, doa, qt, dot_t, kta, vta, kn)
-    gw, part = unproject(dq, dk, dv, ln, mats[: 3 * width])
-    other = lax.ppermute(part[:, own:], "blk", near)
-    grad_rows, gvec_in = finish(x, gmid, dq, part[:, :own], other, mats[:width], vec)
-    layer_grad = unswap(grad_rows)
-    grad_mats = jnp.concatenate([gw, gwo, gup.T, gdown.T], 0)
-    grad_vecs = jnp.concatenate([gvec_in[:2], gvec[2:9]], 0).reshape(-1)
-    matrices_grad = lax.psum_scatter(grad_mats, ("ctx", "blk"), scatter_dimension=0, tiled=True)
-    vectors_grad = lax.psum_scatter(grad_vecs, ("ctx", "blk"), scatter_dimension=0, tiled=True)
+    gw, part = unproject(dq, dk, dv, ln, w_input, (blk_size, owners, per))
+    layer_grad, gw_in, gvec_in = finish(ctx_size, blk_size, rows_all, gmid, dq, part, gw, w_input[:width], vec_in)
+    matrices_grad = jnp.where(flat < in_rows // per, gw_in[:per], summed[:per])
+    early = jnp.pad(gvec_in[:2].reshape(-1), (0, entries * devices - 2 * width))
+    vectors_grad = summed[per + -per % 8, :entries] + lax.dynamic_slice_in_dim(early, flat * entries, entries)
     return layer_out, layer_grad, matrices_grad, vectors_grad
 
 
@@ -548,7 +866,7 @@
     rows = P("ctx", "blk", None)
     flat = P(("ctx", "blk"))
     return jax.shard_map(
-        functools.partial(per_device, mesh.shape["blk"]),
+        functools.partial(per_device, mesh.shape["ctx"], mesh.shape["blk"]),
         mesh=mesh,
         in_specs=(rows, flat, flat, rows),
         out_specs=(rows, rows, flat, flat),

time: 356 us -> 278 us (0.78)
  blocking collectives: 90.3 us -> 0 us
  Pallas kernels: 163 us -> 215 us
  waiting for transfers between devices: 51.7 us -> 13.2 us
  other arithmetic: 9.73 us -> 13.3 us
    unnamed x2 -> x0, blocking collectives: 90.3 us -> none
    pallas_call x2 -> x3, Pallas kernels: 16 us -> 68.5 us  [the longest x1 32.9 us: finish(): pl.pallas_call(functools.partial(finish_kernel, ctx_size, blk_size), in_s...]
    unnamed x3 -> x2, waiting for transfers between devices: 38 us -> 0.03 us
    ppermute x6 -> x2, waiting for transfers between devices: 13.7 us -> 0.01 us  [the longest x1 0.01 us: per_device(): grad = jnp.concatenate([kept, lax.ppermute(sent, 'blk', far)], 0)]
    reduce_scatter x0 -> x1, waiting for transfers between devices: none -> 13.1 us  [per_device(): lax.psum_scatter(jnp.concatenate([late, late_vec], 1), ('ctx', 'blk'), sc...]
    ppermute x6 -> x2, starting transfers between devices: 8.14 us -> 4.89 us  [the longest x1 3.03 us: per_device(): grad = jnp.concatenate([kept, lax.ppermute(sent, 'blk', far)], 0)]
    concatenate x5 -> x4, other arithmetic: 6.86 us -> 8.13 us  [the longest x1 3.57 us: per_device(): jnp.concatenate([jnp.zeros((in_rows, width), F32), gwo, gup.T, gdown.T], 0)]
    slice x6 -> x7, local copies, waits for them, and re-layouts: 6.24 us -> 7.42 us  [the longest x1 2.38 us: per_device(): weights = every[:, :per].reshape(-1, width)[in_rows:]]
  transfers between devices with their start and end apart: 8 -> 4, of which waited for: 3 -> 1; matrix products, arithmetic and copies ran while one was open for 4% -> 3% of each run, Pallas kernels for 2% -> 69%
where the time goes in v2:
time: 278 us; the launch traced here: 277 us
  Pallas kernels  215 us (77%)
  local copies, waits for them, and re-layouts  16.7 us (6%)
  between operations  14.2 us (5%)
  other arithmetic  13.3 us (5%)
  waiting for transfers between devices  13.2 us (5%)
  starting transfers between devices  4.97 us (2%)
    pallas_call x1, Pallas kernels, attend_back(): pl.pallas_call(attend_back_kernel, grid=(HEADS,), in_specs=[per_head(own,...  80.7 us
    pallas_call x1, Pallas kernels, finish(): pl.pallas_call(functools.partial(finish_kernel, ctx_size, blk_size), in_s...  32.9 us
    pallas_call x1, Pallas kernels, attend(): pl.pallas_call(attend_kernel, grid=(HEADS,), in_specs=[per_head(head, own...  32.7 us
    pallas_call x1, Pallas kernels, exchange(): pl.pallas_call(functools.partial(exchange_kernel, ctx_size, blk_size), in...  27.8 us
    pallas_call x1, Pallas kernels, between(): pl.pallas_call(middle_kernel, grid=(own // block,), in_specs=[pl.BlockSpe...  22.3 us
    reduce_scatter x1, waiting for transfers between devices, per_device(): lax.psum_scatter(jnp.concatenate([late, late_vec], 1), ('ctx', 'blk'), sc...  13.1 us
    pallas_call x1, Pallas kernels, prep(): pl.pallas_call(functools.partial(prep_kernel, own_steps), grid=(steps,),...  10.6 us
    pallas_call x1, Pallas kernels, unproject(): pl.pallas_call(functools.partial(unproject_kernel, own_steps, places), gr...  7.85 us
  transfers between devices with their start and end apart: 4, of which 1 were waited for; matrix products, arithmetic and copies ran while one was open for 3% of the time, Pallas kernels for 69%

profile of v2, /device:TPU:0, one launch (start us, length us, event | category | flops | bytes accessed | tf_op | source)
XLA Modules:
  0.0 277.1 jit_solution(5999961080412732513)
XLA Ops:
  7.2 0.0 all-gather.3.cloned.1.call-start
  7.2 1.4 fusion.2.w_ref
  8.7 0.0 all-gather.3.cloned.1.call-update
  8.7 0.0 reduce-scatter.2.cloned.1.call-start
  8.8 1.3 dynamic-slice_bitcast_fusion.1
  10.0 3.0 %collective-permute-start = (bf16[1024,256]{1,0:T(8,128)(2,1)S(1)}, bf16[1024,256]{1,0:T(8,128)(2,1)S(1)}, u32[]{:S(2)}, u32[]{:S(2)}) collective-permute-start(bf16[1024,256]{1,0:T(8,128)(2,1)S(1)} %get-tuple-element.59), channel_id=1, source_target_pairs={{0,2},{1,3},{2,0},{3,1},{4,6},{5,7},{6,4},{7,5},{8,10},{9,11},{10,... | collective-permute-start | bytes 1572872 | tf_op jit(solution)/shard_map/ppermute | solution.py:839
  13.1 27.8 %exchange.1 = (bf16[4096,256]{1,0:T(8,128)(2,1)}, bf16[8,112,256]{2,1,0:T(8,128)(2,1)}) custom-call(bf16[2,1024,256]{2,1,0:T(8,128)(2,1)} %x_ref.1, bf16[112,256]{1,0:T(8,128)(2,1)} %fusion.2.w_ref), custom_call_target="tpu_custom_call" | custom-call | tf_op jit(solution)/shard_map/exchange/pallas_call | solution.py:163
  40.8 1.8 slice.45
  42.7 0.7 slice_reduce_fusion.1
  43.4 0.1 reshape_squeeze.4
  43.5 0.6 pad_convert_fusion.1.vec_ref
  44.1 10.6 %project.1 = (bf16[4096,256]{1,0:T(8,128)(2,1)}, bf16[4,64,2048]{2,1,0:T(8,128)(2,1)}, bf16[4,4096,128]{2,1,0:T(8,128)(2,1)}, bf16[4,80,4096]{2,1,0:T(8,128)(2,1)}, bf16[4,80,4096]{2,1,0:T(8,128)(2,1)}) custom-call(bf16[4096,256]{1,0:T(8,128)(2,1)} %get-tuple-element.30.x_ref.x_hbm, bf16[768,256]{1,0:T(8,128)(2,1)} %bitcast.28, ...), custom_call_target="tpu_custom_call" | custom-call | tf_op jit(solution)/shard_map/project/pallas_call | solution.py:225
  54.7 32.7 %attend.1 = (f32[4,64,2048]{2,1,0:T(8,128)}, f32[4,8,2048]{2,1,0:T(8,128)}) custom-call(bf16[4,64,2048]{2,1,0:T(8,128)(2,1)} %get-tuple-element.32.qt_ref, bf16[4,4096,128]{2,1,0:T(8,128)(2,1)} %get-tuple-element.33.kn_ref, bf16[4,80,4096]{2,1,0:T(8,128)(2,1)} %get-tuple-element.34.kta_ref, bf16[4,80,4096]{2,1,0:T(8,128)(2,1)} %get-tuple-element.35.vta_ref), custom_call_target="tpu_custom_call" | custom-call | tf_op jit(solution)/shard_map/attend/pallas_call | solution.py:315
  87.4 0.0 collective-permute-done
  87.4 1.0 pad_maximum_fusion.1.g_ref
  88.4 0.0 all-gather.3.cloned.1.call-done
  88.4 2.4 slice.59
  90.8 0.9 slice_reduce_fusion
  91.7 0.1 convert_element_type.19
  91.8 0.6 pad_convert_fusion.vec_ref
  92.4 22.3 %between.1 = (bf16[2048,256]{1,0:T(8,128)(2,1)}, f32[2048,256]{1,0:T(8,128)}, bf16[4,2048,128]{2,1,0:T(8,128)(2,1)}, bf16[4,2048,128]{2,1,0:T(8,128)(2,1)}, bf16...) custom-call(bf16[4096,256]{1,0:T(8,128)(2,1)} %get-tuple-element.30., ...), custom_call_target="tpu_custom_call" | custom-call | tf_op jit(solution)/shard_map/between/pallas_call | solution.py:422
  114.7 1.1 copy.12
  115.8 3.6 %pad_maximum_fusion = f32[3072,256]{0,1:T(8,128)} fusion(f32[1024,256]{0,1:T(8,128)} %bitcast.32, f32[1024,256]{0,1:T(8,128)} %bitcast.31, f32[256,256]{0,1:T(8,128)S(1)} %copy.12, f32[3072]{0:T(1024)S(1)} %pad.34.clone), kind=kLoop, calls=%fused_computation.2 | loop fusion | flops 2359296 | bytes 5517312 | tf_op jit(solution)/shard_map/concatenate | solution.py:849
  119.4 0.0 copy-start.1
  119.4 2.4 copy.13
  121.8 0.0 copy-done.1
  121.8 0.1 reshape.34
  121.9 2.1 select_maximum_fusion
  124.0 0.0 copy-start
  124.0 0.0 reduce-scatter.2.cloned.1.call-update
  124.0 1.2 copy-done
  125.2 0.1 slice_bitcast_fusion
  125.3 1.9 collective-permute-start.1
  127.2 1.6 slice.61.w_ref
  128.7 80.7 %attend_back.1 = (bf16[4,2048,128]{2,1,0:T(8,128)(2,1)}, bf16[4,64,4096]{2,1,0:T(8,128)(2,1)}, bf16[4,64,4096]{2,1,0:T(8,128)(2,1)}) custom-call(bf16[4,2048,128]{2,1,0:T(8,128)(2,1)} %get-tuple-element.40.qa_ref, bf16[4,2048,128]{2,1,0:T(8,128)(2,1)} %get-tuple-element.41.doa_ref, bf16[4,64,2048]{2,1,0:T(8,128)(2,1)} %get-tuple-element.32.qt_ref, ...), custom_call_target="tpu_custom_call" | custom-call | tf_op jit(solution)/shard_map/attend_back/pallas_call | solution.py:502
  209.4 7.8 %unproject.1 = (bf16[4,2,96,256]{3,2,1,0:T(8,128)(2,1)}, bf16[256,4096]{1,0:T(8,128)(2,1)}) custom-call(bf16[4,2048,128]{2,1,0:T(8,128)(2,1)} %get-tuple-element.43.dq_ref.dq_hbm, bf16[4,64,4096]{2,1,0:T(8,128)(2,1)} %get-tuple-element.44.dk_ref, bf16[4,64,4096]{2,1,0:T(8,128)(2,1)} %get-tuple-element.45.dv_ref, bf16[4096,256]{1,0:T(8,128)(2,1)} %get-tuple-element.46.ln_ref, ...), custom_call_target="tpu_custom_call" | custom-call | tf_op jit(solution)/shard_map/unproject/pallas_call | solution.py:568
  217.2 32.9 %finish.1 = (bf16[2,1024,256]{2,1,0:T(8,128)(2,1)}, f32[96,256]{1,0:T(8,128)}, f32[8,256]{1,0:T(8,128)}) custom-call(bf16[4096,256]{1,0:T(8,128)(2,1)} %get-tuple-element.30.x_ref.x_hbm, f32[2048,256]{1,0:T(8,128)} %get-tuple-element.39.gmid_hbm, bf16[4,2048,128]{2,1,0:T(8,128)(2,1)} %get-tuple-element.43.dq_ref.dq_hbm, ...), custom_call_target="tpu_custom_call" | custom-call | tf_op jit(solution)/shard_map/finish/pallas_call | solution.py:785
  250.1 0.7 slice_bitcast_fusion.2
  250.8 0.0 collective-permute-done.1
  250.8 1.1 maximum_select_fusion
  252.0 13.1 %reduce-scatter.2.cloned.1.call-done = f32[1,104,256]{2,1,0:T(8,128)} async-done(((f32[32,104,256]{2,1,0:T(8,128)}), f32[1,104,256]{2,1,0:T(8,128)}) %reduce-scatter.2.cloned.1.call-update) | async-done | bytes 106512 | tf_op jit(solution)/shard_map/reduce_scatter | solution.py:854
  265.1 1.3 fusion.3
  266.4 1.6 fusion.1
  267.9 2.3 copy.17
  (7 shorter events, 0.0 us)
Async XLA Ops:
  7.2 81.2 %all-gather.3.cloned.1.call-start = ((), (), s32[]{:S(2)}) async-start(), calls=%async_computation.2 | async-start | bytes 1892352 | tf_op jit(solution)/shard_map/all_gather | solution.py:832
  8.7 256.4 %reduce-scatter.2.cloned.1.call-start = ((), (), s32[]{:S(2)}) async-start(), calls=%async_computation.1 | async-start | bytes 3514368 | tf_op jit(solution)/shard_map/reduce_scatter | solution.py:854
  10.0 77.3 %collective-permute-start = (bf16[1024,256]{1,0:T(8,128)(2,1)S(1)}, bf16[1024,256]{1,0:T(8,128)(2,1)S(1)}, u32[]{:S(2)}, u32[]{:S(2)}) collective-permute-start(bf16[1024,256]{1,0:T(8,128)(2,1)S(1)} %get-tuple-element.59), channel_id=1, source_target_pairs={{0,2},{1,3},{2,0},{3,1},{4,6},{5,7},{6,4},{7,5},{8,10},{9,11},{10,... | collective-permute-start | bytes 1572872 | tf_op jit(solution)/shard_map/ppermute | solution.py:839
  119.4 2.4 copy-start.1
  124.0 1.2 copy-start
  125.3 125.5 %collective-permute-start.1 = (bf16[1024,256]{1,0:T(8,128)(2,1)S(1)}, bf16[1024,256]{1,0:T(8,128)(2,1)S(1)}, u32[]{:S(2)}, u32[]{:S(2)}) collective-permute-start(bf16[1024,256]{1,0:T(8,128)(2,1)S(1)} %get-tuple-element.57), channel_id=1, source_target_pairs={{0,2},{1,3},{2,0},{3,1},{4,6},{5,7},{6,4},{7,5},{8,10},{9,11},{10,... | collective-permute-start | bytes 1572872 | tf_op jit(solution)/shard_map/ppermute | solution.py:846
Sparse Core Ops, SparseCore 0:
  11.5 58.5 all-gather.2
  124.2 140.8 reduce-scatter.1

commit v3 on v2

--- a/solution.py
+++ b/solution.py
@@ -349,8 +349,8 @@
 
 
 def middle_kernel(
-    x_ref, g_ref, att_ref, lse_ref, qt_ref, w_ref, vec_ref,
-    out_ref, gmid_ref, qa_ref, doa_ref, dot_ref, gwo_ref, gup_ref, gdown_ref, gvec_ref,
+    per, x_ref, g_ref, att_ref, lse_ref, qt_ref, w_ref, vec_ref,
+    out_ref, gmid_ref, qa_ref, doa_ref, dot_ref, late_ref, gvec_ref, gwo_ref, gup_ref, gdown_ref,
 ):
     width = x_ref.shape[1]
     head = width // HEADS
@@ -410,8 +410,23 @@
         wide = jnp.concatenate([qt_ref[h].astype(F32), split_rows(-level, AUG - head), spare], 0)
         qa_ref[h] = wide.T.astype(BF)
 
-
-def between(x, grad, att, lse, qt, weights, vec):
+    @pl.when(pl.program_id(0) == pl.num_programs(0) - 1)
+    def _():
+        grads = jnp.concatenate([gwo_ref[...], gup_ref[...].T, gdown_ref[...].T], 0)
+        into_slots(late_ref, grads, per)
+
+
+def into_slots(slots_ref, grads, per):
+    blk_size, owners, padded, width = slots_ref.shape
+    filler = jnp.zeros((padded - per, width), F32)
+    for slot in range(blk_size * owners):
+        piece = grads[slot * per : (slot + 1) * per, :]
+        if padded > per:
+            piece = jnp.concatenate([piece, filler], 0)
+        slots_ref[slot % blk_size, slot // blk_size] = piece.astype(BF)
+
+
+def between(x, grad, att, lse, qt, weights, vec, blk_size, per):
     own, width = grad.shape
     head = width // HEADS
     hidden_width = (weights.shape[0] - width) // 2
@@ -419,8 +434,9 @@
     rows = lambda i: (i, 0)
     lanes = lambda i: (0, 0, i)
     tall = lambda i: (0, i, 0)
+    slots = (blk_size, weights.shape[0] // (blk_size * per), -(-per // 16) * 16, width)
     return pl.pallas_call(
-        middle_kernel,
+        functools.partial(middle_kernel, per),
         grid=(own // block,),
         in_specs=[
             pl.BlockSpec((block, width), rows),
@@ -437,9 +453,7 @@
             pl.BlockSpec((HEADS, block, 128), tall),
             pl.BlockSpec((HEADS, block, 128), tall),
             pl.BlockSpec((HEADS, head, block), lanes),
-            whole(width, width),
-            whole(width, hidden_width),
-            whole(width, hidden_width),
+            whole(*slots),
             whole(16, width),
         ],
         out_shape=[
@@ -448,362 +462,359 @@
             jax.ShapeDtypeStruct((HEADS, own, 128), BF),
             jax.ShapeDtypeStruct((HEADS, own, 128), BF),
             jax.ShapeDtypeStruct((HEADS, head, own), BF),
-            jax.ShapeDtypeStruct((width, width), F32),
-            jax.ShapeDtypeStruct((width, hidden_width), F32),
-            jax.ShapeDtypeStruct((width, hidden_width), F32),
+            jax.ShapeDtypeStruct(slots, BF),
             jax.ShapeDtypeStruct((16, width), F32),
+        ],
+        scratch_shapes=[
+            pltpu.VMEM((width, width), F32), pltpu.VMEM((width, hidden_width), F32), pltpu.VMEM((width, hidden_width), F32),
         ],
         compiler_params=params(),
         name="between",
     )(x, grad, att, lse, qt, weights, vec)
 
 
-def attend_back_kernel(qa_ref, doa_ref, qt_ref, dot_ref, kta_ref, vta_ref, kn_ref, dq_ref, dk_ref, dv_ref, dk_sum, dv_sum):
-    head, own = qt_ref.shape[1:]
-    total = kn_ref.shape[1]
-    tq = min(1024, own)
-    tk = min(512, total)
-    count = total // tk
+def back_kernel(
+    ctx_size, blk_size, per,
+    qa_hbm, doa_hbm, qt_hbm, dot_hbm, kta_hbm, vta_hbm, kn_hbm, ln_hbm, x_hbm, gmid_hbm, out_hbm, late_hbm,
+    gvec_in, w_ref, vec_ref,
+    grad_ref, out_ref, gw_ref, gvec_ref,
+    qa, doa, qt, dot_t, kta, vta, kn, ln, x, gmid, made,
+    dq_sum, dk_sum, dv_sum, gq, gk, gv, part, part_out, part_in, wqt,
+    late_own, late_one, late_pass, late_two, late_sum, late_three,
+    early, early_one, early_pass, early_two, early_sum, early_three,
+    vec_own, vec_one, vec_pair, vec_two, vec_sum, vec_three,
+    head_sem, load_sem, out_sent, out_got, keep_sem, grad_sent, grad_got, part_sent, part_got,
+    l1_sent, l1_got, l2_sent, l2_got, l3_sent, l3_got,
+    e1_sent, e1_got, e2_sent, e2_got, e3_sent, e3_got,
+    v1_sent, v1_got, v2_sent, v2_got, v3_sent, v3_got,
+):
+    ctx, blk, near, far, mine = partners(blk_size)
+    core = lax.rem(blk, 2)
+    own, width = x.shape
+    length = own // 2
+    head = width // HEADS
+    owners = early.shape[1]
+    groups = ctx_size // owners
+    late_count = late_own.shape[1]
+    group, place = lax.div(ctx, owners), lax.rem(ctx, owners)
+    others = [lax.rem(ctx + step, ctx_size) for step in range(1, ctx_size)]
+    peers = [lax.rem(place + step, owners) for step in range(1, owners)]
+
+    def remote(source, target, sent, got, device):
+        return pltpu.make_async_remote_copy(
+            src_ref=source, dst_ref=target, send_sem=sent, recv_sem=got, device_id=device, device_id_type=MESH
+        )
+
+    to_near, to_far = (ctx, near), (ctx, far)
+    local = pltpu.make_async_copy
+
+    def head_loads(h):
+        pairs = ((qa_hbm, qa), (doa_hbm, doa), (qt_hbm, qt), (dot_hbm, dot_t), (kta_hbm, kta), (vta_hbm, vta), (kn_hbm, kn))
+        return [local(a.at[h], b.at[h], head_sem.at[i, h]) for i, (a, b) in enumerate(pairs)]
+
+    loads = [
+        local(ln_hbm, ln, load_sem.at[0]),
+        local(x_hbm.at[pl.ds(0, own)], x, load_sem.at[1]),
+        local(gmid_hbm, gmid, load_sem.at[2]),
+    ]
+    late_loads = [local(late_hbm.at[2 * y + core], late_own.at[y], load_sem.at[3 + y]) for y in range(2)]
+    out_keep = local(out_hbm.at[pl.ds(0, length)], out_ref.at[mine], keep_sem.at[0])
+    out_send = remote(out_hbm.at[pl.ds(length, length)], out_ref.at[mine], out_sent, out_got, to_far)
+
+    late_first = [
+        remote(late_hbm.at[2 * y + 1 - core], late_one.at[y], l1_sent.at[y], l1_got.at[y], to_near) for y in range(2)
+    ]
+    late_second = remote(late_pass.at[1 - mine], late_two, l2_sent, l2_got, to_far)
+
+    def late_third(step):
+        other = others[step]
+        return remote(
+            late_sum.at[jnp.maximum(other - owners, 0)], late_three.at[ctx], l3_sent.at[step], l3_got.at[ctx], (other, blk)
+        )
+
+    def late_third_from(other):
+        return remote(late_sum.at[0], late_three.at[other], l3_sent.at[0], l3_got.at[other], to_near)
+
+    def grad_send(half, c, size):
+        return remote(
+            made.at[pl.ds(half * length + c * size, size)], grad_ref.at[mine, pl.ds(c * size, size)],
+            grad_sent.at[c], grad_got.at[c], to_far,
+        )
+
+    def grad_keep(c, size):
+        return local(made.at[pl.ds(c * size, size)], grad_ref.at[mine, pl.ds(c * size, size)], keep_sem.at[1 + c])
+
+    def part_send(half):
+        return remote(part_out.at[half], part_in.at[half], part_sent.at[half], part_got.at[half], to_near)
+
+    early_first = [
+        remote(early.at[2 * y + 1 - core], early_one.at[y], e1_sent.at[y], e1_got.at[y], to_near) for y in range(2)
+    ]
+    vec_first = remote(vec_own, vec_one, v1_sent, v1_got, to_near)
+    here = mine * owners + place
+    plane = [(1 - mine, place, to_far)]
+    for peer in peers:
+        plane.append((mine, peer, (group * owners + peer, blk)))
+        plane.append((1 - mine, peer, (group * owners + peer, far)))
+    early_second = [
+        remote(early_pass.at[y, r], early_two.at[here], e2_sent.at[i], e2_got.at[here], device)
+        for i, (y, r, device) in enumerate(plane)
+    ]
+    vec_second = [
+        remote(vec_pair, vec_two.at[here], v2_sent.at[i], v2_got.at[here], device) for i, (y, r, device) in enumerate(plane)
+    ]
+    plane_slots = [y * owners + r for y, r, _ in plane]
+    early_third = remote(early_sum, early_three.at[jnp.maximum(group - 1, 0)], e3_sent, e3_got.at[jnp.maximum(group - 1, 0)], (place, blk))
+    other_groups = [lax.rem(group + step, groups) for step in range(1, groups)]
+    vec_third = [
+        remote(vec_sum, vec_three.at[group], v3_sent.at[i], v3_got.at[group], (other * owners + place, blk))
+        for i, other in enumerate(other_groups)
+    ]
+
+    greet([to_near, to_far] + [(other, blk) for other in others] + [(group * owners + peer, far) for peer in peers])
+    for h in range(HEADS):
+        for load in head_loads(h):
+            load.start()
+    for copy in late_first + late_loads + [out_send, out_keep] + loads:
+        copy.start()
+    dq_sum[...] = jnp.zeros_like(dq_sum)
     dk_sum[...] = jnp.zeros_like(dk_sum)
     dv_sum[...] = jnp.zeros_like(dv_sum)
-
-    @pl.loop(0, own // tq)
-    def _(i):
-        where = pl.ds(pl.multiple_of(i * tq, tq), tq)
-        queries, grads = qa_ref[0, where, :AUG], doa_ref[0, where, :AUG]
-        queries_t, grads_t = qt_ref[0, :, where], dot_ref[0, :, where]
-
-        def pair(j):
-            part = slice(j * tk, (j + 1) * tk)
-            return dot(queries, kta_ref[0, :, part]), dot(grads, vta_ref[0, :, part])
-
-        grad_query = jnp.zeros((tq, 128), F32)
-        level, change = pair(0)
-        for j in range(count):
-            part = slice(j * tk, (j + 1) * tk)
+    gq[...] = jnp.zeros_like(gq)
+    gk[...] = jnp.zeros_like(gk)
+    gv[...] = jnp.zeros_like(gv)
+    vec_own[...] = gvec_in[...]
+
+    tk = min(256, length)
+    wk, wv = w_ref[width : 2 * width, :], w_ref[2 * width : 3 * width, :]
+    gain = vec_ref[0:1, :]
+    size = min(512, length)
+    chunks = length // size
+
+    def terms(half):
+        for core_rows in range(2):
+            low = core_rows * own + half * length
+            rows = slice(low, low + length)
+            dk = (dk_sum[:, :, rows] * LN2).astype(BF).reshape(width, length)
+            dv = dv_sum[:, :, rows].astype(BF).reshape(width, length)
+            gk[...] += dot(dk, ln[rows, :])
+            gv[...] += dot(dv, ln[rows, :])
+            both = dot(wk, dk) + dot(wv, dv)
+            if core_rows == 0:
+                part[half] = both
+            else:
+                part_out[half] = both.astype(BF)
+                part_send(half).start()
+        rows = slice(half * length, (half + 1) * length)
+        gq[...] += dot_tn(ln[rows, :], query_grads(rows))
+
+    def query_grads(rows):
+        return jnp.concatenate([(dq_sum[h, rows, :] * (1.0 / math.sqrt(head))).astype(BF) for h in range(HEADS)], 1)
+
+    def rows_back(half):
+        for c in range(chunks):
+            rows = slice(half * length + c * size, half * length + (c + 1) * size)
+            lanes = slice(c * size, (c + 1) * size)
+            grad_ln = dot(query_grads(rows), wqt[...]) + (part[half, :, lanes] + part_in[half, :, lanes].astype(F32)).T
+            normed, inverse = normalize(x[rows, :].astype(F32))
+            vec_own[0:1, :] += jnp.sum(grad_ln * normed, 0, keepdims=True)
+            vec_own[1:2, :] += jnp.sum(grad_ln, 0, keepdims=True)
+            made[rows, :] = (gmid[rows, :] + normalize_back(grad_ln * gain, normed, inverse)).astype(BF)
+            (grad_send(half, c, size) if half else grad_keep(c, size)).start()
+
+    @pl.loop(0, 4 * HEADS)
+    def _(t):
+        block, h = lax.div(t, HEADS), lax.rem(t, HEADS)
+
+        @pl.when(block == 0)
+        def _():
+            for load in head_loads(h):
+                load.wait()
+
+        @pl.when(t == 2)
+        def _():
+            for y in range(2):
+                late_loads[y].wait()
+                late_first[y].wait_recv()
+                late_pass[y] = (late_own[y].astype(F32) + late_one[y].astype(F32)).astype(BF)
+            late_second.start()
+
+        @pl.when(t == 5)
+        def _():
+            late_second.wait_recv()
+            late_sum[...] = (late_pass[mine].astype(F32) + late_two[...].astype(F32)).astype(BF)
+            for step, other in enumerate(others):
+                @pl.when(other >= owners)
+                def _():
+                    late_third(step).start()
+
+        @pl.when(t == 3 * HEADS)
+        def _():
+            turned = w_ref[:width, :].astype(F32).T
+            for head_index in range(HEADS):
+                low = head_index * 128
+                wqt[low : low + head, :] = turned[head_index * head : (head_index + 1) * head, :].astype(BF)
+                wqt[low + head : low + 128, :] = jnp.zeros((128 - head, width), BF)
+            for load in loads:
+                load.wait()
+            terms(1)
+
+        @pl.when(t == 3 * HEADS + 1)
+        def _():
+            part_send(1).wait_recv()
+            rows_back(1)
+
+        first_half = jnp.logical_or(block == 0, block == 3)
+        where = pl.ds(pl.multiple_of(jnp.where(first_half, 0, length), length), length)
+        base = jnp.where(block < 2, length, 0)
+        queries, grads = qa[h, where, :AUG], doa[h, where, :AUG]
+        queries_t, grads_t = qt[h, :, where], dot_t[h, :, where]
+        parts = []
+        for offset in (0, own):
+            for low in range(0, length, tk):
+                parts.append(pl.ds(pl.multiple_of(base + (offset + low), tk), tk))
+
+        def pair(part):
+            return dot(queries, kta[h, :, part]), dot(grads, vta[h, :, part])
+
+        grad_query = jnp.zeros((length, 128), F32)
+        level, change = pair(parts[0])
+        for j, part_now in enumerate(parts):
             probs = jnp.exp2(level)
             probs_low = probs.astype(BF)
             grad_scores = (probs * change).astype(BF)
-            if j + 1 < count:
-                level, change = pair(j + 1)
-            dv_sum[:, part] += dot(grads_t, probs_low)
-            dk_sum[:, part] += dot(queries_t, grad_scores)
-            grad_query = grad_query + dot(grad_scores, kn_ref[0, part, :])
-        dq_ref[0, where, :] = (grad_query * (1.0 / math.sqrt(head))).astype(BF)
-
-    dk_ref[0] = (dk_sum[...] * LN2).astype(BF)
-    dv_ref[0] = dv_sum[...].astype(BF)
-
-
-def attend_back(qa, doa, qt, dot_t, kta, vta, kn):
-    _, head, own = qt.shape
-    total = kn.shape[1]
-    per_head = lambda *shape: pl.BlockSpec((1, *shape), lambda h: (h, 0, 0))
-    return pl.pallas_call(
-        attend_back_kernel,
-        grid=(HEADS,),
-        in_specs=[
-            per_head(own, 128), per_head(own, 128), per_head(head, own), per_head(head, own),
-            per_head(AUG, total), per_head(AUG, total), per_head(total, 128),
-        ],
-        out_specs=[per_head(own, 128), per_head(head, total), per_head(head, total)],
-        out_shape=[
-            jax.ShapeDtypeStruct((HEADS, own, 128), BF),
-            jax.ShapeDtypeStruct((HEADS, head, total), BF),
-            jax.ShapeDtypeStruct((HEADS, head, total), BF),
-        ],
-        scratch_shapes=[pltpu.VMEM((head, total), F32), pltpu.VMEM((head, total), F32)],
-        compiler_params=params(),
-        name="attend_back",
-    )(qa, doa, qt, dot_t, kta, vta, kn)
-
-
-def unproject_kernel(own_steps, places, dq_ref, dk_ref, dv_ref, ln_ref, w_ref, gw_ref, part_ref, gq, gk, gv):
-    width = ln_ref.shape[1]
-    head = width // HEADS
-    rows = ln_ref.shape[0]
-    step = pl.program_id(0)
-
-    @pl.when(step == 0)
-    def _():
-        gq[...] = jnp.zeros_like(gq)
-        gk[...] = jnp.zeros_like(gk)
-        gv[...] = jnp.zeros_like(gv)
-
-    ln = ln_ref[...]
-    dk = dk_ref[...].reshape(width, rows)
-    dv = dv_ref[...].reshape(width, rows)
-    gk[...] += dot(dk, ln)
-    gv[...] += dot(dv, ln)
-    part_ref[...] = (dot(w_ref[width : 2 * width, :], dk) + dot(w_ref[2 * width : 3 * width, :], dv)).astype(BF)
-
-    @pl.when(step < own_steps)
-    def _():
-        dq = jnp.concatenate([dq_ref[h] for h in range(HEADS)], 1)
-        gq[...] += dot_tn(ln, dq)
-
-    @pl.when(step == pl.num_programs(0) - 1)
-    def _():
-        narrow = jnp.concatenate([gq[:, h * 128 : h * 128 + head] for h in range(HEADS)], 1)
-        grads = jnp.concatenate([narrow, gk[...].T, gv[...].T], 0)
-        blk_size, owners, per = places
-        filler = jnp.zeros((gw_ref.shape[2] - per, width), F32)
-        for slot in range(blk_size * owners):
-            o, k = slot // blk_size, slot % blk_size
-            piece = grads[slot * per : (slot + 1) * per, :]
-            if filler.shape[0]:
-                piece = jnp.concatenate([piece, filler], 0)
-            gw_ref[k, o] = piece.astype(BF)
-
-
-def unproject(dq, dk, dv, ln, w_input, places):
-    total, width = ln.shape
-    _, own, _ = dq.shape
-    head = width // HEADS
-    block = min(1024, own)
-    own_steps = own // block
-    last = own_steps - 1
-    blk_size, owners, per = places
-    slots = (blk_size, owners, -(-per // 16) * 16, width)
-    return pl.pallas_call(
-        functools.partial(unproject_kernel, own_steps, places),
-        grid=(total // block,),
-        in_specs=[
-            pl.BlockSpec((HEADS, block, 128), lambda i: (0, jnp.minimum(i, last), 0)),
-            pl.BlockSpec((HEADS, head, block), lambda i: (0, 0, i)),
-            pl.BlockSpec((HEADS, head, block), lambda i: (0, 0, i)),
-            pl.BlockSpec((block, width), lambda i: (i, 0)),
-            whole(3 * width, width),
-        ],
-        out_specs=[whole(*slots), pl.BlockSpec((width, block), lambda i: (0, i))],
-        out_shape=[
-            jax.ShapeDtypeStruct(slots, BF),
-            jax.ShapeDtypeStruct((width, total), BF),
-        ],
-        scratch_shapes=[
-            pltpu.VMEM((width, HEADS * 128), F32), pltpu.VMEM((width, width), F32), pltpu.VMEM((width, width), F32),
-        ],
-        compiler_params=params(),
-        name="unproject",
-    )(dq, dk, dv, ln, w_input)
-
-
-def finish_kernel(
-    ctx_size, blk_size, x_hbm, gmid_hbm, dq_hbm, part_hbm, gw_hbm, w_ref, vec_ref,
-    grad_ref, gw_ref, gvec_ref,
-    x, gmid, dq, part, other, gw_own, gw_first, gw_pass, gw_second, gw_sum, gw_third, gw_fourth,
-    made, vec_own, vec_near, vec_pair, vec_far, vec_four, vec_group, vec_all, vec_every, wqt,
-    load_sem, part_sent, part_got, first_sent, first_got, second_sent, second_got, third_sent, third_got,
-    fourth_sent, fourth_got, out_sent, out_got, keep_sem, vn_sent, vn_got, vf_sent, vf_got, vg_sent, vg_got,
-    va_sent, va_got,
-):
-    ctx, blk, near, far, mine = partners(blk_size)
-    width = x.shape[1]
-    head = width // HEADS
-    own = x.shape[0]
-    length = own // 2
-    owners = gw_hbm.shape[1]
-    groups = ctx_size // owners
-    core = lax.rem(blk, 2)
-    group, place = lax.div(ctx, owners), lax.rem(ctx, owners)
-    peers = [lax.rem(place + step, owners) for step in range(1, owners)]
-    peer_devices = [(group * owners + peer, blk) for peer in peers]
-    others = [lax.rem(group + step, groups) for step in range(1, groups)]
-    other_devices = [(other_group * owners + place, blk) for other_group in others]
-    greet([(ctx, near), (ctx, far)] + peer_devices + other_devices)
-
-    first = [send(gw_hbm.at[2 * y + 1 - core], gw_first.at[y], first_sent.at[y], first_got.at[y], (ctx, near)) for y in range(2)]
-    halves = []
-    for half in (1, 0):
-        there = pl.ds(half * length, length)
-        halves.append(
-            send(part_hbm.at[:, pl.ds(own + half * length, length)], other.at[:, there], part_sent.at[half], part_got.at[half], (ctx, near))
-        )
-    loads = [
-        pltpu.make_async_copy(gw_hbm.at[2 * y + core], gw_own.at[y], load_sem.at[y]) for y in range(2)
-    ]
-    for half in (1, 0):
-        rows = pl.ds(half * length, length)
-        base = 2 + 4 * half
-        loads += [
-            pltpu.make_async_copy(x_hbm.at[rows], x.at[rows], load_sem.at[base]),
-            pltpu.make_async_copy(gmid_hbm.at[rows], gmid.at[rows], load_sem.at[base + 1]),
-            pltpu.make_async_copy(dq_hbm.at[:, rows], dq.at[:, rows], load_sem.at[base + 2]),
-            pltpu.make_async_copy(part_hbm.at[:, rows], part.at[:, rows], load_sem.at[base + 3]),
-        ]
-    for load in loads:
-        load.start()
-
-    turned = w_ref[...].astype(F32).T
-    for h in range(HEADS):
-        wqt[h * 128 : h * 128 + head, :] = turned[h * head : (h + 1) * head, :].astype(BF)
-        wqt[h * 128 + head : (h + 1) * 128, :] = jnp.zeros((128 - head, width), BF)
-
-    gain = vec_ref[0:1, :]
-    size = min(512, length)
-    state = [jnp.zeros((1, width), F32), jnp.zeros((1, width), F32)]
-
-    def rows_back(low):
-        rows = slice(low, low + size)
-        from_q = dot(jnp.concatenate([dq[h, rows, :] for h in range(HEADS)], 1), wqt[...])
-        grad_ln = from_q + (part[:, rows].astype(F32) + other[:, rows].astype(F32)).T
-        normed, inverse = normalize(x[rows, :].astype(F32))
-        state[0] = state[0] + jnp.sum(grad_ln * normed, 0, keepdims=True)
-        state[1] = state[1] + jnp.sum(grad_ln, 0, keepdims=True)
-        made[rows, :] = (gmid[rows, :] + normalize_back(grad_ln * gain, normed, inverse)).astype(BF)
-
-    sums = (2, owners) + gw_hbm.shape[2:]
-
+            if j + 1 < len(parts):
+                level, change = pair(parts[j + 1])
+            dv_sum[h, :, part_now] += dot(grads_t, probs_low)
+            dk_sum[h, :, part_now] += dot(queries_t, grad_scores)
+            grad_query = grad_query + dot(grad_scores, kn[h, part_now, :])
+        dq_sum[h, where, :] += grad_query
+
+    terms(0)
+    grads = jnp.concatenate([jnp.concatenate([gq[:, h * 128 : h * 128 + head] for h in range(HEADS)], 1), gk[...].T, gv[...].T], 0)
+    into_slots(early, grads, per)
+    for copy in early_first:
+        copy.start()
+    part_send(0).wait_recv()
+    rows_back(0)
+    vec_first.start()
     for y in range(2):
-        loads[y].wait()
-        first[y].wait_recv()
-    for y in range(2):
-        gw_pass[y] = (gw_own[y].astype(F32) + gw_first[y].astype(F32)).astype(BF)
-    second = send(gw_pass.at[1 - mine], gw_second, second_sent, second_got, (ctx, far))
-
-    for load in loads[2:6]:
-        load.wait()
-    halves[0].wait_recv()
-    outs = []
-    chunk = 0
-    for low in range(length, own, size):
-        rows_back(low)
-        outs.append(
-            send(
-                made.at[pl.ds(low, size)], grad_ref.at[mine, pl.ds(low - length, size)],
-                out_sent.at[chunk], out_got.at[chunk], (ctx, far),
-            )
-        )
-        chunk += 1
-
-    second.wait_recv()
-    gw_sum[...] = (gw_pass[mine].astype(F32) + gw_second[...].astype(F32)).astype(BF)
-    third = [
-        send(gw_sum.at[peer], gw_third.at[place], third_sent.at[step], third_got.at[place], peer_devices[step])
-        for step, peer in enumerate(peers)
-    ]
-
-    for load in loads[6:]:
-        load.wait()
-    halves[1].wait_recv()
-    keeps = []
-    for low in range(0, length, size):
-        rows_back(low)
-        keeps.append(
-            pltpu.make_async_copy(made.at[pl.ds(low, size)], grad_ref.at[mine, pl.ds(low, size)], keep_sem.at[low // size])
-        )
-        keeps[-1].start()
-
-    row = lax.broadcasted_iota(jnp.int32, (8, width), 0)
-    vec_own[...] = jnp.where(row == 0, state[0], jnp.where(row == 1, state[1], 0.0))
-    to_near = send(vec_own, vec_near, vn_sent, vn_got, (ctx, near))
-
-    def from_peer(slot, holder, got, which):
-        return pltpu.make_async_remote_copy(
-            src_ref=holder.at[slot], dst_ref=holder.at[slot], send_sem=got.at[slot], recv_sem=got.at[slot],
-            device_id=(ctx, near), device_id_type=MESH,
-        )
-
-    total = gw_sum[place].astype(F32)
-    for slot in range(owners):
-        @pl.when(place != slot)
-        def _():
-            from_peer(slot, gw_third, third_got, None).wait_recv()
-
-        total = total + jnp.where(place != slot, gw_third[slot].astype(F32), 0.0)
-    gw_ref[...] = total
-    gw_own[0, 0] = total.astype(BF)
+        early_first[y].wait_recv()
+        early_pass[y] = (early[2 * y + core].astype(F32) + early_one[y].astype(F32)).astype(BF)
+    for copy in early_second:
+        copy.start()
+    vec_first.wait_recv()
+    vec_pair[...] = vec_own[...] + vec_one[...]
+    for copy in vec_second:
+        copy.start()
+
+    @pl.when(ctx >= owners)
+    def _():
+        total = late_sum[jnp.maximum(ctx - owners, 0)].astype(F32)
+        for other in others:
+            late_third_from(other).wait_recv()
+            total = total + late_three[other].astype(F32)
+        gw_ref[...] = total
+
+    def from_plane(slot, holder, got):
+        return remote(holder.at[slot], holder.at[slot], got.at[slot], got.at[slot], to_near)
+
+    total = early_pass[mine, place].astype(F32)
+    for slot in plane_slots:
+        from_plane(slot, early_two, e2_got).wait_recv()
+        total = total + early_two[slot].astype(F32)
+    early_sum[...] = total.astype(BF)
     if groups > 1:
         @pl.when(group > 0)
         def _():
-            send(gw_own.at[0, 0], gw_fourth.at[group - 1], fourth_sent, fourth_got.at[group - 1], (place, blk))
-
-    to_near.wait_recv()
-    vec_pair[...] = vec_own[...] + vec_near[...]
-    to_far = send(vec_pair, vec_far, vf_sent, vf_got, (ctx, far))
-    to_far.wait_recv()
-    vec_four[...] = vec_pair[...] + vec_far[...]
-    to_peers = [
-        send(vec_four, vec_group.at[place], vg_sent.at[step], vg_got.at[place], device)
-        for step, device in enumerate(peer_devices)
-    ]
-    vec_total = vec_four[...]
-    for slot in range(owners):
-        @pl.when(place != slot)
+            early_third.start()
+
+    vec_total = vec_pair[...]
+    for slot in plane_slots:
+        from_plane(slot, vec_two, v2_got).wait_recv()
+        vec_total = vec_total + vec_two[slot]
+    vec_sum[...] = vec_total
+    for copy in vec_third:
+        copy.start()
+
+    @pl.when(group == 0)
+    def _():
+        whole_sum = total
+        for slot in range(groups - 1):
+            from_plane(slot, early_three, e3_got).wait_recv()
+            whole_sum = whole_sum + early_three[slot].astype(F32)
+        gw_ref[...] = whole_sum
+
+    for other in other_groups:
+        from_plane(other, vec_three, v3_got).wait_recv()
+        vec_total = vec_total + vec_three[other]
+    gvec_ref[...] = vec_total
+
+    for copy in late_first + [late_second, part_send(0), part_send(1), vec_first] + early_first + early_second + vec_second + vec_third:
+        copy.wait_send()
+    for step, other in enumerate(others):
+        @pl.when(other >= owners)
         def _():
-            from_peer(slot, vec_group, vg_got, None).wait_recv()
-
-        vec_total = vec_total + jnp.where(place != slot, vec_group[slot], 0.0)
-    vec_all[...] = vec_total
-    to_others = [
-        send(vec_all, vec_every.at[group], va_sent.at[step], va_got.at[group], device)
-        for step, device in enumerate(other_devices)
-    ]
-    for slot in range(groups):
-        @pl.when(group != slot)
-        def _():
-            from_peer(slot, vec_every, va_got, None).wait_recv()
-
-        vec_total = vec_total + jnp.where(group != slot, vec_every[slot], 0.0)
-    gvec_ref[...] = vec_total
+            late_third(step).wait_send()
 
     if groups > 1:
-        @pl.when(group == 0)
-        def _():
-            total = gw_ref[...]
-            for slot in range(groups - 1):
-                from_peer(slot, gw_fourth, fourth_got, None).wait_recv()
-                total = total + gw_fourth[slot].astype(F32)
-            gw_ref[...] = total
-
         @pl.when(group > 0)
         def _():
-            pltpu.make_async_remote_copy(
-                src_ref=gw_own.at[0, 0], dst_ref=gw_fourth.at[group - 1], send_sem=fourth_sent,
-                recv_sem=fourth_got.at[group - 1], device_id=(place, blk), device_id_type=MESH,
-            ).wait_send()
-
-    for copy in first + halves + [second] + third + [to_near, to_far] + to_peers + to_others:
-        copy.wait_send()
-    for copy in outs:
-        copy.wait()
-    for copy in keeps:
-        copy.wait()
-
-
-def finish(ctx_size, blk_size, rows_all, gmid, dq, part, gw, w_query, vec):
+            early_third.wait_send()
+
+    out_keep.wait()
+    out_send.wait()
+    for c in range(chunks):
+        grad_keep(c, size).wait()
+        grad_send(1, c, size).wait()
+
+
+def back(ctx_size, blk_size, per, owners, qa, doa, qt, dot_t, kta, vta, kn, ln, rows_all, gmid, out, late, gvec, w_input, vec):
     own, width = gmid.shape
+    head = width // HEADS
+    total = 2 * own
     length = own // 2
-    _, owners, per, _ = gw.shape
     groups = ctx_size // owners
+    _, late_count, padded, _ = late.shape
     dma = pltpu.SemaphoreType.DMA
     place = pl.BlockSpec(memory_space=pl.ANY)
     vmem = pl.BlockSpec(memory_space=pltpu.VMEM)
     chunks = length // min(512, length)
     low = lambda *shape: pltpu.VMEM(shape, BF)
     single = lambda *shape: pltpu.VMEM(shape, F32)
+    plane = 2 * owners
+    some = lambda count: dma((max(count, 1),))
     return pl.pallas_call(
-        functools.partial(finish_kernel, ctx_size, blk_size),
-        in_specs=[place] * 5 + [vmem] * 2,
-        out_specs=[place, vmem, vmem],
+        functools.partial(back_kernel, ctx_size, blk_size, per),
+        in_specs=[place] * 12 + [vmem] * 3,
+        out_specs=[place, place, vmem, vmem],
         out_shape=[
             jax.ShapeDtypeStruct((2, length, width), BF),
-            jax.ShapeDtypeStruct((per, width), F32),
-            jax.ShapeDtypeStruct((8, width), F32),
+            jax.ShapeDtypeStruct((2, length, width), BF),
+            jax.ShapeDtypeStruct((padded, width), F32),
+            jax.ShapeDtypeStruct((16, width), F32),
         ],
         scratch_shapes=[
-            low(own, width), single(own, width), low(HEADS, own, 128), low(width, own), low(width, own),
-            low(2, owners, per, width), low(2, owners, per, width), low(2, owners, per, width),
-            low(owners, per, width), low(owners, per, width), low(owners, per, width), low(max(groups - 1, 1), per, width),
-            low(own, width), single(8, width), single(8, width), single(8, width), single(8, width), single(8, width),
-            single(owners, 8, width), single(8, width), single(groups, 8, width), low(HEADS * 128, width),
-            dma((10,)), dma((2,)), dma((2,)), dma((2,)), dma((2,)), dma, dma, dma((max(owners - 1, 1),)), dma((owners,)),
-            dma, dma((max(groups - 1, 1),)), dma((chunks,)), dma((chunks,)), dma((chunks,)), dma, dma, dma, dma,
-            dma((max(owners - 1, 1),)), dma((owners,)), dma((max(groups - 1, 1),)), dma((groups,)),
+            low(HEADS, own, 128), low(HEADS, own, 128), low(HEADS, head, own), low(HEADS, head, own),
+            low(HEADS, AUG, total), low(HEADS, AUG, total), low(HEADS, total, 128), low(total, width),
+            low(own, width), single(own, width), low(own, width),
+            single(HEADS, own, 128), single(HEADS, head, total), single(HEADS, head, total),
+            single(width, HEADS * 128), single(width, width), single(width, width),
+            single(2, width, length), low(2, width, length), low(2, width, length), low(HEADS * 128, width),
+            low(2, late_count, padded, width), low(2, late_count, padded, width), low(2, late_count, padded, width),
+            low(late_count, padded, width), low(late_count, padded, width), low(ctx_size, padded, width),
+            low(blk_size, owners, padded, width), low(2, owners, padded, width), low(2, owners, padded, width),
+            low(plane, padded, width), low(padded, width), low(max(groups - 1, 1), padded, width),
+            single(16, width), single(16, width), single(16, width), single(plane, 16, width), single(16, width),
+            single(groups, 16, width),
+            dma((7, HEADS)), dma((5,)), dma, dma, dma((1 + chunks,)), dma((chunks,)), dma((chunks,)), dma((2,)), dma((2,)),
+            dma((2,)), dma((2,)), dma, dma, some(ctx_size - 1), dma((ctx_size,)),
+            dma((2,)), dma((2,)), some(plane - 1), dma((plane,)), dma, some(groups - 1),
+            dma, dma, some(plane - 1), dma((plane,)), some(groups - 1), dma((groups,)),
         ],
         compiler_params=params(collective_id=2, has_side_effects=True),
-        name="finish",
-    )(rows_all, gmid, dq, part, gw, w_query, vec)
+        name="back",
+    )(qa, doa, qt, dot_t, kta, vta, kn, ln, rows_all, gmid, out, late, gvec, w_input, vec)
 
 
 def per_device(ctx_size, blk_size, layer_in, matrices, vectors, out_grad):
@@ -834,6 +845,7 @@
     vec = every[:, slots, :entries].reshape(-1, width).astype(F32)
     vec = jnp.pad(vec, ((0, 16 - vec.shape[0]), (0, 0)))
 
+    rows_all, out_grad = lax.optimization_barrier((rows_all, out_grad))
     kept = lax.dynamic_index_in_dim(out_grad, mine, 0, keepdims=False)
     sent = lax.dynamic_index_in_dim(out_grad, 1 - mine, 0, keepdims=False)
     grad = jnp.concatenate([kept, lax.ppermute(sent, "blk", far)], 0)
@@ -841,25 +853,12 @@
     own = 2 * local_rows
     ln, qt, kn, kta, vta = prep(rows_all, own, w_input, vec_in)
     att, lse = attend(qt, kn, kta, vta)
-    out, gmid, qa, doa, dot_t, gwo, gup, gdown, gvec = between(rows_all, grad, att, lse, qt, weights, vec)
-
-    got = lax.ppermute(out[local_rows:], "blk", far)
-    layer_out = jnp.where(mine == 0, jnp.stack([out[:local_rows], got]), jnp.stack([got, out[:local_rows]]))
-
-    late = jnp.concatenate([jnp.zeros((in_rows, width), F32), gwo, gup.T, gdown.T], 0).reshape(devices, per, width)
-    count = entries * devices // width
-    late_vec = jnp.concatenate([jnp.zeros((2, width), F32), gvec[2:count]], 0).reshape(devices, 1, entries)
-    late_vec = jnp.pad(late_vec, ((0, 0), (0, 7), (0, width - entries)))
-    late = jnp.pad(late, ((0, 0), (0, -per % 8), (0, 0)))
-    summed = lax.psum_scatter(jnp.concatenate([late, late_vec], 1), ("ctx", "blk"), scatter_dimension=0, tiled=False)
-
-    dq, dk, dv = attend_back(qa, doa, qt, dot_t, kta, vta, kn)
-    gw, part = unproject(dq, dk, dv, ln, w_input, (blk_size, owners, per))
-    layer_grad, gw_in, gvec_in = finish(ctx_size, blk_size, rows_all, gmid, dq, part, gw, w_input[:width], vec_in)
-    matrices_grad = jnp.where(flat < in_rows // per, gw_in[:per], summed[:per])
-    early = jnp.pad(gvec_in[:2].reshape(-1), (0, entries * devices - 2 * width))
-    vectors_grad = summed[per + -per % 8, :entries] + lax.dynamic_slice_in_dim(early, flat * entries, entries)
-    return layer_out, layer_grad, matrices_grad, vectors_grad
+    out, gmid, qa, doa, dot_t, late, gvec = between(rows_all, grad, att, lse, qt, weights, vec, blk_size, per)
+    layer_grad, layer_out, matrices_grad, vecs = back(
+        ctx_size, blk_size, per, owners, qa, doa, qt, dot_t, kta, vta, kn, ln, rows_all, gmid, out, late, gvec, w_input, vec_in
+    )
+    vectors_grad = lax.dynamic_slice_in_dim(vecs.reshape(-1), flat * entries, entries)
+    return layer_out, layer_grad, matrices_grad[:per], vectors_grad
 
 
 def solution(mesh):

time: 278 us -> 222 us (0.80)
  Pallas kernels: 215 us -> 192 us
  waiting for transfers between devices: 13.2 us -> 0.02 us
  other arithmetic: 13.3 us -> 3.7 us
  local copies, waits for them, and re-layouts: 16.7 us -> 10.9 us
  starting transfers between devices: 4.97 us -> 1.62 us
    pallas_call x4 -> x2, Pallas kernels: 144 us -> 123 us  [the longest x1 101 us: back(): pl.pallas_call(functools.partial(back_kernel, ctx_size, blk_size, per), i...]
    reduce_scatter x1 -> x0, waiting for transfers between devices: 13.1 us -> none  [per_device(): lax.psum_scatter(jnp.concatenate([late, late_vec], 1), ('ctx', 'blk'), sc...]
    concatenate x2 -> x0, other arithmetic: 5.65 us -> none  [the longest x1 3.57 us: per_device(): jnp.concatenate([jnp.zeros((in_rows, width), F32), gwo, gup.T, gdown.T], 0)]
  transfers between devices with their start and end apart: 4 -> 2, of which waited for: 1 -> 0; matrix products, arithmetic and copies ran while one was open for 3% -> 2% of each run, Pallas kernels for 69% -> 31%
where the time goes in v3:
time: 222 us
  Pallas kernels  192 us (86%)
  between operations  14.1 us (6%)
  local copies, waits for them, and re-layouts  10.9 us (5%)
  other arithmetic  3.7 us (2%)
    pallas_call x1, Pallas kernels, back(): pl.pallas_call(functools.partial(back_kernel, ctx_size, blk_size, per), i...  101 us
    pallas_call x1, Pallas kernels, attend(): pl.pallas_call(attend_kernel, grid=(HEADS,), in_specs=[per_head(head, own...  32.5 us
    pallas_call x1, Pallas kernels, exchange(): pl.pallas_call(functools.partial(exchange_kernel, ctx_size, blk_size), in...  25.1 us
    pallas_call x1, Pallas kernels, between(): pl.pallas_call(functools.partial(middle_kernel, per), grid=(own // block,...  22.5 us
    pallas_call x1, Pallas kernels, prep(): pl.pallas_call(functools.partial(prep_kernel, own_steps), grid=(steps,),...  10.7 us
    unnamed x10, local copies, waits for them, and re-layouts  4.73 us
  transfers between devices with their start and end apart: 2, of which 0 were waited for; matrix products, arithmetic and copies ran while one was open for 2% of the time, Pallas kernels for 31%

profile of v3, /device:TPU:0, one launch (start us, length us, event | category | flops | bytes accessed | tf_op | source)
XLA Modules:
  0.0 221.9 jit_solution(17620383393069850475)
XLA Ops:
  7.2 0.0 all-gather.3.cloned.1.call-start
  7.2 1.4 fusion.1.w_ref
  8.7 0.0 all-gather.3.cloned.1.call-update
  8.7 25.1 %exchange.1 = (bf16[4096,256]{1,0:T(8,128)(2,1)}, bf16[8,112,256]{2,1,0:T(8,128)(2,1)}) custom-call(bf16[2,1024,256]{2,1,0:T(8,128)(2,1)} %x_ref.1, bf16[112,256]{1,0:T(8,128)(2,1)} %fusion.1.w_ref), custom_call_target="tpu_custom_call" | custom-call | tf_op jit(solution)/shard_map/exchange/pallas_call | solution.py:163
  33.8 0.0 copy-start.1
  33.9 1.3 dynamic-slice_bitcast_fusion.1
  35.2 1.6 collective-permute-start
  36.8 0.0 copy-done.1
  36.8 0.8 slice.20
  37.6 0.1 reshape_squeeze.4
  37.7 0.6 pad_convert_fusion.1.vec_ref
  38.3 10.7 %project.1 = (bf16[4096,256]{1,0:T(8,128)(2,1)}, bf16[4,64,2048]{2,1,0:T(8,128)(2,1)}, bf16[4,4096,128]{2,1,0:T(8,128)(2,1)}, bf16[4,80,4096]{2,1,0:T(8,128)(2,1)}, bf16[4,80,4096]{2,1,0:T(8,128)(2,1)}) custom-call(bf16[4096,256]{1,0:T(8,128)(2,1)} %get-tuple-element.27.x_ref.x_hbm, bf16[768,256]{1,0:T(8,128)(2,1)} %bitcast.11, ...), custom_call_target="tpu_custom_call" | custom-call | tf_op jit(solution)/shard_map/project/pallas_call | solution.py:225
  49.0 32.5 %attend.1 = (f32[4,64,2048]{2,1,0:T(8,128)}, f32[4,8,2048]{2,1,0:T(8,128)}) custom-call(bf16[4,64,2048]{2,1,0:T(8,128)(2,1)} %get-tuple-element.30.qt_ref.qt_hbm, bf16[4,4096,128]{2,1,0:T(8,128)(2,1)} %get-tuple-element.31.kn_ref.kn_hbm, bf16[4,80,4096]{2,1,0:T(8,128)(2,1)} %get-tuple-element.32.kta_ref.kta_hbm, ...), custom_call_target="tpu_custom_call" | custom-call | tf_op jit(solution)/shard_map/attend/pallas_call | solution.py:315
  81.5 0.0 collective-permute-done
  81.5 1.0 pad_maximum_fusion.g_ref
  82.5 0.0 all-gather.3.cloned.1.call-done
  82.5 0.9 slice_reduce_fusion
  83.4 2.4 %slice.26 = bf16[24,96,256]{2,1,0:T(8,128)(2,1)} slice(bf16[32,112,256]{2,1,0:T(8,128)(2,1)} %bitcast.14), slice={[8:32], [0:96], [0:256]} | slice | bytes 2359296 | tf_op jit(solution)/shard_map/slice | solution.py:844
  85.8 0.1 convert_element_type.15
  85.9 0.6 pad_convert_fusion.vec_ref
  86.5 22.5 %between.1 = (bf16[2048,256]{1,0:T(8,128)(2,1)}, f32[2048,256]{1,0:T(8,128)}, bf16[4,2048,128]{2,1,0:T(8,128)(2,1)}, bf16[4,2048,128]{2,1,0:T(8,128)(2,1)}, bf16...) custom-call(bf16[4096,256]{1,0:T(8,128)(2,1)} %get-tuple-element.27.x_ref.x_hbm, ...), custom_call_target="tpu_custom_call" | custom-call | tf_op jit(solution)/shard_map/between/pallas_call | solution.py:438
  109.0 100.7 %back.1 = (bf16[2,1024,256]{2,1,0:T(8,128)(2,1)}, bf16[2,1024,256]{2,1,0:T(8,128)(2,1)}, f32[96,256]{1,0:T(8,128)}, f32[16,256]{1,0:T(8,128)}) custom-call(bf16[4,2048,128]{2,1,0:T(8,128)(2,1)} %get-tuple-element.36.qa_hbm, bf16[4,2048,128]{2,1,0:T(8,128)(2,1)} %get-tuple-element.37.doa_hbm, bf16[4,64,2048]{2,1,0:T(8,128)(2,1)} %get-tuple-element.30.qt_ref.qt_hbm, ...), custom_call_target="tpu_custom_call" | custom-call | tf_op jit(solution)/shard_map/back/pallas_call | solution.py:787
  209.7 0.0 copy-start
  209.7 0.8 copy.11
  210.6 0.6 dynamic_slice.12
  211.2 0.0 copy-start.2
  211.2 2.3 %copy.15 = bf16[2,1024,256]{2,1,0:T(8,128)(2,1)} copy(bf16[2,1024,256]{2,1,0:T(8,128)(2,1)} %get-tuple-element.54) | data formatting | bytes 2097152
  213.5 0.0 copy-done
  213.5 1.0 copy.16
  214.4 0.0 copy-done.2
  214.4 0.6 copy.17
  (3 shorter events, 0.0 us)
Async XLA Ops:
  7.2 75.3 %all-gather.3.cloned.1.call-start = ((), (), s32[]{:S(2)}) async-start(), calls=%async_computation | async-start | bytes 1892352 | tf_op jit(solution)/shard_map/all_gather | solution.py:843
  33.8 2.9 %copy-start.1 = (bf16[8,112,256]{2,1,0:T(8,128)(2,1)S(1)}, bf16[8,112,256]{2,1,0:T(8,128)(2,1)}, u32[]{:S(2)}) copy-start(bf16[8,112,256]{2,1,0:T(8,128)(2,1)} %get-tuple-element.29) | copy-start | bytes 1376260
  35.2 46.3 %collective-permute-start = (bf16[1024,256]{1,0:T(8,128)(2,1)S(1)}, bf16[1024,256]{1,0:T(8,128)(2,1)S(1)}, u32[]{:S(2)}, u32[]{:S(2)}) collective-permute-start(bf16[1024,256]{1,0:T(8,128)(2,1)S(1)} %get-tuple-element.49), channel_id=1, source_target_pairs={{0,2},{1,3},{2,0},{3,1},{4,6},{5,7},{6,4},{7,5},{8,10},{9,11},{10,... | collective-permute-start | bytes 1572872 | tf_op jit(solution)/shard_map/ppermute | solution.py:851
  209.7 3.7 %copy-start = (bf16[2,1024,256]{2,1,0:T(8,128)(2,1)S(1)}, bf16[2,1024,256]{2,1,0:T(8,128)(2,1)}, u32[]{:S(2)}) copy-start(bf16[2,1024,256]{2,1,0:T(8,128)(2,1)} %get-tuple-element.55) | copy-start | bytes 3145732
  211.2 3.3 %copy-start.2 = (f32[96,256]{1,0:T(8,128)S(1)}, f32[96,256]{1,0:T(8,128)}, u32[]{:S(2)}) copy-start(f32[96,256]{1,0:T(8,128)} %get-tuple-element.56) | copy-start | bytes 294916
Sparse Core Ops, SparseCore 0:
  11.5 58.9 all-gather.2

commit v4 on v3

--- a/solution.py
+++ b/solution.py
@@ -16,6 +16,8 @@
 SAFE_BOUND = 90.0
 BF = jnp.bfloat16
 F32 = jnp.float32
+F8 = jnp.float8_e4m3fn
+PIECES = (256.0, 16.0, 1.0, 0.0625)
 NT = (((1,), (1,)), ((), ()))
 TN = (((0,), (0,)), ((), ()))
 
@@ -58,14 +60,6 @@
 MESH = pl.DeviceIdType.MESH
 
 
-def send(source, target, sent, received, device):
-    copy = pltpu.make_async_remote_copy(
-        src_ref=source, dst_ref=target, send_sem=sent, recv_sem=received, device_id=device, device_id_type=MESH
-    )
-    copy.start()
-    return copy
-
-
 def greet(devices):
     barrier = pltpu.get_barrier_semaphore()
     for device in devices:
@@ -79,180 +73,287 @@
     return ctx, blk, blk + 1 - 2 * lax.rem(blk, 2), lax.rem(blk + half, blk_size), lax.div(blk, half)
 
 
-def exchange_kernel(
-    ctx_size, blk_size, x_ref, w_ref, rows_ref, all_ref,
-    far_sent, far_got, near_sent, near_got, relay_sent, relay_got, own_sem,
-    first_sent, first_got, second_sent, second_got, third_sent, third_got, keep_sem,
+def start_kernel(
+    ctx_size, blk_size, per,
+    x_hbm, w_hbm, v_ref,
+    rows_out, ln_out, qt_out, kn_out, kta_out, vta_out, vec_ref,
+    x, ln, qt, kn, kta, vta, w_slots, w_all, wt, wkp, v_own, v_slots,
+    x_sem, far_sent, far_got, near_sent, near_got, relay_sent, relay_got, keep_sem,
+    w1_sent, w1_got, w2_sent, w2_got, w3_sent, w3_got, v1_sent, v1_got, v2_sent, v2_got, v3_sent, v3_got,
+    rows_sem, out_sem,
 ):
     ctx, blk, near, far, mine = partners(blk_size)
-    length = x_ref.shape[1]
-    owners = all_ref.shape[0] // blk_size
+    _, length, width = x_hbm.shape
+    head = width // HEADS
+    entries = v_ref.shape[1]
+    owners = w_slots.shape[0] // blk_size
     chunks = far_sent.shape[0]
     size = length // chunks
+    to_near, to_far = (ctx, near), (ctx, far)
     others = [lax.rem(ctx + step, ctx_size) for step in range(1, ctx_size)]
-    greet([(ctx, near), (ctx, far)] + [(other, blk) for other in others])
-
-    @pl.when(ctx < owners)
+
+    def remote(source, target, sent, got, device):
+        return pltpu.make_async_remote_copy(
+            src_ref=source, dst_ref=target, send_sem=sent, recv_sem=got, device_id=device, device_id_type=MESH
+        )
+
+    local = pltpu.make_async_copy
+    own_rows = local(x_hbm.at[mine], x.at[pl.ds(0, length)], x_sem)
+    near_rows = remote(x_hbm.at[mine], x.at[pl.ds(2 * length, length)], near_sent, near_got, to_near)
+    far_rows = [
+        remote(x_hbm.at[1 - mine, pl.ds(c * size, size)], x.at[pl.ds(length + c * size, size)], far_sent.at[c], far_got.at[c], to_far)
+        for c in range(chunks)
+    ]
+    relay_rows = [
+        remote(
+            x.at[pl.ds(length + c * size, size)], x.at[pl.ds(3 * length + c * size, size)],
+            relay_sent.at[c], relay_got.at[c], to_near,
+        )
+        for c in range(chunks)
+    ]
+    groups = ctx_size // owners
+    group, place = lax.div(ctx, owners), lax.rem(ctx, owners)
+    peers = [lax.rem(place + step, owners) for step in range(1, owners)]
+    mine_slot = place * blk_size + blk
+    keep_w = local(w_hbm, w_slots.at[mine_slot], keep_sem)
+    w_first = [
+        remote(w_hbm, w_slots.at[mine_slot], w1_sent.at[g - 1], w1_got, (g * owners + place, blk)) for g in range(1, groups)
+    ]
+    plane = [(place, far, to_far)]
+    for peer in peers:
+        plane += [(peer, blk, (group * owners + peer, blk)), (peer, far, (group * owners + peer, far))]
+    here = place * 2 + mine
+    w_second = [
+        remote(w_slots.at[mine_slot], w_slots.at[mine_slot], w2_sent.at[i], w2_got.at[here], device)
+        for i, (_, _, device) in enumerate(plane)
+    ]
+    w_third = [
+        remote(w_slots.at[r * blk_size + b], w_slots.at[r * blk_size + b], w3_sent.at[i], w3_got.at[i], to_near)
+        for i, (r, b, _) in enumerate([(place, blk, None)] + plane)
+    ]
+    v_first = [remote(v_own, v_slots.at[blk, ctx], v1_sent.at[i], v1_got.at[ctx], (other, blk)) for i, other in enumerate(others)]
+    v_second = remote(v_slots.at[blk], v_slots.at[blk], v2_sent, v2_got, to_far)
+    v_third = [remote(v_slots.at[b], v_slots.at[b], v3_sent.at[i], v3_got.at[i], to_near) for i, b in enumerate((blk, far))]
+    rows_keep = local(x.at[pl.ds(0, 2 * length)], rows_out, rows_sem)
+
+    greet([to_near, to_far] + [(other, blk) for other in others] + [(group * owners + peer, far) for peer in peers])
+    v_own[...] = jnp.zeros_like(v_own)
+    v_own[0:1, :entries] = v_ref[...].astype(F32)
+
+    @pl.when(group == 0)
     def _():
-        keep = pltpu.make_async_copy(w_ref, all_ref.at[ctx * blk_size + blk], keep_sem)
-        keep.start()
-        for step, other in enumerate(others):
-            send(w_ref, all_ref.at[ctx * blk_size + blk], first_sent.at[step], first_got.at[ctx], (other, blk))
-
-    far_copies = []
-    for c in range(chunks):
-        part = pl.ds(c * size, size)
-        far_copies.append(
-            send(x_ref.at[1 - mine, part], rows_ref.at[pl.ds(length + c * size, size)], far_sent.at[c], far_got.at[c], (ctx, far))
-        )
-    near_copy = send(x_ref.at[mine], rows_ref.at[pl.ds(2 * length, length)], near_sent, near_got, (ctx, near))
-    own_copy = pltpu.make_async_copy(x_ref.at[mine], rows_ref.at[pl.ds(0, length)], own_sem)
-    own_copy.start()
-
-    @pl.when(ctx < owners)
+        keep_w.start()
+        for copy in w_first:
+            copy.start()
+
+    early = max(chunks // 2, 1)
+    for copy in far_rows[:early]:
+        copy.start()
+    own_rows.start()
+    near_rows.start()
+    for copy in v_first:
+        copy.start()
+    v_slots[blk, ctx] = v_own[...]
+
+    @pl.when(group == 0)
     def _():
-        pltpu.make_async_copy(w_ref, all_ref.at[ctx * blk_size + blk], keep_sem).wait()
-
-    def copy_of(slot, sent, got, device):
-        return pltpu.make_async_remote_copy(
-            src_ref=all_ref.at[slot], dst_ref=all_ref.at[slot], send_sem=sent, recv_sem=got,
-            device_id=device, device_id_type=MESH,
-        )
-
-    for o in range(owners):
-        @pl.when(ctx != o)
-        def _():
-            copy_of(o * blk_size + blk, first_sent.at[0], first_got.at[o], (ctx, near)).wait_recv()
-
-        copy_of(o * blk_size + blk, second_sent.at[o], second_got.at[o], (ctx, far)).start()
-        copy_of(o * blk_size + blk, third_sent.at[o], third_got.at[o], (ctx, near)).start()
-    relays = []
-    for c in range(chunks):
-        far_copies[c].wait_recv()
-        here = rows_ref.at[pl.ds(length + c * size, size)]
-        there = rows_ref.at[pl.ds(3 * length + c * size, size)]
-        relays.append(send(here, there, relay_sent.at[c], relay_got.at[c], (ctx, near)))
-    for o in range(owners):
-        copy_of(o * blk_size + far, second_sent.at[o], second_got.at[o], (ctx, far)).wait_recv()
-        copy_of(o * blk_size + far, third_sent.at[owners + o], third_got.at[owners + o], (ctx, near)).start()
-
-    for o in range(owners):
-        copy_of(o * blk_size + blk, second_sent.at[o], second_got.at[o], (ctx, far)).wait_send()
-        for turn in range(2):
-            copy_of(o * blk_size + blk, third_sent.at[turn * owners + o], third_got.at[turn * owners + o], (ctx, near)).wait()
-    for c in range(chunks):
-        far_copies[c].wait_send()
-        relays[c].wait()
-    near_copy.wait()
-    own_copy.wait()
-
-    @pl.when(ctx < owners)
+        keep_w.wait()
+
+    if groups > 1:
+        @pl.when(group > 0)
+        def _():
+            w_first[0].wait_recv()
+
+    for copy in w_second:
+        copy.start()
+    w_third[0].start()
+    for other in others:
+        remote(v_own, v_slots.at[blk, other], v1_sent.at[0], v1_got.at[other], to_far).wait_recv()
+    v_second.start()
+    v_third[0].start()
+    for copy in far_rows[early:]:
+        copy.start()
+    for i, (r, b, _) in enumerate(plane):
+        slot = r * blk_size + b
+        remote(w_slots.at[slot], w_slots.at[slot], w2_sent.at[0], w2_got.at[r * 2 + lax.div(b, 2)], to_far).wait_recv()
+        w_third[i + 1].start()
+    remote(v_slots.at[far], v_slots.at[far], v2_sent, v2_got, to_far).wait_recv()
+    v_third[1].start()
+    for c in range(early):
+        far_rows[c].wait_recv()
+        relay_rows[c].start()
+    for copy in w_third + v_third:
+        copy.wait_recv()
+
+    total = jnp.zeros((16, width), F32)
+    place = lax.broadcasted_iota(jnp.int32, (16, width), 0)
+    lane = lax.broadcasted_iota(jnp.int32, (16, width), 1)
+    for o in range(ctx_size * blk_size):
+        row, shift = (o * entries) // width, (o * entries) % width
+        piece = jnp.concatenate([v_slots[o % blk_size, o // blk_size], jnp.zeros((8, width - 128), F32)], 1)
+        if shift:
+            piece = pltpu.roll(piece, shift, 1)
+        piece = jnp.broadcast_to(piece[0:1, :], (16, width))
+        total = total + jnp.where((place == row) & (lane >= shift), piece, 0.0)
+        if shift + entries > width:
+            total = total + jnp.where((place == row + 1) & (lane < shift), piece, 0.0)
+    vec_ref[...] = total
+    for slot in range(w_slots.shape[0]):
+        w_all[slot * per : (slot + 1) * per, :] = w_slots[slot, :per, :].astype(F32)
+    for index in range(3):
+        wt[index * width : (index + 1) * width, :] = w_all[index * width : (index + 1) * width, :].T.astype(BF)
+    wk = w_all[width : 2 * width, :]
+    for h in range(HEADS):
+        wide = jnp.concatenate([wk[:, h * head : (h + 1) * head], jnp.zeros((width, 128 - head), F32)], 1)
+        wkp[:, h * 128 : (h + 1) * 128] = wide.astype(BF)
+    own_rows.wait()
+
+    block = min(512, length)
+    per_quarter = length // block
+    extra = (lax.broadcasted_iota(jnp.int32, (AUG - head, block), 0) < 3).astype(F32).astype(BF)
+
+    def out_copies(base, index):
+        rows = pl.ds(base, block)
+        pairs = ((ln, ln_out), (kn, kn_out), (kta, kta_out), (vta, vta_out))
+        copies = []
+        for i, (a, b) in enumerate(pairs):
+            if i == 0:
+                copies.append(local(a.at[rows], b.at[rows], out_sem.at[i, index]))
+            elif i == 1:
+                copies.append(local(a.at[:, rows], b.at[:, rows], out_sem.at[i, index]))
+            else:
+                copies.append(local(a.at[:, :, rows], b.at[:, :, rows], out_sem.at[i, index]))
+        return copies
+
+    def first_row(index):
+        quarter = lax.div(index, per_quarter)
+        order = lax.rem(quarter, 2) * 2 + lax.div(quarter, 2)
+        return pl.multiple_of(order * length + lax.rem(index, per_quarter) * block, block)
+
+    @pl.loop(0, 4 * per_quarter)
+    def _(index):
+        quarter = lax.div(index, per_quarter)
+
+        @pl.when(index == per_quarter)
+        def _():
+            near_rows.wait_recv()
+
+        @pl.when(index == 2 * per_quarter)
+        def _():
+            for c in range(early, chunks):
+                far_rows[c].wait_recv()
+                relay_rows[c].start()
+            rows_keep.start()
+
+        @pl.when(index == 3 * per_quarter)
+        def _():
+            for c in range(chunks):
+                relay_rows[c].wait_recv()
+
+        base = first_row(index)
+        rows = pl.ds(base, block)
+        normed, _ = normalize(x[rows, :].astype(F32))
+        low = (normed * vec_ref[0:1, :] + vec_ref[1:2, :]).astype(BF)
+        ln[rows, :] = low
+        kt = dot_nt(wt[width : 2 * width, :], low).astype(BF)
+        vt = dot_nt(wt[2 * width : 3 * width, :], low).astype(BF)
+        wide = dot(low, wkp[...]).astype(BF)
+        for h in range(HEADS):
+            kta[h, :head, rows] = kt[h * head : (h + 1) * head, :]
+            kta[h, head:, rows] = extra
+            vta[h, :head, rows] = vt[h * head : (h + 1) * head, :]
+            vta[h, head:, rows] = extra
+            kn[h, rows, :] = wide[:, h * 128 : (h + 1) * 128]
+
+        @pl.when(lax.rem(quarter, 2) == 0)
+        def _():
+            queries = dot_nt(wt[0:width, :], low) * (LOG2E / math.sqrt(head))
+            for h in range(HEADS):
+                qt[h, :, rows] = queries[h * head : (h + 1) * head, :].astype(BF)
+
+        for copy in out_copies(base, index):
+            copy.start()
+
+    qt_copy = local(qt, qt_out, x_sem)
+    qt_copy.start()
+
+    @pl.loop(0, 4 * per_quarter)
+    def _(index):
+        for copy in out_copies(first_row(index), index):
+            copy.wait()
+
+    qt_copy.wait()
+    rows_keep.wait()
+
+    @pl.when(group == 0)
     def _():
-        for step, other in enumerate(others):
-            pltpu.make_async_remote_copy(
-                src_ref=w_ref, dst_ref=all_ref.at[ctx * blk_size + blk], send_sem=first_sent.at[step],
-                recv_sem=first_got.at[ctx], device_id=(other, blk), device_id_type=MESH,
-            ).wait_send()
-
-
-def exchange(ctx_size, blk_size, layer_in, block, owners):
+        for copy in w_first:
+            copy.wait_send()
+
+    for copy in v_first + [v_second] + v_third + far_rows + relay_rows + [near_rows] + w_second + w_third:
+        copy.wait_send()
+
+
+def start(ctx_size, blk_size, layer_in, matrices, vectors, owners):
     seq_count, length, width = layer_in.shape
+    per, entries = matrices.shape[0], vectors.shape[0]
+    padded = -(-per // 16) * 16
+    if padded > per:
+        matrices = jnp.pad(matrices, ((0, padded - per), (0, 0)))
+    head = width // HEADS
+    own, total = 2 * length, 4 * length
     chunks = 4 if length % 64 == 0 else 1
+    blocks = total // min(512, length)
     dma = pltpu.SemaphoreType.DMA
     place = pl.BlockSpec(memory_space=pl.ANY)
+    vmem = pl.BlockSpec(memory_space=pltpu.VMEM)
+    low = lambda *shape: pltpu.VMEM(shape, BF)
+    single = lambda *shape: pltpu.VMEM(shape, F32)
+    some = dma((max(ctx_size - 1, 1),))
+    shapes = [(own, width), (total, width), (HEADS, head, own), (HEADS, total, 128), (HEADS, AUG, total), (HEADS, AUG, total)]
     return pl.pallas_call(
-        functools.partial(exchange_kernel, ctx_size, blk_size),
-        in_specs=[place] * 2,
-        out_specs=[place] * 2,
-        out_shape=[
-            jax.ShapeDtypeStruct((4 * length, width), BF),
-            jax.ShapeDtypeStruct((owners * blk_size, *block.shape), BF),
-        ],
+        functools.partial(start_kernel, ctx_size, blk_size, per),
+        in_specs=[place, place, vmem],
+        out_specs=[place] * 6 + [vmem],
+        out_shape=[jax.ShapeDtypeStruct(shape, BF) for shape in shapes] + [jax.ShapeDtypeStruct((16, width), F32)],
         scratch_shapes=[
-            dma((chunks,)), dma((chunks,)), dma, dma, dma((chunks,)), dma((chunks,)), dma,
-            dma((ctx_size - 1,)) if ctx_size > 1 else dma((1,)), dma((owners,)), dma((owners,)), dma((owners,)),
-            dma((2 * owners,)), dma((2 * owners,)), dma,
+            low(total, width), low(total, width), low(HEADS, head, own), low(HEADS, total, 128),
+            low(HEADS, AUG, total), low(HEADS, AUG, total),
+            low(owners * blk_size, padded, width), single(owners * blk_size * per, width),
+            low(3 * width, width), low(width, HEADS * 128), single(8, 128), single(blk_size, ctx_size, 8, 128),
+            dma, dma((chunks,)), dma((chunks,)), dma, dma, dma((chunks,)), dma((chunks,)), dma,
+            dma((max(ctx_size // owners - 1, 1),)), dma, dma((2 * owners,)), dma((2 * owners,)), dma((2 * owners,)), dma((2 * owners,)),
+            some, dma((ctx_size,)), dma, dma, dma((2,)), dma((2,)),
+            dma, dma((4, blocks)),
         ],
         compiler_params=params(collective_id=1, has_side_effects=True),
-        name="exchange",
-    )(layer_in, block)
-
-
-def prep_kernel(own_steps, x_ref, w_ref, vec_ref, ln_ref, qt_ref, kn_ref, kta_ref, vta_ref, wt, wkp):
-    width = x_ref.shape[1]
-    head = width // HEADS
-    step = pl.program_id(0)
-
-    @pl.when(step == 0)
-    def _():
-        for index in range(3):
-            piece = w_ref[index * width : (index + 1) * width, :].astype(F32)
-            wt[index * width : (index + 1) * width, :] = piece.T.astype(BF)
-        wk = w_ref[width : 2 * width, :].astype(F32)
-        for h in range(HEADS):
-            wide = jnp.concatenate([wk[:, h * head : (h + 1) * head], jnp.zeros((width, 128 - head), F32)], 1)
-            wkp[:, h * 128 : (h + 1) * 128] = wide.astype(BF)
-
-    normed, _ = normalize(x_ref[...].astype(F32))
-    ln = (normed * vec_ref[0:1, :] + vec_ref[1:2, :]).astype(BF)
-    ln_ref[...] = ln
-    rows = ln.shape[0]
-    extra = (lax.broadcasted_iota(jnp.int32, (AUG - head, rows), 0) < 3).astype(F32).astype(BF)
-
-    kt = dot_nt(wt[width : 2 * width, :], ln).astype(BF)
-    vt = dot_nt(wt[2 * width : 3 * width, :], ln).astype(BF)
-    kn = dot(ln, wkp[...]).astype(BF)
-    for h in range(HEADS):
-        kta_ref[h, :head, :] = kt[h * head : (h + 1) * head, :]
-        kta_ref[h, head:, :] = extra
-        vta_ref[h, :head, :] = vt[h * head : (h + 1) * head, :]
-        vta_ref[h, head:, :] = extra
-        kn_ref[h] = kn[:, h * 128 : (h + 1) * 128]
-
-    @pl.when(step < own_steps)
-    def _():
-        qt = dot_nt(wt[0:width, :], ln) * (LOG2E / math.sqrt(head))
-        for h in range(HEADS):
-            qt_ref[h] = qt[h * head : (h + 1) * head, :].astype(BF)
-
-
-def prep(rows_all, own, w_input, vec):
-    total, width = rows_all.shape
-    head = width // HEADS
-    block = min(512, own)
-    steps, own_steps = total // block, own // block
-    last = own_steps - 1
-    return pl.pallas_call(
-        functools.partial(prep_kernel, own_steps),
-        grid=(steps,),
-        in_specs=[
-            pl.BlockSpec((block, width), lambda i: (i, 0)),
-            whole(3 * width, width),
-            whole(*vec.shape),
-        ],
-        out_specs=[
-            pl.BlockSpec((block, width), lambda i: (i, 0)),
-            pl.BlockSpec((HEADS, head, block), lambda i: (0, 0, jnp.minimum(i, last))),
-            pl.BlockSpec((HEADS, block, 128), lambda i: (0, i, 0)),
-            pl.BlockSpec((HEADS, AUG, block), lambda i: (0, 0, i)),
-            pl.BlockSpec((HEADS, AUG, block), lambda i: (0, 0, i)),
-        ],
-        out_shape=[
-            jax.ShapeDtypeStruct((total, width), BF),
-            jax.ShapeDtypeStruct((HEADS, head, own), BF),
-            jax.ShapeDtypeStruct((HEADS, total, 128), BF),
-            jax.ShapeDtypeStruct((HEADS, AUG, total), BF),
-            jax.ShapeDtypeStruct((HEADS, AUG, total), BF),
-        ],
-        scratch_shapes=[pltpu.VMEM((3 * width, width), BF), pltpu.VMEM((width, HEADS * 128), BF)],
-        compiler_params=params(),
-        name="project",
-    )(rows_all, w_input, vec)
-
-
-def attend_kernel(qt_ref, kn_ref, kta_ref, vta_ref, att_ref, lse_ref):
+        name="start",
+    )(layer_in, matrices, vectors.reshape(1, entries))
+
+
+def scale_of(values):
+    peak = jnp.max(jnp.max(jnp.abs(values), 0, keepdims=True), 1, keepdims=True)
+    return jnp.exp2(4.0 - jnp.ceil(jnp.log2(jnp.clip(peak, 1e-30, 1e30))))
+
+
+def two_parts(values):
+    high = values.astype(F8).astype(F32)
+    return high, (values - high).astype(F8).astype(F32)
+
+
+def attend_kernel(qt_ref, kn_ref, kta_ref, vta_ref, att_ref, lse_ref, v8_ref, scale_ref):
     head, own = qt_ref.shape[1:]
     total = kn_ref.shape[1]
+    values = vta_ref[0, :head, :].astype(F32)
+    scale = scale_of(values)
+    scale_ref[0] = jnp.broadcast_to(scale, (8, 128))
+    high, low = two_parts(values * scale)
+    place = lax.broadcasted_iota(jnp.int32, (head, total), 0)
+    ones = jnp.zeros((head, total), F32)
+    for index, piece in enumerate(PIECES):
+        ones = jnp.where(place == index, piece, ones)
+    for index, rows in enumerate((high, high, low, ones)):
+        v8_ref[0, index * head : (index + 1) * head, :] = rows.astype(F8)
     tq = min(1024, own)
     tk = min(256, total)
     count = total // tk
@@ -316,10 +417,12 @@
         attend_kernel,
         grid=(HEADS,),
         in_specs=[per_head(head, own), per_head(total, 128), per_head(AUG, total), per_head(AUG, total)],
-        out_specs=[per_head(head, own), per_head(8, own)],
+        out_specs=[per_head(head, own), per_head(8, own), per_head(4 * head, total), per_head(8, 128)],
         out_shape=[
             jax.ShapeDtypeStruct((HEADS, head, own), F32),
             jax.ShapeDtypeStruct((HEADS, 8, own), F32),
+            jax.ShapeDtypeStruct((HEADS, 4 * head, total), F8),
+            jax.ShapeDtypeStruct((HEADS, 8, 128), F32),
         ],
         compiler_params=params(),
         name="attend",
@@ -327,16 +430,17 @@
 
 
 def gelu_both(value):
-    square = value * value
-    density = jnp.exp(-0.5 * square)
-    place = pl.reciprocal(1.0 + (0.3275911 / math.sqrt(2.0)) * jnp.abs(value), approx=True)
-    series = 1.061405429 * place - 1.453152027
-    series = series * place + 1.421413741
-    series = series * place - 0.284496736
-    series = series * place + 0.254829592
-    tail = 0.5 * series * place * density
+    root = math.sqrt(2.0 * math.pi)
+    density = jnp.exp2(value * value * (-0.5 * LOG2E) - math.log2(root))
+    place = pl.reciprocal((0.3275911 / math.sqrt(2.0)) * jnp.abs(value) + 1.0, approx=True)
+    half = 0.5 * root
+    series = (1.061405429 * half) * place - 1.453152027 * half
+    series = series * place + 1.421413741 * half
+    series = series * place - 0.284496736 * half
+    series = series * place + 0.254829592 * half
+    tail = series * place * density
     below = jnp.where(value >= 0.0, 1.0 - tail, tail)
-    return value * below, below + value * density * (1.0 / math.sqrt(2.0 * math.pi))
+    return value * below, below + value * density
 
 
 def split_rows(level, count):
@@ -349,18 +453,15 @@
 
 
 def middle_kernel(
-    per, x_ref, g_ref, att_ref, lse_ref, qt_ref, w_ref, vec_ref,
-    out_ref, gmid_ref, qa_ref, doa_ref, dot_ref, late_ref, gvec_ref, gwo_ref, gup_ref, gdown_ref,
+    per, mine_ref, x_ref, near_ref, far_ref, att_ref, lse_ref, qt_ref, scale_ref, w_ref, vec_ref,
+    out_ref, gmid_ref, qa_ref, do8_ref, dot_ref, qs_ref, unscale_ref, late_ref, gvec_ref, gwo_ref, gup_ref, gdown_ref,
 ):
     width = x_ref.shape[1]
     head = width // HEADS
     rows = x_ref.shape[0]
-    hidden_width = (w_ref.shape[0] - width) // 2
-    wo = w_ref[:width, :]
-    up = w_ref[width : width + hidden_width, :]
-    down = w_ref[width + hidden_width :, :]
+    hidden_width = (w_ref.shape[0] - 4 * width) // 2
+    wo = w_ref[3 * width : 4 * width, :]
     pieces = hidden_width // width
-    up_bias = jnp.concatenate([vec_ref[4 + p : 5 + p, :] for p in range(pieces)], 1)
     down_bias = vec_ref[4 + pieces : 5 + pieces, :]
     gain, bias = vec_ref[2:3, :], vec_ref[3:4, :]
 
@@ -373,25 +474,32 @@
 
     att = att_ref[...].reshape(width, rows)
     att_low = att.astype(BF)
-    grad = g_ref[...]
+    grad = jnp.where(pl.program_id(0) < pl.num_programs(0) // 2, near_ref[0], far_ref[0])
     gradf = grad.astype(F32)
+    grad_t = gradf.T.astype(BF)
     middle = x_ref[...].astype(F32) + dot_tn(att_low, wo)
     normed, inverse = normalize(middle)
     ln_mid = (normed * gain + bias).astype(BF)
-    upper = dot_nt(ln_mid, up) + up_bias
-    grad_hidden = dot_nt(grad, down)
-    activated, slope = gelu_both(upper)
-    hidden = activated.astype(BF)
-    grad_upper = (grad_hidden * slope).astype(BF)
-    out_ref[...] = (middle + dot(hidden, down) + down_bias).astype(BF)
-    gdown_ref[...] += dot_tn(grad, hidden)
-    gup_ref[...] += dot_tn(ln_mid, grad_upper)
-    grad_ln = dot(grad_upper, up)
-    total_up = jnp.sum(grad_upper.astype(F32), 0, keepdims=True)
+    ln_mid_t = ln_mid.astype(F32).T.astype(BF)
+    result = middle + down_bias
+    grad_ln = jnp.zeros((rows, width), F32)
+    for p in range(pieces):
+        columns = slice(p * width, (p + 1) * width)
+        up = w_ref[(4 + p) * width : (5 + p) * width, :]
+        down = w_ref[(4 + pieces + p) * width : (5 + pieces + p) * width, :]
+        upper = dot_nt(ln_mid, up) + vec_ref[4 + p : 5 + p, :]
+        activated, slope = gelu_both(upper)
+        hidden = activated.astype(BF)
+        grad_upper = dot_nt(grad, down) * slope
+        grad_low = grad_upper.astype(BF)
+        result = result + dot(hidden, down)
+        grad_ln = grad_ln + dot(grad_low, up)
+        gdown_ref[:, columns] += dot(grad_t, hidden)
+        gup_ref[:, columns] += dot(ln_mid_t, grad_low)
+        gvec_ref[4 + p : 5 + p, :] += jnp.sum(grad_low.astype(F32), 0, keepdims=True)
+    out_ref[...] = result.astype(BF)
     gvec_ref[2:3, :] += jnp.sum(grad_ln * normed, 0, keepdims=True)
     gvec_ref[3:4, :] += jnp.sum(grad_ln, 0, keepdims=True)
-    for p in range(pieces):
-        gvec_ref[4 + p : 5 + p, :] += total_up[:, p * width : (p + 1) * width]
     gvec_ref[4 + pieces : 5 + pieces, :] += jnp.sum(gradf, 0, keepdims=True)
     grad_mid = gradf + normalize_back(grad_ln * gain, normed, inverse)
     gmid_ref[...] = grad_mid
@@ -399,15 +507,29 @@
     gwo_ref[...] += dot(att_low, branch)
     grad_att = dot_nt(wo, branch).astype(BF)
     spare = jnp.zeros((128 - AUG, rows), F32)
+    place = lax.broadcasted_iota(jnp.int32, (head, rows), 0)
     for h in range(HEADS):
         mine = slice(h * head, (h + 1) * head)
         grad_head = grad_att[mine, :]
         dot_ref[h] = grad_head
-        delta = jnp.sum(grad_head.astype(F32) * att[mine, :], 0, keepdims=True)
-        wide = jnp.concatenate([grad_head.astype(F32), split_rows(-delta, AUG - head), spare], 0)
-        doa_ref[h] = wide.T.astype(BF)
+        grad_head = grad_head.astype(F32)
+        delta = jnp.sum(grad_head * att[mine, :], 0, keepdims=True)
+        scale = scale_of(grad_head)
+        both = scale * scale_ref[h, 0:1, 0:1]
+        high, low = two_parts(grad_head * scale)
+        left = -delta * both
+        folded = jnp.zeros((head, rows), F32)
+        for index, piece in enumerate(PIECES):
+            part = (left * (1.0 / piece)).astype(F8).astype(F32)
+            left = left - part * piece
+            folded = jnp.where(place == index, part, folded)
+        do8_ref[h, :, : 2 * head] = jnp.concatenate([high, low], 0).T.astype(F8)
+        do8_ref[h, :, 2 * head :] = jnp.concatenate([high, folded], 0).T.astype(F8)
+        unscale_ref[0, h * 8 : (h + 1) * 8, :] = jnp.broadcast_to(1.0 / both, (8, 128))
+        queries = qt_ref[h].astype(F32)
+        qs_ref[h] = (queries / both).astype(BF)
         level = lse_ref[h, 0:1, :]
-        wide = jnp.concatenate([qt_ref[h].astype(F32), split_rows(-level, AUG - head), spare], 0)
+        wide = jnp.concatenate([queries, split_rows(-level, AUG - head), spare], 0)
         qa_ref[h] = wide.T.astype(BF)
 
     @pl.when(pl.program_id(0) == pl.num_programs(0) - 1)
@@ -426,24 +548,27 @@
         slots_ref[slot % blk_size, slot // blk_size] = piece.astype(BF)
 
 
-def between(x, grad, att, lse, qt, weights, vec, blk_size, per):
-    own, width = grad.shape
+def between(x, mine, grad_near, grad_far, att, lse, qt, scale, weights, vec, blk_size, per):
+    own, width = x.shape
     head = width // HEADS
-    hidden_width = (weights.shape[0] - width) // 2
-    block = min(512, own)
-    rows = lambda i: (i, 0)
-    lanes = lambda i: (0, 0, i)
-    tall = lambda i: (0, i, 0)
-    slots = (blk_size, weights.shape[0] // (blk_size * per), -(-per // 16) * 16, width)
-    return pl.pallas_call(
-        functools.partial(middle_kernel, per),
+    hidden_width = (weights.shape[0] - 4 * width) // 2
+    block = min(512, own // 2)
+    half = own // 2 // block
+    rows = lambda i, m: (i, 0)
+    lanes = lambda i, m: (0, 0, i)
+    tall = lambda i, m: (0, i, 0)
+    slots = (blk_size, (weights.shape[0] - 3 * width) // (blk_size * per), -(-per // 16) * 16, width)
+    grid_spec = pltpu.PrefetchScalarGridSpec(
+        num_scalar_prefetch=1,
         grid=(own // block,),
         in_specs=[
             pl.BlockSpec((block, width), rows),
-            pl.BlockSpec((block, width), rows),
+            pl.BlockSpec((1, block, width), lambda i, m: (m[0], jnp.minimum(i, half - 1), 0)),
+            pl.BlockSpec((1, block, width), lambda i, m: (m[0], jnp.maximum(i - half, 0), 0)),
             pl.BlockSpec((HEADS, head, block), lanes),
             pl.BlockSpec((HEADS, 8, block), lanes),
             pl.BlockSpec((HEADS, head, block), lanes),
+            whole(*scale.shape),
             whole(*weights.shape),
             whole(*vec.shape),
         ],
@@ -451,34 +576,42 @@
             pl.BlockSpec((block, width), rows),
             pl.BlockSpec((block, width), rows),
             pl.BlockSpec((HEADS, block, 128), tall),
-            pl.BlockSpec((HEADS, block, 128), tall),
+            pl.BlockSpec((HEADS, block, 4 * head), tall),
             pl.BlockSpec((HEADS, head, block), lanes),
+            pl.BlockSpec((HEADS, head, block), lanes),
+            pl.BlockSpec((1, HEADS * 8, 128), lambda i, m: (i, 0, 0)),
             whole(*slots),
             whole(16, width),
         ],
+        scratch_shapes=[
+            pltpu.VMEM((width, width), F32), pltpu.VMEM((width, hidden_width), F32), pltpu.VMEM((width, hidden_width), F32),
+        ],
+    )
+    return pl.pallas_call(
+        functools.partial(middle_kernel, per),
+        grid_spec=grid_spec,
         out_shape=[
             jax.ShapeDtypeStruct((own, width), BF),
             jax.ShapeDtypeStruct((own, width), F32),
             jax.ShapeDtypeStruct((HEADS, own, 128), BF),
-            jax.ShapeDtypeStruct((HEADS, own, 128), BF),
+            jax.ShapeDtypeStruct((HEADS, own, 4 * head), F8),
             jax.ShapeDtypeStruct((HEADS, head, own), BF),
+            jax.ShapeDtypeStruct((HEADS, head, own), BF),
+            jax.ShapeDtypeStruct((own // block, HEADS * 8, 128), F32),
             jax.ShapeDtypeStruct(slots, BF),
             jax.ShapeDtypeStruct((16, width), F32),
         ],
-        scratch_shapes=[
-            pltpu.VMEM((width, width), F32), pltpu.VMEM((width, hidden_width), F32), pltpu.VMEM((width, hidden_width), F32),
-        ],
         compiler_params=params(),
         name="between",
-    )(x, grad, att, lse, qt, weights, vec)
+    )(mine, x, grad_near, grad_far, att, lse, qt, scale, weights, vec)
 
 
 def back_kernel(
     ctx_size, blk_size, per,
-    qa_hbm, doa_hbm, qt_hbm, dot_hbm, kta_hbm, vta_hbm, kn_hbm, ln_hbm, x_hbm, gmid_hbm, out_hbm, late_hbm,
-    gvec_in, w_ref, vec_ref,
+    qa_hbm, do8_hbm, qs_hbm, dot_hbm, kta_hbm, v8_hbm, kn_hbm, ln_hbm, x_hbm, gmid_hbm, out_hbm, late_hbm,
+    unscale_ref, gvec_in, w_ref, vec_ref,
     grad_ref, out_ref, gw_ref, gvec_ref,
-    qa, doa, qt, dot_t, kta, vta, kn, ln, x, gmid, made,
+    qa, do8, qs, dot_t, kta, v8, kn, ln, x, gmid, made,
     dq_sum, dk_sum, dv_sum, gq, gk, gv, part, part_out, part_in, wqt,
     late_own, late_one, late_pass, late_two, late_sum, late_three,
     early, early_one, early_pass, early_two, early_sum, early_three,
@@ -509,7 +642,7 @@
     local = pltpu.make_async_copy
 
     def head_loads(h):
-        pairs = ((qa_hbm, qa), (doa_hbm, doa), (qt_hbm, qt), (dot_hbm, dot_t), (kta_hbm, kta), (vta_hbm, vta), (kn_hbm, kn))
+        pairs = ((qa_hbm, qa), (do8_hbm, do8), (qs_hbm, qs), (dot_hbm, dot_t), (kta_hbm, kta), (v8_hbm, v8), (kn_hbm, kn))
         return [local(a.at[h], b.at[h], head_sem.at[i, h]) for i, (a, b) in enumerate(pairs)]
 
     loads = [
@@ -605,17 +738,21 @@
             else:
                 part_out[half] = both.astype(BF)
                 part_send(half).start()
-        rows = slice(half * length, (half + 1) * length)
-        gq[...] += dot_tn(ln[rows, :], query_grads(rows))
-
-    def query_grads(rows):
-        return jnp.concatenate([(dq_sum[h, rows, :] * (1.0 / math.sqrt(head))).astype(BF) for h in range(HEADS)], 1)
+        for c in range(chunks):
+            low = half * length + c * size
+            gq[...] += dot_tn(ln[low : low + size, :], query_grads(low))
+
+    def query_grads(low):
+        unscale = unscale_ref[low // size] * (1.0 / math.sqrt(head))
+        return jnp.concatenate(
+            [(dq_sum[h, low : low + size, :] * unscale[h * 8 : h * 8 + 1, :]).astype(BF) for h in range(HEADS)], 1
+        )
 
     def rows_back(half):
         for c in range(chunks):
             rows = slice(half * length + c * size, half * length + (c + 1) * size)
             lanes = slice(c * size, (c + 1) * size)
-            grad_ln = dot(query_grads(rows), wqt[...]) + (part[half, :, lanes] + part_in[half, :, lanes].astype(F32)).T
+            grad_ln = dot(query_grads(half * length + c * size), wqt[...]) + (part[half, :, lanes] + part_in[half, :, lanes].astype(F32)).T
             normed, inverse = normalize(x[rows, :].astype(F32))
             vec_own[0:1, :] += jnp.sum(grad_ln * normed, 0, keepdims=True)
             vec_own[1:2, :] += jnp.sum(grad_ln, 0, keepdims=True)
@@ -667,15 +804,15 @@
         first_half = jnp.logical_or(block == 0, block == 3)
         where = pl.ds(pl.multiple_of(jnp.where(first_half, 0, length), length), length)
         base = jnp.where(block < 2, length, 0)
-        queries, grads = qa[h, where, :AUG], doa[h, where, :AUG]
-        queries_t, grads_t = qt[h, :, where], dot_t[h, :, where]
+        queries, grads = qa[h, where, :AUG], do8[h, where, :]
+        queries_t, grads_t = qs[h, :, where], dot_t[h, :, where]
         parts = []
         for offset in (0, own):
             for low in range(0, length, tk):
                 parts.append(pl.ds(pl.multiple_of(base + (offset + low), tk), tk))
 
         def pair(part):
-            return dot(queries, kta[h, :, part]), dot(grads, vta[h, :, part])
+            return dot(queries, kta[h, :, part]), dot(grads, v8[h, :, part])
 
         grad_query = jnp.zeros((length, 128), F32)
         level, change = pair(parts[0])
@@ -769,7 +906,7 @@
         grad_send(1, c, size).wait()
 
 
-def back(ctx_size, blk_size, per, owners, qa, doa, qt, dot_t, kta, vta, kn, ln, rows_all, gmid, out, late, gvec, w_input, vec):
+def back(ctx_size, blk_size, per, owners, qa, do8, qs, dot_t, kta, v8, kn, ln, rows_all, gmid, out, late, unscale, gvec, w_input, vec):
     own, width = gmid.shape
     head = width // HEADS
     total = 2 * own
@@ -786,7 +923,7 @@
     some = lambda count: dma((max(count, 1),))
     return pl.pallas_call(
         functools.partial(back_kernel, ctx_size, blk_size, per),
-        in_specs=[place] * 12 + [vmem] * 3,
+        in_specs=[place] * 12 + [vmem] * 4,
         out_specs=[place, place, vmem, vmem],
         out_shape=[
             jax.ShapeDtypeStruct((2, length, width), BF),
@@ -795,8 +932,8 @@
             jax.ShapeDtypeStruct((16, width), F32),
         ],
         scratch_shapes=[
-            low(HEADS, own, 128), low(HEADS, own, 128), low(HEADS, head, own), low(HEADS, head, own),
-            low(HEADS, AUG, total), low(HEADS, AUG, total), low(HEADS, total, 128), low(total, width),
+            low(HEADS, own, 128), pltpu.VMEM((HEADS, own, 4 * head), F8), low(HEADS, head, own), low(HEADS, head, own),
+            low(HEADS, AUG, total), pltpu.VMEM((HEADS, 4 * head, total), F8), low(HEADS, total, 128), low(total, width),
             low(own, width), single(own, width), low(own, width),
             single(HEADS, own, 128), single(HEADS, head, total), single(HEADS, head, total),
             single(width, HEADS * 128), single(width, width), single(width, width),
@@ -814,48 +951,27 @@
         ],
         compiler_params=params(collective_id=2, has_side_effects=True),
         name="back",
-    )(qa, doa, qt, dot_t, kta, vta, kn, ln, rows_all, gmid, out, late, gvec, w_input, vec)
+    )(qa, do8, qs, dot_t, kta, v8, kn, ln, rows_all, gmid, out, late, unscale, gvec, w_input, vec)
 
 
 def per_device(ctx_size, blk_size, layer_in, matrices, vectors, out_grad):
     seq_count, local_rows, width = layer_in.shape
     per, entries = matrices.shape[0], vectors.shape[0]
-    slots = -(-per // 16) * 16
-    devices = ctx_size * blk_size
     flat = lax.axis_index("ctx") * blk_size + lax.axis_index("blk")
     mine = lax.axis_index("blk") // (blk_size // seq_count)
     far = [(b, (b + blk_size // 2) % blk_size) for b in range(blk_size)]
-    in_rows = 3 * width
-    owners = max(-(-in_rows // (per * blk_size)), -(-2 * width // (entries * blk_size)))
-
-    block = jnp.concatenate(
-        [
-            jnp.pad(matrices, ((0, slots - per), (0, 0))),
-            jnp.pad(vectors.reshape(1, entries), ((0, 15), (0, width - entries))),
-        ],
-        0,
+    owners = 3 * width // (per * blk_size)
+    weights = lax.all_gather(matrices, ("ctx", "blk"), axis=0, tiled=True)
+    rows, ln, qt, kn, kta, vta, vec = start(ctx_size, blk_size, layer_in, matrices, vectors, owners)
+
+    out_grad, qt = lax.optimization_barrier((out_grad, qt))
+    grad_far = lax.ppermute(out_grad, "blk", far)
+    att, lse, v8, scale = attend(qt, kn, kta, vta)
+    out, gmid, qa, do8, dot_t, qs, unscale, late, gvec = between(
+        rows, jnp.reshape(mine, (1,)).astype(jnp.int32), out_grad, grad_far, att, lse, qt, scale, weights, vec, blk_size, per
     )
-    rows_all, first = exchange(ctx_size, blk_size, layer_in, block, owners)
-    w_input = first[:, :per].reshape(-1, width)[:in_rows]
-    vec_in = first[:, slots, :entries].reshape(-1)[: 2 * width].reshape(2, width).astype(F32)
-    vec_in = jnp.pad(vec_in, ((0, 6), (0, 0)))
-
-    every = lax.all_gather(block, ("ctx", "blk"), axis=0)
-    weights = every[:, :per].reshape(-1, width)[in_rows:]
-    vec = every[:, slots, :entries].reshape(-1, width).astype(F32)
-    vec = jnp.pad(vec, ((0, 16 - vec.shape[0]), (0, 0)))
-
-    rows_all, out_grad = lax.optimization_barrier((rows_all, out_grad))
-    kept = lax.dynamic_index_in_dim(out_grad, mine, 0, keepdims=False)
-    sent = lax.dynamic_index_in_dim(out_grad, 1 - mine, 0, keepdims=False)
-    grad = jnp.concatenate([kept, lax.ppermute(sent, "blk", far)], 0)
-
-    own = 2 * local_rows
-    ln, qt, kn, kta, vta = prep(rows_all, own, w_input, vec_in)
-    att, lse = attend(qt, kn, kta, vta)
-    out, gmid, qa, doa, dot_t, late, gvec = between(rows_all, grad, att, lse, qt, weights, vec, blk_size, per)
     layer_grad, layer_out, matrices_grad, vecs = back(
-        ctx_size, blk_size, per, owners, qa, doa, qt, dot_t, kta, vta, kn, ln, rows_all, gmid, out, late, gvec, w_input, vec_in
+        ctx_size, blk_size, per, owners, qa, do8, qs, dot_t, kta, v8, kn, ln, rows, gmid, out, late, unscale, gvec, weights, vec
     )
     vectors_grad = lax.dynamic_slice_in_dim(vecs.reshape(-1), flat * entries, entries)
     return layer_out, layer_grad, matrices_grad[:per], vectors_grad

time: 222 us -> 205 us (0.923)
  Pallas kernels: 192 us -> 183 us
  local copies, waits for them, and re-layouts: 10.9 us -> 6.25 us
  other arithmetic: 3.7 us -> 0 us
    pallas_call x1, Pallas kernels: 101 us -> 95.5 us  [back(): pl.pallas_call(functools.partial(back_kernel, ctx_size, blk_size, per), i...]
    pallas_call x3 -> x2, Pallas kernels: 58.3 us -> 53.2 us  [the longest x1 29.5 us: start(): pl.pallas_call(functools.partial(start_kernel, ctx_size, blk_size, per),...]
    slice x5 -> x0, local copies, waits for them, and re-layouts: 4.07 us -> none  [the longest x1 2.36 us: per_device(): weights = every[:, :per].reshape(-1, width)[in_rows:]]
    concatenate x2 -> x0, other arithmetic: 2.48 us -> none  [the longest x1 1.44 us: per_device(): jnp.concatenate([jnp.pad(matrices, ((0, slots - per), (0, 0))), jnp.pad(v...]
  transfers between devices with their start and end apart: 2 -> 2, of which waited for: 0 -> 0; matrix products, arithmetic and copies ran while one was open for 2% -> 0% of each run, Pallas kernels for 31% -> 31%
where the time goes in v4:
time: 205 us; the launch traced here: 204 us
  Pallas kernels  183 us (89%)
  between operations  14.1 us (7%)
  local copies, waits for them, and re-layouts  6.25 us (3%)
    pallas_call x1, Pallas kernels, back(): pl.pallas_call(functools.partial(back_kernel, ctx_size, blk_size, per), i...  95.5 us
    pallas_call x1, Pallas kernels, attend(): pl.pallas_call(attend_kernel, grid=(HEADS,), in_specs=[per_head(head, own...  34.1 us
    pallas_call x1, Pallas kernels, start(): pl.pallas_call(functools.partial(start_kernel, ctx_size, blk_size, per),...  29.5 us
    pallas_call x1, Pallas kernels, between(): pl.pallas_call(functools.partial(middle_kernel, per), grid_spec=grid_spec...  23.7 us
    unnamed x10, local copies, waits for them, and re-layouts  5.66 us
  transfers between devices with their start and end apart: 2, of which 0 were waited for; matrix products, arithmetic and copies ran while one was open for 0% of the time, Pallas kernels for 31%

profile of v4, /device:TPU:0, one launch (start us, length us, event | category | flops | bytes accessed | tf_op | source)
XLA Modules:
  0.0 204.4 jit_solution(16211326560442636228)
XLA Ops:
  7.2 0.0 all-gather.2.cloned.1.call-start
  7.2 0.7 all-gather.2.cloned.1.call-update
  7.9 29.5 %start.1 = (bf16[2048,256]{1,0:T(8,128)(2,1)}, bf16[4096,256]{1,0:T(8,128)(2,1)}, bf16[4,64,2048]{2,1,0:T(8,128)(2,1)}, bf16[4,4096,128]{2,1,0:T(8,128)(2,1)}, b...) custom-call(bf16[2,1024,256]{2,1,0:T(8,128)(2,1)} %x_hbm.1, bf16[96,256]{1,0:T(8,128)(2,1)} %w_hbm.1, ...), custom_call_target="tpu_custom_call" | custom-call | tf_op jit(solution)/shard_map/start/pallas_call | solution.py:314
  37.4 0.6 collective-permute-start
  38.0 34.1 %attend.1 = (f32[4,64,2048]{2,1,0:T(8,128)}, f32[4,8,2048]{2,1,0:T(8,128)}, f8e4m3fn[4,256,4096]{2,1,0:T(32,128)(4,1)}, f32[4,8,128]{2,1,0:T(8,128)}) custom-call(bf16[4,64,2048]{2,1,0:T(8,128)(2,1)} %get-tuple-element.33.qt_ref, bf16[4,4096,128]{2,1,0:T(8,128)(2,1)} %get-tuple-element.34.kn_ref.kn_hbm, ...), custom_call_target="tpu_custom_call" | custom-call | tf_op jit(solution)/shard_map/attend/pallas_call | solution.py:416
  72.1 0.0 collective-permute-done.far_ref
  72.1 0.0 copy-start.1
  72.1 0.0 all-gather.2.cloned.1.call-done.w_ref
  72.2 0.9 copy-done.1
  73.1 23.7 %between.1 = (bf16[2048,256]{1,0:T(8,128)(2,1)}, f32[2048,256]{1,0:T(8,128)}, bf16[4,2048,128]{2,1,0:T(8,128)(2,1)}, f8e4m3fn[4,2048,256]{2,1,0:T(32,128)(4,1)},...) custom-call(s32[1]{0:T(128)} %bitcast.mine_ref, ...), custom_call_target="tpu_custom_call" | custom-call | tf_op jit(solution)/shard_map/between/pallas_call | solution.py:590
  96.8 95.5 %back.1 = (bf16[2,1024,256]{2,1,0:T(8,128)(2,1)}, bf16[2,1024,256]{2,1,0:T(8,128)(2,1)}, f32[96,256]{1,0:T(8,128)}, f32[16,256]{1,0:T(8,128)}) custom-call(bf16[4,2048,128]{2,1,0:T(8,128)(2,1)} %get-tuple-element.41.qa_hbm, f8e4m3fn[4,2048,256]{2,1,0:T(32,128)(4,1)} %get-tuple-element.42.do8_hbm, bf16[4,64,2048]{2,1,0:T(8,128)(2,1)} %get-tuple-element.43.qs_hbm, ...), custom_call_target="tpu_custom_call" | custom-call | tf_op jit(solution)/shard_map/back/pallas_call | solution.py:924
  192.3 0.0 copy-start
  192.3 0.8 copy.8
  193.1 0.6 dynamic_slice.3
  193.7 0.0 copy-start.2
  193.7 2.3 %copy.12 = bf16[2,1024,256]{2,1,0:T(8,128)(2,1)} copy(bf16[2,1024,256]{2,1,0:T(8,128)(2,1)} %get-tuple-element.60) | data formatting | bytes 2097152
  196.0 0.0 copy-done
  196.0 1.0 copy.13
  196.9 0.0 copy-done.2
  196.9 0.6 copy.14
Async XLA Ops:
  7.2 65.0 %all-gather.2.cloned.1.call-start = ((), (), s32[]{:S(2)}) async-start(), calls=%async_computation | async-start | bytes 1622016 | tf_op jit(solution)/shard_map/all_gather | solution.py:964
  37.4 34.7 %collective-permute-start = (bf16[2,1024,256]{2,1,0:T(8,128)(2,1)}, bf16[2,1024,256]{2,1,0:T(8,128)(2,1)S(1)}, u32[]{:S(2)}, u32[]{:S(2)}) collective-permute-start(bf16[2,1024,256]{2,1,0:T(8,128)(2,1)} %near_ref), channel_id=1, source_target_pairs={{0,2},{1,3},{2,0},{3,1},{4,6},{5,7},{6,4},{7,5},{8,10},{9,11},{10,... | collective-permute-start | bytes 3145736 | tf_op jit(solution)/shard_map/ppermute | solution.py:968
  72.1 1.0 copy-start.1
  192.3 3.7 %copy-start = (bf16[2,1024,256]{2,1,0:T(8,128)(2,1)S(1)}, bf16[2,1024,256]{2,1,0:T(8,128)(2,1)}, u32[]{:S(2)}) copy-start(bf16[2,1024,256]{2,1,0:T(8,128)(2,1)} %get-tuple-element.61) | copy-start | bytes 3145732
  193.7 3.3 %copy-start.2 = (f32[96,256]{1,0:T(8,128)S(1)}, f32[96,256]{1,0:T(8,128)}, u32[]{:S(2)}) copy-start(f32[96,256]{1,0:T(8,128)} %get-tuple-element.62) | copy-start | bytes 294916
Sparse Core Ops, SparseCore 0:
  10.9 59.9 all-gather.1

commit v5 on v4

--- a/solution.py
+++ b/solution.py
@@ -16,8 +16,6 @@
 SAFE_BOUND = 90.0
 BF = jnp.bfloat16
 F32 = jnp.float32
-F8 = jnp.float8_e4m3fn
-PIECES = (256.0, 16.0, 1.0, 0.0625)
 NT = (((1,), (1,)), ((), ()))
 TN = (((0,), (0,)), ((), ()))
 
@@ -267,7 +265,7 @@
 
         @pl.when(lax.rem(quarter, 2) == 0)
         def _():
-            queries = dot_nt(wt[0:width, :], low) * (LOG2E / math.sqrt(head))
+            queries = dot_nt(wt[0:width, :], low)
             for h in range(HEADS):
                 qt[h, :, rows] = queries[h * head : (h + 1) * head, :].astype(BF)
 
@@ -331,29 +329,10 @@
     )(layer_in, matrices, vectors.reshape(1, entries))
 
 
-def scale_of(values):
-    peak = jnp.max(jnp.max(jnp.abs(values), 0, keepdims=True), 1, keepdims=True)
-    return jnp.exp2(4.0 - jnp.ceil(jnp.log2(jnp.clip(peak, 1e-30, 1e30))))
-
-
-def two_parts(values):
-    high = values.astype(F8).astype(F32)
-    return high, (values - high).astype(F8).astype(F32)
-
-
-def attend_kernel(qt_ref, kn_ref, kta_ref, vta_ref, att_ref, lse_ref, v8_ref, scale_ref):
+def attend_kernel(qt_ref, kn_ref, kta_ref, vta_ref, att_ref, lse_ref):
     head, own = qt_ref.shape[1:]
     total = kn_ref.shape[1]
-    values = vta_ref[0, :head, :].astype(F32)
-    scale = scale_of(values)
-    scale_ref[0] = jnp.broadcast_to(scale, (8, 128))
-    high, low = two_parts(values * scale)
-    place = lax.broadcasted_iota(jnp.int32, (head, total), 0)
-    ones = jnp.zeros((head, total), F32)
-    for index, piece in enumerate(PIECES):
-        ones = jnp.where(place == index, piece, ones)
-    for index, rows in enumerate((high, high, low, ones)):
-        v8_ref[0, index * head : (index + 1) * head, :] = rows.astype(F8)
+    to_log2 = LOG2E / math.sqrt(head)
     tq = min(1024, own)
     tk = min(256, total)
     count = total // tk
@@ -362,7 +341,7 @@
         rows = rows.astype(F32)
         return jnp.max(jnp.sum(rows * rows, 0, keepdims=True))
 
-    bound = longest(qt_ref[0]) * longest(kta_ref[0, :head, :])
+    bound = longest(qt_ref[0]) * longest(kta_ref[0, :head, :]) * (to_log2 * to_log2)
 
     def finish(where, summed, top):
         totals = summed[head : head + 1, :]
@@ -382,7 +361,7 @@
             summed = jnp.zeros((AUG, tq), F32)
             now = scores(queries, 0)
             for j in range(count):
-                expo = jnp.exp2(now).astype(BF)
+                expo = jnp.exp2(now * to_log2).astype(BF)
                 if j + 1 < count:
                     now = scores(queries, j + 1)
                 summed = summed + dot(vta_ref[0, :, j * tk : (j + 1) * tk], expo)
@@ -398,7 +377,7 @@
             def absorb(j, carry):
                 summed, top = carry
                 part = pl.ds(pl.multiple_of(j * tk, tk), tk)
-                now = dot(kn_ref[0, part, :head], queries)
+                now = dot(kn_ref[0, part, :head], queries) * to_log2
                 higher = jnp.maximum(top, jnp.max(now, 0, keepdims=True))
                 expo = jnp.exp2(now - higher).astype(BF)
                 summed = summed * jnp.exp2(top - higher) + dot(vta_ref[0, :, part], expo)
@@ -417,12 +396,10 @@
         attend_kernel,
         grid=(HEADS,),
         in_specs=[per_head(head, own), per_head(total, 128), per_head(AUG, total), per_head(AUG, total)],
-        out_specs=[per_head(head, own), per_head(8, own), per_head(4 * head, total), per_head(8, 128)],
+        out_specs=[per_head(head, own), per_head(8, own)],
         out_shape=[
             jax.ShapeDtypeStruct((HEADS, head, own), F32),
             jax.ShapeDtypeStruct((HEADS, 8, own), F32),
-            jax.ShapeDtypeStruct((HEADS, 4 * head, total), F8),
-            jax.ShapeDtypeStruct((HEADS, 8, 128), F32),
         ],
         compiler_params=params(),
         name="attend",
@@ -430,16 +407,8 @@
 
 
 def gelu_both(value):
-    root = math.sqrt(2.0 * math.pi)
-    density = jnp.exp2(value * value * (-0.5 * LOG2E) - math.log2(root))
-    place = pl.reciprocal((0.3275911 / math.sqrt(2.0)) * jnp.abs(value) + 1.0, approx=True)
-    half = 0.5 * root
-    series = (1.061405429 * half) * place - 1.453152027 * half
-    series = series * place + 1.421413741 * half
-    series = series * place - 0.284496736 * half
-    series = series * place + 0.254829592 * half
-    tail = series * place * density
-    below = jnp.where(value >= 0.0, 1.0 - tail, tail)
+    below = 0.5 + 0.5 * lax.erf(value * math.sqrt(0.5))
+    density = jnp.exp2(value * value * (-0.5 * LOG2E) - math.log2(math.sqrt(2.0 * math.pi)))
     return value * below, below + value * density
 
 
@@ -453,8 +422,8 @@
 
 
 def middle_kernel(
-    per, mine_ref, x_ref, near_ref, far_ref, att_ref, lse_ref, qt_ref, scale_ref, w_ref, vec_ref,
-    out_ref, gmid_ref, qa_ref, do8_ref, dot_ref, qs_ref, unscale_ref, late_ref, gvec_ref, gwo_ref, gup_ref, gdown_ref,
+    per, mine_ref, x_ref, near_ref, far_ref, att_ref, lse_ref, qt_ref, w_ref, vec_ref,
+    out_ref, gmid_ref, qa_ref, doa_ref, dot_ref, late_ref, gvec_ref, gwo_ref, gup_ref, gdown_ref,
 ):
     width = x_ref.shape[1]
     head = width // HEADS
@@ -507,29 +476,17 @@
     gwo_ref[...] += dot(att_low, branch)
     grad_att = dot_nt(wo, branch).astype(BF)
     spare = jnp.zeros((128 - AUG, rows), F32)
-    place = lax.broadcasted_iota(jnp.int32, (head, rows), 0)
+    from_log2 = math.sqrt(head) * LN2
     for h in range(HEADS):
         mine = slice(h * head, (h + 1) * head)
         grad_head = grad_att[mine, :]
         dot_ref[h] = grad_head
         grad_head = grad_head.astype(F32)
         delta = jnp.sum(grad_head * att[mine, :], 0, keepdims=True)
-        scale = scale_of(grad_head)
-        both = scale * scale_ref[h, 0:1, 0:1]
-        high, low = two_parts(grad_head * scale)
-        left = -delta * both
-        folded = jnp.zeros((head, rows), F32)
-        for index, piece in enumerate(PIECES):
-            part = (left * (1.0 / piece)).astype(F8).astype(F32)
-            left = left - part * piece
-            folded = jnp.where(place == index, part, folded)
-        do8_ref[h, :, : 2 * head] = jnp.concatenate([high, low], 0).T.astype(F8)
-        do8_ref[h, :, 2 * head :] = jnp.concatenate([high, folded], 0).T.astype(F8)
-        unscale_ref[0, h * 8 : (h + 1) * 8, :] = jnp.broadcast_to(1.0 / both, (8, 128))
-        queries = qt_ref[h].astype(F32)
-        qs_ref[h] = (queries / both).astype(BF)
-        level = lse_ref[h, 0:1, :]
-        wide = jnp.concatenate([queries, split_rows(-level, AUG - head), spare], 0)
+        wide = jnp.concatenate([grad_head, split_rows(-delta, AUG - head), spare], 0)
+        doa_ref[h] = wide.T.astype(BF)
+        level = lse_ref[h, 0:1, :] * from_log2
+        wide = jnp.concatenate([qt_ref[h].astype(F32), split_rows(-level, AUG - head), spare], 0)
         qa_ref[h] = wide.T.astype(BF)
 
     @pl.when(pl.program_id(0) == pl.num_programs(0) - 1)
@@ -548,7 +505,7 @@
         slots_ref[slot % blk_size, slot // blk_size] = piece.astype(BF)
 
 
-def between(x, mine, grad_near, grad_far, att, lse, qt, scale, weights, vec, blk_size, per):
+def between(x, mine, grad_near, grad_far, att, lse, qt, weights, vec, blk_size, per):
     own, width = x.shape
     head = width // HEADS
     hidden_width = (weights.shape[0] - 4 * width) // 2
@@ -568,7 +525,6 @@
             pl.BlockSpec((HEADS, head, block), lanes),
             pl.BlockSpec((HEADS, 8, block), lanes),
             pl.BlockSpec((HEADS, head, block), lanes),
-            whole(*scale.shape),
             whole(*weights.shape),
             whole(*vec.shape),
         ],
@@ -576,10 +532,8 @@
             pl.BlockSpec((block, width), rows),
             pl.BlockSpec((block, width), rows),
             pl.BlockSpec((HEADS, block, 128), tall),
-            pl.BlockSpec((HEADS, block, 4 * head), tall),
+            pl.BlockSpec((HEADS, block, 128), tall),
             pl.BlockSpec((HEADS, head, block), lanes),
-            pl.BlockSpec((HEADS, head, block), lanes),
-            pl.BlockSpec((1, HEADS * 8, 128), lambda i, m: (i, 0, 0)),
             whole(*slots),
             whole(16, width),
         ],
@@ -594,24 +548,22 @@
             jax.ShapeDtypeStruct((own, width), BF),
             jax.ShapeDtypeStruct((own, width), F32),
             jax.ShapeDtypeStruct((HEADS, own, 128), BF),
-            jax.ShapeDtypeStruct((HEADS, own, 4 * head), F8),
+            jax.ShapeDtypeStruct((HEADS, own, 128), BF),
             jax.ShapeDtypeStruct((HEADS, head, own), BF),
-            jax.ShapeDtypeStruct((HEADS, head, own), BF),
-            jax.ShapeDtypeStruct((own // block, HEADS * 8, 128), F32),
             jax.ShapeDtypeStruct(slots, BF),
             jax.ShapeDtypeStruct((16, width), F32),
         ],
         compiler_params=params(),
         name="between",
-    )(mine, x, grad_near, grad_far, att, lse, qt, scale, weights, vec)
+    )(mine, x, grad_near, grad_far, att, lse, qt, weights, vec)
 
 
 def back_kernel(
     ctx_size, blk_size, per,
-    qa_hbm, do8_hbm, qs_hbm, dot_hbm, kta_hbm, v8_hbm, kn_hbm, ln_hbm, x_hbm, gmid_hbm, out_hbm, late_hbm,
-    unscale_ref, gvec_in, w_ref, vec_ref,
+    qa_hbm, doa_hbm, qt_hbm, dot_hbm, kta_hbm, vta_hbm, kn_hbm, ln_hbm, x_hbm, gmid_hbm, out_hbm, late_hbm,
+    gvec_in, w_ref, vec_ref,
     grad_ref, out_ref, gw_ref, gvec_ref,
-    qa, do8, qs, dot_t, kta, v8, kn, ln, x, gmid, made,
+    qa, doa, qt, dot_t, kta, vta, kn, ln, x, gmid, made,
     dq_sum, dk_sum, dv_sum, gq, gk, gv, part, part_out, part_in, wqt,
     late_own, late_one, late_pass, late_two, late_sum, late_three,
     early, early_one, early_pass, early_two, early_sum, early_three,
@@ -642,7 +594,7 @@
     local = pltpu.make_async_copy
 
     def head_loads(h):
-        pairs = ((qa_hbm, qa), (do8_hbm, do8), (qs_hbm, qs), (dot_hbm, dot_t), (kta_hbm, kta), (v8_hbm, v8), (kn_hbm, kn))
+        pairs = ((qa_hbm, qa), (doa_hbm, doa), (qt_hbm, qt), (dot_hbm, dot_t), (kta_hbm, kta), (vta_hbm, vta), (kn_hbm, kn))
         return [local(a.at[h], b.at[h], head_sem.at[i, h]) for i, (a, b) in enumerate(pairs)]
 
     loads = [
@@ -705,9 +657,8 @@
     ]
 
     greet([to_near, to_far] + [(other, blk) for other in others] + [(group * owners + peer, far) for peer in peers])
-    for h in range(HEADS):
-        for load in head_loads(h):
-            load.start()
+    for load in head_loads(0):
+        load.start()
     for copy in late_first + late_loads + [out_send, out_keep] + loads:
         copy.start()
     dq_sum[...] = jnp.zeros_like(dq_sum)
@@ -719,34 +670,32 @@
     vec_own[...] = gvec_in[...]
 
     tk = min(256, length)
+    inverse_root = 1.0 / math.sqrt(head)
     wk, wv = w_ref[width : 2 * width, :], w_ref[2 * width : 3 * width, :]
     gain = vec_ref[0:1, :]
     size = min(512, length)
     chunks = length // size
 
     def terms(half):
-        for core_rows in range(2):
+        for core_rows in (1, 0):
             low = core_rows * own + half * length
             rows = slice(low, low + length)
-            dk = (dk_sum[:, :, rows] * LN2).astype(BF).reshape(width, length)
+            dk = (dk_sum[:, :, rows] * inverse_root).astype(BF).reshape(width, length)
             dv = dv_sum[:, :, rows].astype(BF).reshape(width, length)
+            both = dot(wk, dk) + dot(wv, dv)
+            if core_rows:
+                part_out[half] = both.astype(BF)
+                part_send(half).start()
+            else:
+                part[half] = both
             gk[...] += dot(dk, ln[rows, :])
             gv[...] += dot(dv, ln[rows, :])
-            both = dot(wk, dk) + dot(wv, dv)
-            if core_rows == 0:
-                part[half] = both
-            else:
-                part_out[half] = both.astype(BF)
-                part_send(half).start()
         for c in range(chunks):
             low = half * length + c * size
             gq[...] += dot_tn(ln[low : low + size, :], query_grads(low))
 
     def query_grads(low):
-        unscale = unscale_ref[low // size] * (1.0 / math.sqrt(head))
-        return jnp.concatenate(
-            [(dq_sum[h, low : low + size, :] * unscale[h * 8 : h * 8 + 1, :]).astype(BF) for h in range(HEADS)], 1
-        )
+        return jnp.concatenate([(dq_sum[h, low : low + size, :] * inverse_root).astype(BF) for h in range(HEADS)], 1)
 
     def rows_back(half):
         for c in range(chunks):
@@ -768,6 +717,11 @@
             for load in head_loads(h):
                 load.wait()
 
+        @pl.when(t < HEADS - 1)
+        def _():
+            for load in head_loads(t + 1):
+                load.start()
+
         @pl.when(t == 2)
         def _():
             for y in range(2):
@@ -804,20 +758,20 @@
         first_half = jnp.logical_or(block == 0, block == 3)
         where = pl.ds(pl.multiple_of(jnp.where(first_half, 0, length), length), length)
         base = jnp.where(block < 2, length, 0)
-        queries, grads = qa[h, where, :AUG], do8[h, where, :]
-        queries_t, grads_t = qs[h, :, where], dot_t[h, :, where]
+        queries, grads = qa[h, where, :AUG], doa[h, where, :AUG]
+        queries_t, grads_t = qt[h, :, where], dot_t[h, :, where]
         parts = []
         for offset in (0, own):
             for low in range(0, length, tk):
                 parts.append(pl.ds(pl.multiple_of(base + (offset + low), tk), tk))
 
         def pair(part):
-            return dot(queries, kta[h, :, part]), dot(grads, v8[h, :, part])
+            return dot(queries, kta[h, :, part]), dot(grads, vta[h, :, part])
 
         grad_query = jnp.zeros((length, 128), F32)
         level, change = pair(parts[0])
         for j, part_now in enumerate(parts):
-            probs = jnp.exp2(level)
+            probs = jnp.exp2(level * (LOG2E * inverse_root))
             probs_low = probs.astype(BF)
             grad_scores = (probs * change).astype(BF)
             if j + 1 < len(parts):
@@ -906,7 +860,7 @@
         grad_send(1, c, size).wait()
 
 
-def back(ctx_size, blk_size, per, owners, qa, do8, qs, dot_t, kta, v8, kn, ln, rows_all, gmid, out, late, unscale, gvec, w_input, vec):
+def back(ctx_size, blk_size, per, owners, qa, doa, qt, dot_t, kta, vta, kn, ln, rows_all, gmid, out, late, gvec, w_input, vec):
     own, width = gmid.shape
     head = width // HEADS
     total = 2 * own
@@ -923,7 +877,7 @@
     some = lambda count: dma((max(count, 1),))
     return pl.pallas_call(
         functools.partial(back_kernel, ctx_size, blk_size, per),
-        in_specs=[place] * 12 + [vmem] * 4,
+        in_specs=[place] * 12 + [vmem] * 3,
         out_specs=[place, place, vmem, vmem],
         out_shape=[
             jax.ShapeDtypeStruct((2, length, width), BF),
@@ -932,8 +886,8 @@
             jax.ShapeDtypeStruct((16, width), F32),
         ],
         scratch_shapes=[
-            low(HEADS, own, 128), pltpu.VMEM((HEADS, own, 4 * head), F8), low(HEADS, head, own), low(HEADS, head, own),
-            low(HEADS, AUG, total), pltpu.VMEM((HEADS, 4 * head, total), F8), low(HEADS, total, 128), low(total, width),
+            low(HEADS, own, 128), low(HEADS, own, 128), low(HEADS, head, own), low(HEADS, head, own),
+            low(HEADS, AUG, total), low(HEADS, AUG, total), low(HEADS, total, 128), low(total, width),
             low(own, width), single(own, width), low(own, width),
             single(HEADS, own, 128), single(HEADS, head, total), single(HEADS, head, total),
             single(width, HEADS * 128), single(width, width), single(width, width),
@@ -951,7 +905,7 @@
         ],
         compiler_params=params(collective_id=2, has_side_effects=True),
         name="back",
-    )(qa, do8, qs, dot_t, kta, v8, kn, ln, rows_all, gmid, out, late, unscale, gvec, w_input, vec)
+    )(qa, doa, qt, dot_t, kta, vta, kn, ln, rows_all, gmid, out, late, gvec, w_input, vec)
 
 
 def per_device(ctx_size, blk_size, layer_in, matrices, vectors, out_grad):
@@ -966,12 +920,12 @@
 
     out_grad, qt = lax.optimization_barrier((out_grad, qt))
     grad_far = lax.ppermute(out_grad, "blk", far)
-    att, lse, v8, scale = attend(qt, kn, kta, vta)
-    out, gmid, qa, do8, dot_t, qs, unscale, late, gvec = between(
-        rows, jnp.reshape(mine, (1,)).astype(jnp.int32), out_grad, grad_far, att, lse, qt, scale, weights, vec, blk_size, per
+    att, lse = attend(qt, kn, kta, vta)
+    out, gmid, qa, doa, dot_t, late, gvec = between(
+        rows, jnp.reshape(mine, (1,)).astype(jnp.int32), out_grad, grad_far, att, lse, qt, weights, vec, blk_size, per
     )
     layer_grad, layer_out, matrices_grad, vecs = back(
-        ctx_size, blk_size, per, owners, qa, do8, qs, dot_t, kta, v8, kn, ln, rows, gmid, out, late, unscale, gvec, weights, vec
+        ctx_size, blk_size, per, owners, qa, doa, qt, dot_t, kta, vta, kn, ln, rows, gmid, out, late, gvec, weights, vec
     )
     vectors_grad = lax.dynamic_slice_in_dim(vecs.reshape(-1), flat * entries, entries)
     return layer_out, layer_grad, matrices_grad[:per], vectors_grad

time: 205 us -> 205 us (level)
    pallas_call x1, Pallas kernels: 95.5 us -> 103 us  [back(): pl.pallas_call(functools.partial(back_kernel, ctx_size, blk_size, per), i...]
    pallas_call x1, Pallas kernels: 23.7 us -> 17.5 us  [between(): pl.pallas_call(functools.partial(middle_kernel, per), grid_spec=grid_spec...]
  transfers between devices with their start and end apart: 2 -> 2, of which waited for: 0 -> 0; matrix products, arithmetic and copies ran while one was open for 0% -> 0% of each run, Pallas kernels for 31% -> 30%
where the time goes in v5:
time: 205 us
  Pallas kernels  183 us (89%)
  between operations  14.1 us (7%)
  local copies, waits for them, and re-layouts  6.25 us (3%)
    pallas_call x1, Pallas kernels, back(): pl.pallas_call(functools.partial(back_kernel, ctx_size, blk_size, per), i...  103 us
    pallas_call x1, Pallas kernels, attend(): pl.pallas_call(attend_kernel, grid=(HEADS,), in_specs=[per_head(head, own...  33.1 us
    pallas_call x1, Pallas kernels, start(): pl.pallas_call(functools.partial(start_kernel, ctx_size, blk_size, per),...  29.3 us
    pallas_call x1, Pallas kernels, between(): pl.pallas_call(functools.partial(middle_kernel, per), grid_spec=grid_spec...  17.5 us
    unnamed x10, local copies, waits for them, and re-layouts  5.66 us
  transfers between devices with their start and end apart: 2, of which 0 were waited for; matrix products, arithmetic and copies ran while one was open for 0% of the time, Pallas kernels for 30%

profile of v5, /device:TPU:0, one launch (start us, length us, event | category | flops | bytes accessed | tf_op | source)
XLA Modules:
  0.0 204.8 jit_solution(14132900665807897516)
XLA Ops:
  7.2 0.0 all-gather.2.cloned.1.call-start
  7.2 0.7 all-gather.2.cloned.1.call-update
  7.9 29.3 %start.1 = (bf16[2048,256]{1,0:T(8,128)(2,1)}, bf16[4096,256]{1,0:T(8,128)(2,1)}, bf16[4,64,2048]{2,1,0:T(8,128)(2,1)}, bf16[4,4096,128]{2,1,0:T(8,128)(2,1)}, b...) custom-call(bf16[2,1024,256]{2,1,0:T(8,128)(2,1)} %x_hbm.1, bf16[96,256]{1,0:T(8,128)(2,1)} %w_hbm.1, ...), custom_call_target="tpu_custom_call" | custom-call | tf_op jit(solution)/shard_map/start/pallas_call | solution.py:312
  37.3 0.6 collective-permute-start
  37.8 33.1 %attend.1 = (f32[4,64,2048]{2,1,0:T(8,128)}, f32[4,8,2048]{2,1,0:T(8,128)}) custom-call(bf16[4,64,2048]{2,1,0:T(8,128)(2,1)} %get-tuple-element.29.qt_ref.qt_hbm, bf16[4,4096,128]{2,1,0:T(8,128)(2,1)} %get-tuple-element.30.kn_ref.kn_hbm, bf16[4,80,4096]{2,1,0:T(8,128)(2,1)} %get-tuple-element.31.kta_ref.kta_hbm, ...), custom_call_target="tpu_custom_call" | custom-call | tf_op jit(solution)/shard_map/attend/pallas_call | solution.py:395
  70.9 0.0 collective-permute-done.far_ref
  70.9 0.0 copy-start.1
  70.9 0.0 all-gather.2.cloned.1.call-done.w_ref
  70.9 0.9 copy-done.1
  71.9 17.5 %between.1 = (bf16[2048,256]{1,0:T(8,128)(2,1)}, f32[2048,256]{1,0:T(8,128)}, bf16[4,2048,128]{2,1,0:T(8,128)(2,1)}, bf16[4,2048,128]{2,1,0:T(8,128)(2,1)}, bf16...) custom-call(s32[1]{0:T(128)} %bitcast.mine_ref, ...), custom_call_target="tpu_custom_call" | custom-call | tf_op jit(solution)/shard_map/between/pallas_call | solution.py:544
  89.4 103.2 %back.1 = (bf16[2,1024,256]{2,1,0:T(8,128)(2,1)}, bf16[2,1024,256]{2,1,0:T(8,128)(2,1)}, f32[96,256]{1,0:T(8,128)}, f32[16,256]{1,0:T(8,128)}) custom-call(bf16[4,2048,128]{2,1,0:T(8,128)(2,1)} %get-tuple-element.36.qa_hbm, bf16[4,2048,128]{2,1,0:T(8,128)(2,1)} %get-tuple-element.37.doa_hbm, bf16[4,64,2048]{2,1,0:T(8,128)(2,1)} %get-tuple-element.29.qt_ref.qt_hbm, ...), custom_call_target="tpu_custom_call" | custom-call | tf_op jit(solution)/shard_map/back/pallas_call | solution.py:878
  192.6 0.0 copy-start
  192.6 0.8 copy.8
  193.4 0.6 dynamic_slice.3
  194.0 0.0 copy-start.2
  194.0 2.3 %copy.12 = bf16[2,1024,256]{2,1,0:T(8,128)(2,1)} copy(bf16[2,1024,256]{2,1,0:T(8,128)(2,1)} %get-tuple-element.52) | data formatting | bytes 2097152
  196.3 0.0 copy-done
  196.3 1.0 copy.13
  197.3 0.0 copy-done.2
  197.3 0.6 copy.14
Async XLA Ops:
  7.2 63.8 %all-gather.2.cloned.1.call-start = ((), (), s32[]{:S(2)}) async-start(), calls=%async_computation | async-start | bytes 1622016 | tf_op jit(solution)/shard_map/all_gather | solution.py:918
  37.3 33.7 %collective-permute-start = (bf16[2,1024,256]{2,1,0:T(8,128)(2,1)}, bf16[2,1024,256]{2,1,0:T(8,128)(2,1)S(1)}, u32[]{:S(2)}, u32[]{:S(2)}) collective-permute-start(bf16[2,1024,256]{2,1,0:T(8,128)(2,1)} %near_ref), channel_id=1, source_target_pairs={{0,2},{1,3},{2,0},{3,1},{4,6},{5,7},{6,4},{7,5},{8,10},{9,11},{10,... | collective-permute-start | bytes 3145736 | tf_op jit(solution)/shard_map/ppermute | solution.py:922
  70.9 1.0 copy-start.1
  192.6 3.7 %copy-start = (bf16[2,1024,256]{2,1,0:T(8,128)(2,1)S(1)}, bf16[2,1024,256]{2,1,0:T(8,128)(2,1)}, u32[]{:S(2)}) copy-start(bf16[2,1024,256]{2,1,0:T(8,128)(2,1)} %get-tuple-element.53) | copy-start | bytes 3145732
  194.0 3.3 %copy-start.2 = (f32[96,256]{1,0:T(8,128)S(1)}, f32[96,256]{1,0:T(8,128)}, u32[]{:S(2)}) copy-start(f32[96,256]{1,0:T(8,128)} %get-tuple-element.54) | copy-start | bytes 294916
Sparse Core Ops, SparseCore 0:
  10.9 59.9 all-gather.1

commit v6 on v5

--- a/solution.py
+++ b/solution.py
@@ -75,7 +75,7 @@
     ctx_size, blk_size, per,
     x_hbm, w_hbm, v_ref,
     rows_out, ln_out, qt_out, kn_out, kta_out, vta_out, vec_ref,
-    x, ln, qt, kn, kta, vta, w_slots, w_all, wt, wkp, v_own, v_slots,
+    x, norms, ln, qt, kn, kta, vta, w_slots, w_all, wt, wkp, v_own, v_slots,
     x_sem, far_sent, far_got, near_sent, near_got, relay_sent, relay_got, keep_sem,
     w1_sent, w1_got, w2_sent, w2_got, w3_sent, w3_got, v1_sent, v1_got, v2_sent, v2_got, v3_sent, v3_got,
     rows_sem, out_sem,
@@ -152,6 +152,15 @@
     for copy in v_first:
         copy.start()
     v_slots[blk, ctx] = v_own[...]
+    block = min(512, length)
+
+    def norm(low):
+        normed, _ = normalize(x[pl.ds(low, block), :].astype(F32))
+        norms[pl.ds(low, block), :] = normed
+
+    own_rows.wait()
+    for low in range(0, length, block):
+        norm(low)
 
     @pl.when(group == 0)
     def _():
@@ -180,6 +189,9 @@
     for c in range(early):
         far_rows[c].wait_recv()
         relay_rows[c].start()
+    near_rows.wait_recv()
+    for low in range(2 * length, 3 * length, block):
+        norm(low)
     for copy in w_third + v_third:
         copy.wait_recv()
 
@@ -204,9 +216,6 @@
     for h in range(HEADS):
         wide = jnp.concatenate([wk[:, h * head : (h + 1) * head], jnp.zeros((width, 128 - head), F32)], 1)
         wkp[:, h * 128 : (h + 1) * 128] = wide.astype(BF)
-    own_rows.wait()
-
-    block = min(512, length)
     per_quarter = length // block
     extra = (lax.broadcasted_iota(jnp.int32, (AUG - head, block), 0) < 3).astype(F32).astype(BF)
 
@@ -232,10 +241,6 @@
     def _(index):
         quarter = lax.div(index, per_quarter)
 
-        @pl.when(index == per_quarter)
-        def _():
-            near_rows.wait_recv()
-
         @pl.when(index == 2 * per_quarter)
         def _():
             for c in range(early, chunks):
@@ -250,8 +255,12 @@
 
         base = first_row(index)
         rows = pl.ds(base, block)
-        normed, _ = normalize(x[rows, :].astype(F32))
-        low = (normed * vec_ref[0:1, :] + vec_ref[1:2, :]).astype(BF)
+
+        @pl.when(quarter >= 2)
+        def _():
+            norm(base)
+
+        low = (norms[rows, :] * vec_ref[0:1, :] + vec_ref[1:2, :]).astype(BF)
         ln[rows, :] = low
         kt = dot_nt(wt[width : 2 * width, :], low).astype(BF)
         vt = dot_nt(wt[2 * width : 3 * width, :], low).astype(BF)
@@ -315,7 +324,7 @@
         out_specs=[place] * 6 + [vmem],
         out_shape=[jax.ShapeDtypeStruct(shape, BF) for shape in shapes] + [jax.ShapeDtypeStruct((16, width), F32)],
         scratch_shapes=[
-            low(total, width), low(total, width), low(HEADS, head, own), low(HEADS, total, 128),
+            low(total, width), single(total, width), low(total, width), low(HEADS, head, own), low(HEADS, total, 128),
             low(HEADS, AUG, total), low(HEADS, AUG, total),
             low(owners * blk_size, padded, width), single(owners * blk_size * per, width),
             low(3 * width, width), low(width, HEADS * 128), single(8, 128), single(blk_size, ctx_size, 8, 128),
@@ -421,80 +430,6 @@
     return rows
 
 
-def middle_kernel(
-    per, mine_ref, x_ref, near_ref, far_ref, att_ref, lse_ref, qt_ref, w_ref, vec_ref,
-    out_ref, gmid_ref, qa_ref, doa_ref, dot_ref, late_ref, gvec_ref, gwo_ref, gup_ref, gdown_ref,
-):
-    width = x_ref.shape[1]
-    head = width // HEADS
-    rows = x_ref.shape[0]
-    hidden_width = (w_ref.shape[0] - 4 * width) // 2
-    wo = w_ref[3 * width : 4 * width, :]
-    pieces = hidden_width // width
-    down_bias = vec_ref[4 + pieces : 5 + pieces, :]
-    gain, bias = vec_ref[2:3, :], vec_ref[3:4, :]
-
-    @pl.when(pl.program_id(0) == 0)
-    def _():
-        gwo_ref[...] = jnp.zeros_like(gwo_ref)
-        gup_ref[...] = jnp.zeros_like(gup_ref)
-        gdown_ref[...] = jnp.zeros_like(gdown_ref)
-        gvec_ref[...] = jnp.zeros_like(gvec_ref)
-
-    att = att_ref[...].reshape(width, rows)
-    att_low = att.astype(BF)
-    grad = jnp.where(pl.program_id(0) < pl.num_programs(0) // 2, near_ref[0], far_ref[0])
-    gradf = grad.astype(F32)
-    grad_t = gradf.T.astype(BF)
-    middle = x_ref[...].astype(F32) + dot_tn(att_low, wo)
-    normed, inverse = normalize(middle)
-    ln_mid = (normed * gain + bias).astype(BF)
-    ln_mid_t = ln_mid.astype(F32).T.astype(BF)
-    result = middle + down_bias
-    grad_ln = jnp.zeros((rows, width), F32)
-    for p in range(pieces):
-        columns = slice(p * width, (p + 1) * width)
-        up = w_ref[(4 + p) * width : (5 + p) * width, :]
-        down = w_ref[(4 + pieces + p) * width : (5 + pieces + p) * width, :]
-        upper = dot_nt(ln_mid, up) + vec_ref[4 + p : 5 + p, :]
-        activated, slope = gelu_both(upper)
-        hidden = activated.astype(BF)
-        grad_upper = dot_nt(grad, down) * slope
-        grad_low = grad_upper.astype(BF)
-        result = result + dot(hidden, down)
-        grad_ln = grad_ln + dot(grad_low, up)
-        gdown_ref[:, columns] += dot(grad_t, hidden)
-        gup_ref[:, columns] += dot(ln_mid_t, grad_low)
-        gvec_ref[4 + p : 5 + p, :] += jnp.sum(grad_low.astype(F32), 0, keepdims=True)
-    out_ref[...] = result.astype(BF)
-    gvec_ref[2:3, :] += jnp.sum(grad_ln * normed, 0, keepdims=True)
-    gvec_ref[3:4, :] += jnp.sum(grad_ln, 0, keepdims=True)
-    gvec_ref[4 + pieces : 5 + pieces, :] += jnp.sum(gradf, 0, keepdims=True)
-    grad_mid = gradf + normalize_back(grad_ln * gain, normed, inverse)
-    gmid_ref[...] = grad_mid
-    branch = grad_mid.astype(BF)
-    gwo_ref[...] += dot(att_low, branch)
-    grad_att = dot_nt(wo, branch).astype(BF)
-    spare = jnp.zeros((128 - AUG, rows), F32)
-    from_log2 = math.sqrt(head) * LN2
-    for h in range(HEADS):
-        mine = slice(h * head, (h + 1) * head)
-        grad_head = grad_att[mine, :]
-        dot_ref[h] = grad_head
-        grad_head = grad_head.astype(F32)
-        delta = jnp.sum(grad_head * att[mine, :], 0, keepdims=True)
-        wide = jnp.concatenate([grad_head, split_rows(-delta, AUG - head), spare], 0)
-        doa_ref[h] = wide.T.astype(BF)
-        level = lse_ref[h, 0:1, :] * from_log2
-        wide = jnp.concatenate([qt_ref[h].astype(F32), split_rows(-level, AUG - head), spare], 0)
-        qa_ref[h] = wide.T.astype(BF)
-
-    @pl.when(pl.program_id(0) == pl.num_programs(0) - 1)
-    def _():
-        grads = jnp.concatenate([gwo_ref[...], gup_ref[...].T, gdown_ref[...].T], 0)
-        into_slots(late_ref, grads, per)
-
-
 def into_slots(slots_ref, grads, per):
     blk_size, owners, padded, width = slots_ref.shape
     filler = jnp.zeros((padded - per, width), F32)
@@ -505,67 +440,15 @@
         slots_ref[slot % blk_size, slot // blk_size] = piece.astype(BF)
 
 
-def between(x, mine, grad_near, grad_far, att, lse, qt, weights, vec, blk_size, per):
-    own, width = x.shape
-    head = width // HEADS
-    hidden_width = (weights.shape[0] - 4 * width) // 2
-    block = min(512, own // 2)
-    half = own // 2 // block
-    rows = lambda i, m: (i, 0)
-    lanes = lambda i, m: (0, 0, i)
-    tall = lambda i, m: (0, i, 0)
-    slots = (blk_size, (weights.shape[0] - 3 * width) // (blk_size * per), -(-per // 16) * 16, width)
-    grid_spec = pltpu.PrefetchScalarGridSpec(
-        num_scalar_prefetch=1,
-        grid=(own // block,),
-        in_specs=[
-            pl.BlockSpec((block, width), rows),
-            pl.BlockSpec((1, block, width), lambda i, m: (m[0], jnp.minimum(i, half - 1), 0)),
-            pl.BlockSpec((1, block, width), lambda i, m: (m[0], jnp.maximum(i - half, 0), 0)),
-            pl.BlockSpec((HEADS, head, block), lanes),
-            pl.BlockSpec((HEADS, 8, block), lanes),
-            pl.BlockSpec((HEADS, head, block), lanes),
-            whole(*weights.shape),
-            whole(*vec.shape),
-        ],
-        out_specs=[
-            pl.BlockSpec((block, width), rows),
-            pl.BlockSpec((block, width), rows),
-            pl.BlockSpec((HEADS, block, 128), tall),
-            pl.BlockSpec((HEADS, block, 128), tall),
-            pl.BlockSpec((HEADS, head, block), lanes),
-            whole(*slots),
-            whole(16, width),
-        ],
-        scratch_shapes=[
-            pltpu.VMEM((width, width), F32), pltpu.VMEM((width, hidden_width), F32), pltpu.VMEM((width, hidden_width), F32),
-        ],
-    )
-    return pl.pallas_call(
-        functools.partial(middle_kernel, per),
-        grid_spec=grid_spec,
-        out_shape=[
-            jax.ShapeDtypeStruct((own, width), BF),
-            jax.ShapeDtypeStruct((own, width), F32),
-            jax.ShapeDtypeStruct((HEADS, own, 128), BF),
-            jax.ShapeDtypeStruct((HEADS, own, 128), BF),
-            jax.ShapeDtypeStruct((HEADS, head, own), BF),
-            jax.ShapeDtypeStruct(slots, BF),
-            jax.ShapeDtypeStruct((16, width), F32),
-        ],
-        compiler_params=params(),
-        name="between",
-    )(mine, x, grad_near, grad_far, att, lse, qt, weights, vec)
-
-
 def back_kernel(
-    ctx_size, blk_size, per,
-    qa_hbm, doa_hbm, qt_hbm, dot_hbm, kta_hbm, vta_hbm, kn_hbm, ln_hbm, x_hbm, gmid_hbm, out_hbm, late_hbm,
-    gvec_in, w_ref, vec_ref,
+    ctx_size, blk_size, per, entries,
+    att_hbm, lse_hbm, qt_hbm, kta_hbm, vta_hbm, kn_hbm, ln_hbm, x_hbm, near_hbm, far_hbm, w_hbm,
+    vec_ref,
     grad_ref, out_ref, gw_ref, gvec_ref,
+    w_ref, att, lse, cotangent, gwo, gup, gdown, late,
     qa, doa, qt, dot_t, kta, vta, kn, ln, x, gmid, made,
     dq_sum, dk_sum, dv_sum, gq, gk, gv, part, part_out, part_in, wqt,
-    late_own, late_one, late_pass, late_two, late_sum, late_three,
+    late_one, late_pass, late_two, late_sum, late_three,
     early, early_one, early_pass, early_two, early_sum, early_three,
     vec_own, vec_one, vec_pair, vec_two, vec_sum, vec_three,
     head_sem, load_sem, out_sent, out_got, keep_sem, grad_sent, grad_got, part_sent, part_got,
@@ -580,7 +463,6 @@
     head = width // HEADS
     owners = early.shape[1]
     groups = ctx_size // owners
-    late_count = late_own.shape[1]
     group, place = lax.div(ctx, owners), lax.rem(ctx, owners)
     others = [lax.rem(ctx + step, ctx_size) for step in range(1, ctx_size)]
     peers = [lax.rem(place + step, owners) for step in range(1, owners)]
@@ -594,20 +476,24 @@
     local = pltpu.make_async_copy
 
     def head_loads(h):
-        pairs = ((qa_hbm, qa), (doa_hbm, doa), (qt_hbm, qt), (dot_hbm, dot_t), (kta_hbm, kta), (vta_hbm, vta), (kn_hbm, kn))
+        pairs = ((kta_hbm, kta), (vta_hbm, vta), (kn_hbm, kn))
         return [local(a.at[h], b.at[h], head_sem.at[i, h]) for i, (a, b) in enumerate(pairs)]
 
-    loads = [
-        local(ln_hbm, ln, load_sem.at[0]),
-        local(x_hbm.at[pl.ds(0, own)], x, load_sem.at[1]),
-        local(gmid_hbm, gmid, load_sem.at[2]),
-    ]
-    late_loads = [local(late_hbm.at[2 * y + core], late_own.at[y], load_sem.at[3 + y]) for y in range(2)]
-    out_keep = local(out_hbm.at[pl.ds(0, length)], out_ref.at[mine], keep_sem.at[0])
-    out_send = remote(out_hbm.at[pl.ds(length, length)], out_ref.at[mine], out_sent, out_got, to_far)
+    middle_loads = [
+        local(w_hbm, w_ref, load_sem.at[7]),
+        local(att_hbm, att, load_sem.at[0]),
+        local(x_hbm, x, load_sem.at[1]),
+        local(near_hbm.at[mine], cotangent.at[pl.ds(0, length)], load_sem.at[2]),
+        local(far_hbm.at[mine], cotangent.at[pl.ds(length, length)], load_sem.at[3]),
+        local(lse_hbm, lse, load_sem.at[4]),
+        local(qt_hbm, qt, load_sem.at[5]),
+    ]
+    ln_load = local(ln_hbm, ln, load_sem.at[6])
+    out_keep = local(made.at[pl.ds(0, length)], out_ref.at[mine], keep_sem.at[0])
+    out_send = remote(made.at[pl.ds(length, length)], out_ref.at[mine], out_sent, out_got, to_far)
 
     late_first = [
-        remote(late_hbm.at[2 * y + 1 - core], late_one.at[y], l1_sent.at[y], l1_got.at[y], to_near) for y in range(2)
+        remote(late.at[2 * y + 1 - core], late_one.at[y], l1_sent.at[y], l1_got.at[y], to_near) for y in range(2)
     ]
     late_second = remote(late_pass.at[1 - mine], late_two, l2_sent, l2_got, to_far)
 
@@ -656,18 +542,76 @@
         for i, other in enumerate(other_groups)
     ]
 
+    for load in middle_loads + head_loads(0):
+        load.start()
     greet([to_near, to_far] + [(other, blk) for other in others] + [(group * owners + peer, far) for peer in peers])
-    for load in head_loads(0):
-        load.start()
-    for copy in late_first + late_loads + [out_send, out_keep] + loads:
+    for ref in (gwo, gup, gdown, vec_own, gq, gk, gv, dq_sum, dk_sum, dv_sum):
+        ref[...] = jnp.zeros_like(ref)
+    for load in middle_loads:
+        load.wait()
+    ln_load.start()
+
+    gain_mid, bias_mid = vec_ref[2:3, :], vec_ref[3:4, :]
+    wo = w_ref[3 * width : 4 * width, :]
+    pieces = (w_ref.shape[0] - 4 * width) // (2 * width)
+    down_bias = vec_ref[4 + pieces : 5 + pieces, :]
+    from_log2 = math.sqrt(head) * LN2
+    count = min(512, length)
+
+    @pl.loop(0, own // count)
+    def _(index):
+        rows = pl.ds(pl.multiple_of(index * count, count), count)
+        attended = att[:, :, rows].reshape(width, count)
+        att_low = attended.astype(BF)
+        grad = cotangent[rows, :]
+        gradf = grad.astype(F32)
+        grad_t = gradf.T.astype(BF)
+        middle = x[rows, :].astype(F32) + dot_tn(att_low, wo)
+        normed, inverse = normalize(middle)
+        ln_mid = (normed * gain_mid + bias_mid).astype(BF)
+        ln_mid_t = ln_mid.astype(F32).T.astype(BF)
+        result = middle + down_bias
+        grad_ln = jnp.zeros((count, width), F32)
+        for p in range(pieces):
+            columns = slice(p * width, (p + 1) * width)
+            up = w_ref[(4 + p) * width : (5 + p) * width, :]
+            down = w_ref[(4 + pieces + p) * width : (5 + pieces + p) * width, :]
+            upper = dot_nt(ln_mid, up) + vec_ref[4 + p : 5 + p, :]
+            activated, slope = gelu_both(upper)
+            hidden = activated.astype(BF)
+            grad_low = (dot_nt(grad, down) * slope).astype(BF)
+            result = result + dot(hidden, down)
+            grad_ln = grad_ln + dot(grad_low, up)
+            gdown[:, columns] += dot(grad_t, hidden)
+            gup[:, columns] += dot(ln_mid_t, grad_low)
+            vec_own[4 + p : 5 + p, :] += jnp.sum(grad_low.astype(F32), 0, keepdims=True)
+        made[rows, :] = result.astype(BF)
+        vec_own[2:3, :] += jnp.sum(grad_ln * normed, 0, keepdims=True)
+        vec_own[3:4, :] += jnp.sum(grad_ln, 0, keepdims=True)
+        vec_own[4 + pieces : 5 + pieces, :] += jnp.sum(gradf, 0, keepdims=True)
+        grad_mid = gradf + normalize_back(grad_ln * gain_mid, normed, inverse)
+        gmid[rows, :] = grad_mid
+        branch = grad_mid.astype(BF)
+        gwo[...] += dot(att_low, branch)
+        grad_att = dot_nt(wo, branch).astype(BF)
+        spare = jnp.zeros((128 - AUG, count), F32)
+        for h in range(HEADS):
+            part_of = slice(h * head, (h + 1) * head)
+            grad_head = grad_att[part_of, :]
+            dot_t[h, :, rows] = grad_head
+            grad_head = grad_head.astype(F32)
+            delta = jnp.sum(grad_head * attended[part_of, :], 0, keepdims=True)
+            wide = jnp.concatenate([grad_head, split_rows(-delta, AUG - head), spare], 0)
+            doa[h, rows, :] = wide.T.astype(BF)
+            level = lse[h, 0:1, rows] * from_log2
+            wide = jnp.concatenate([qt[h, :, rows].astype(F32), split_rows(-level, AUG - head), spare], 0)
+            qa[h, rows, :] = wide.T.astype(BF)
+
+    out_send.start()
+    out_keep.start()
+    into_slots(late, jnp.concatenate([gwo[...], gup[...].T, gdown[...].T], 0), per)
+    for copy in late_first:
         copy.start()
-    dq_sum[...] = jnp.zeros_like(dq_sum)
-    dk_sum[...] = jnp.zeros_like(dk_sum)
-    dv_sum[...] = jnp.zeros_like(dv_sum)
-    gq[...] = jnp.zeros_like(gq)
-    gk[...] = jnp.zeros_like(gk)
-    gv[...] = jnp.zeros_like(gv)
-    vec_own[...] = gvec_in[...]
 
     tk = min(256, length)
     inverse_root = 1.0 / math.sqrt(head)
@@ -725,9 +669,8 @@
         @pl.when(t == 2)
         def _():
             for y in range(2):
-                late_loads[y].wait()
                 late_first[y].wait_recv()
-                late_pass[y] = (late_own[y].astype(F32) + late_one[y].astype(F32)).astype(BF)
+                late_pass[y] = (late[2 * y + core].astype(F32) + late_one[y].astype(F32)).astype(BF)
             late_second.start()
 
         @pl.when(t == 5)
@@ -746,8 +689,9 @@
                 low = head_index * 128
                 wqt[low : low + head, :] = turned[head_index * head : (head_index + 1) * head, :].astype(BF)
                 wqt[low + head : low + 128, :] = jnp.zeros((128 - head, width), BF)
-            for load in loads:
-                load.wait()
+            ln_load.wait()
+            out_keep.wait()
+            out_send.wait()
             terms(1)
 
         @pl.when(t == 3 * HEADS + 1)
@@ -836,12 +780,20 @@
             whole_sum = whole_sum + early_three[slot].astype(F32)
         gw_ref[...] = whole_sum
 
+    for copy in vec_third:
+        copy.wait_send()
     for other in other_groups:
         from_plane(other, vec_three, v3_got).wait_recv()
         vec_total = vec_total + vec_three[other]
-    gvec_ref[...] = vec_total
-
-    for copy in late_first + [late_second, part_send(0), part_send(1), vec_first] + early_first + early_second + vec_second + vec_third:
+    vec_sum[...] = vec_total
+    begin = (ctx * blk_size + blk) * entries
+    row, shift = lax.div(begin, width), lax.rem(begin, width)
+    after = jnp.minimum(row + 1, vec_sum.shape[0] - 1)
+    pair_rows = jnp.concatenate([vec_sum[pl.ds(row, 1), :], vec_sum[pl.ds(after, 1), :]], 1)
+    pair_rows = jnp.broadcast_to(pair_rows, (8, 2 * width))
+    gvec_ref[...] = pltpu.roll(pair_rows, lax.rem(2 * width - shift, 2 * width), 1)[:, :128]
+
+    for copy in late_first + [late_second, part_send(0), part_send(1), vec_first] + early_first + early_second + vec_second:
         copy.wait_send()
     for step, other in enumerate(others):
         @pl.when(other >= owners)
@@ -853,20 +805,20 @@
         def _():
             early_third.wait_send()
 
-    out_keep.wait()
-    out_send.wait()
     for c in range(chunks):
         grad_keep(c, size).wait()
         grad_send(1, c, size).wait()
 
 
-def back(ctx_size, blk_size, per, owners, qa, doa, qt, dot_t, kta, vta, kn, ln, rows_all, gmid, out, late, gvec, w_input, vec):
-    own, width = gmid.shape
+def back(ctx_size, blk_size, per, entries, owners, att, lse, qt, kta, vta, kn, ln, rows, grad_near, grad_far, weights, vec):
+    own, width = rows.shape
     head = width // HEADS
     total = 2 * own
     length = own // 2
     groups = ctx_size // owners
-    _, late_count, padded, _ = late.shape
+    hidden_width = (weights.shape[0] - 4 * width) // 2
+    late_count = (weights.shape[0] - 3 * width) // (blk_size * per)
+    padded = -(-per // 16) * 16
     dma = pltpu.SemaphoreType.DMA
     place = pl.BlockSpec(memory_space=pl.ANY)
     vmem = pl.BlockSpec(memory_space=pltpu.VMEM)
@@ -876,43 +828,84 @@
     plane = 2 * owners
     some = lambda count: dma((max(count, 1),))
     return pl.pallas_call(
-        functools.partial(back_kernel, ctx_size, blk_size, per),
-        in_specs=[place] * 12 + [vmem] * 3,
+        functools.partial(back_kernel, ctx_size, blk_size, per, entries),
+        in_specs=[place] * 11 + [vmem],
         out_specs=[place, place, vmem, vmem],
         out_shape=[
             jax.ShapeDtypeStruct((2, length, width), BF),
             jax.ShapeDtypeStruct((2, length, width), BF),
             jax.ShapeDtypeStruct((padded, width), F32),
-            jax.ShapeDtypeStruct((16, width), F32),
+            jax.ShapeDtypeStruct((8, 128), F32),
         ],
         scratch_shapes=[
+            low(*weights.shape), single(HEADS, head, own), single(HEADS, 8, own), low(own, width), single(width, width), single(width, hidden_width),
+            single(width, hidden_width), low(blk_size, late_count, padded, width),
             low(HEADS, own, 128), low(HEADS, own, 128), low(HEADS, head, own), low(HEADS, head, own),
             low(HEADS, AUG, total), low(HEADS, AUG, total), low(HEADS, total, 128), low(total, width),
             low(own, width), single(own, width), low(own, width),
             single(HEADS, own, 128), single(HEADS, head, total), single(HEADS, head, total),
             single(width, HEADS * 128), single(width, width), single(width, width),
             single(2, width, length), low(2, width, length), low(2, width, length), low(HEADS * 128, width),
-            low(2, late_count, padded, width), low(2, late_count, padded, width), low(2, late_count, padded, width),
+            low(2, late_count, padded, width), low(2, late_count, padded, width),
             low(late_count, padded, width), low(late_count, padded, width), low(ctx_size, padded, width),
             low(blk_size, owners, padded, width), low(2, owners, padded, width), low(2, owners, padded, width),
             low(plane, padded, width), low(padded, width), low(max(groups - 1, 1), padded, width),
             single(16, width), single(16, width), single(16, width), single(plane, 16, width), single(16, width),
             single(groups, 16, width),
-            dma((7, HEADS)), dma((5,)), dma, dma, dma((1 + chunks,)), dma((chunks,)), dma((chunks,)), dma((2,)), dma((2,)),
+            dma((3, HEADS)), dma((8,)), dma, dma, dma((1 + chunks,)), dma((chunks,)), dma((chunks,)), dma((2,)), dma((2,)),
             dma((2,)), dma((2,)), dma, dma, some(ctx_size - 1), dma((ctx_size,)),
             dma((2,)), dma((2,)), some(plane - 1), dma((plane,)), dma, some(groups - 1),
             dma, dma, some(plane - 1), dma((plane,)), some(groups - 1), dma((groups,)),
         ],
         compiler_params=params(collective_id=2, has_side_effects=True),
         name="back",
-    )(qa, doa, qt, dot_t, kta, vta, kn, ln, rows_all, gmid, out, late, gvec, w_input, vec)
+    )(att, lse, qt, kta, vta, kn, ln, rows, grad_near, grad_far, weights, vec)
+
+
+def publish_kernel(grad_ref, out_ref, mats_ref, vec_ref, grad_to, out_to, mats_to, vec_to, grad, out, mats, vecs, sems):
+    ways = []
+    for a, b, c in ((grad_ref, grad, grad_to), (out_ref, out, out_to)):
+        pieces = 2
+        size = a.shape[1] // pieces
+        for half in range(2):
+            for piece in range(pieces):
+                part = pl.ds(piece * size, size)
+                ways.append((a.at[half, part], b.at[half, part], c.at[half, part]))
+    kept = pl.ds(0, mats_to.shape[0])
+    ways.append((mats_ref.at[kept], mats.at[kept], mats_to))
+    ways.append((vec_ref, vecs, vec_to))
+    come = [pltpu.make_async_copy(a, b, sems.at[0, i]) for i, (a, b, _) in enumerate(ways)]
+    go = [pltpu.make_async_copy(b, c, sems.at[1, i]) for i, (_, b, c) in enumerate(ways)]
+    for copy in come:
+        copy.start()
+    for first, second in zip(come, go):
+        first.wait()
+        second.start()
+    for copy in go:
+        copy.wait()
+
+
+def publish(grad, out, mats, vecs, per):
+    place = pl.BlockSpec(memory_space=pl.ANY)
+    shapes = [grad.shape, out.shape, (per, mats.shape[1]) if per % 8 == 0 else mats.shape, vecs.shape]
+    types = [BF, BF, F32, F32]
+    return pl.pallas_call(
+        publish_kernel,
+        in_specs=[place] * 4,
+        out_specs=[place] * 4,
+        out_shape=[jax.ShapeDtypeStruct(shape, kind) for shape, kind in zip(shapes, types)],
+        scratch_shapes=[
+            pltpu.VMEM(grad.shape, BF), pltpu.VMEM(out.shape, BF), pltpu.VMEM(mats.shape, F32), pltpu.VMEM(vecs.shape, F32),
+            pltpu.SemaphoreType.DMA((2, 10)),
+        ],
+        compiler_params=params(),
+        name="publish",
+    )(grad, out, mats, vecs)
 
 
 def per_device(ctx_size, blk_size, layer_in, matrices, vectors, out_grad):
     seq_count, local_rows, width = layer_in.shape
     per, entries = matrices.shape[0], vectors.shape[0]
-    flat = lax.axis_index("ctx") * blk_size + lax.axis_index("blk")
-    mine = lax.axis_index("blk") // (blk_size // seq_count)
     far = [(b, (b + blk_size // 2) % blk_size) for b in range(blk_size)]
     owners = 3 * width // (per * blk_size)
     weights = lax.all_gather(matrices, ("ctx", "blk"), axis=0, tiled=True)
@@ -921,14 +914,11 @@
     out_grad, qt = lax.optimization_barrier((out_grad, qt))
     grad_far = lax.ppermute(out_grad, "blk", far)
     att, lse = attend(qt, kn, kta, vta)
-    out, gmid, qa, doa, dot_t, late, gvec = between(
-        rows, jnp.reshape(mine, (1,)).astype(jnp.int32), out_grad, grad_far, att, lse, qt, weights, vec, blk_size, per
+    layer_grad, layer_out, matrices_grad, vecs = back(
+        ctx_size, blk_size, per, entries, owners, att, lse, qt, kta, vta, kn, ln, rows, out_grad, grad_far, weights, vec
     )
-    layer_grad, layer_out, matrices_grad, vecs = back(
-        ctx_size, blk_size, per, owners, qa, doa, qt, dot_t, kta, vta, kn, ln, rows, gmid, out, late, gvec, weights, vec
-    )
-    vectors_grad = lax.dynamic_slice_in_dim(vecs.reshape(-1), flat * entries, entries)
-    return layer_out, layer_grad, matrices_grad[:per], vectors_grad
+    layer_grad, layer_out, matrices_grad, vecs = publish(layer_grad, layer_out, matrices_grad, vecs, per)
+    return layer_out, layer_grad, matrices_grad[:per], vecs[0, :entries]
 
 
 def solution(mesh):

time: 205 us -> 197 us (0.961)
  local copies, waits for them, and re-layouts: 6.25 us -> 2.12 us
  Pallas kernels: 183 us -> 180 us
    unnamed x10 -> x2, local copies, waits for them, and re-layouts: 5.66 us -> 0.94 us
    pallas_call x2, Pallas kernels: 121 us -> 117 us  [the longest x1 115 us: back(): pl.pallas_call(functools.partial(back_kernel, ctx_size, blk_size, per, en...]
  transfers between devices with their start and end apart: 2 -> 2, of which waited for: 0 -> 0; matrix products, arithmetic and copies ran while one was open for 0% -> 0% of each run, Pallas kernels for 30% -> 32%
where the time goes in v6:
time: 197 us
  Pallas kernels  180 us (91%)
  between operations  14.1 us (7%)
  local copies, waits for them, and re-layouts  2.12 us (1%)
    pallas_call x1, Pallas kernels, back(): pl.pallas_call(functools.partial(back_kernel, ctx_size, blk_size, per, en...  115 us
    pallas_call x1, Pallas kernels, attend(): pl.pallas_call(attend_kernel, grid=(HEADS,), in_specs=[per_head(head, own...  33 us
    pallas_call x1, Pallas kernels, start(): pl.pallas_call(functools.partial(start_kernel, ctx_size, blk_size, per),...  29.6 us
  transfers between devices with their start and end apart: 2, of which 0 were waited for; matrix products, arithmetic and copies ran while one was open for 0% of the time, Pallas kernels for 32%

profile of v6, /device:TPU:0, one launch (start us, length us, event | category | flops | bytes accessed | tf_op | source)
XLA Modules:
  0.0 197.2 jit_solution(7015815245577562515)
XLA Ops:
  7.2 0.0 all-gather.2.cloned.1.call-start
  7.2 0.7 all-gather.2.cloned.1.call-update
  7.9 29.6 %start.1 = (bf16[2048,256]{1,0:T(8,128)(2,1)}, bf16[4096,256]{1,0:T(8,128)(2,1)}, bf16[4,64,2048]{2,1,0:T(8,128)(2,1)}, bf16[4,4096,128]{2,1,0:T(8,128)(2,1)}, b...) custom-call(bf16[2,1024,256]{2,1,0:T(8,128)(2,1)} %x_hbm.1, bf16[96,256]{1,0:T(8,128)(2,1)} %w_hbm.1, ...), custom_call_target="tpu_custom_call" | custom-call | tf_op jit(solution)/shard_map/start/pallas_call | solution.py:321
  37.5 0.6 collective-permute-start
  38.1 33.0 %attend.1 = (f32[4,64,2048]{2,1,0:T(8,128)}, f32[4,8,2048]{2,1,0:T(8,128)}) custom-call(bf16[4,64,2048]{2,1,0:T(8,128)(2,1)} %get-tuple-element.24.qt_ref.qt_hbm, bf16[4,4096,128]{2,1,0:T(8,128)(2,1)} %get-tuple-element.25.kn_ref.kn_hbm, bf16[4,80,4096]{2,1,0:T(8,128)(2,1)} %get-tuple-element.26.kta_ref.kta_hbm, ...), custom_call_target="tpu_custom_call" | custom-call | tf_op jit(solution)/shard_map/attend/pallas_call | solution.py:404
  71.1 0.0 collective-permute-done.far_hbm
  71.1 0.0 copy-start
  71.1 0.0 all-gather.2.cloned.1.call-done.w_hbm
  71.1 0.9 copy-done
  72.1 114.6 %back.1 = (bf16[2,1024,256]{2,1,0:T(8,128)(2,1)}, bf16[2,1024,256]{2,1,0:T(8,128)(2,1)}, f32[96,256]{1,0:T(8,128)}, f32[8,128]{1,0:T(8,128)}) custom-call(f32[4,64,2048]{2,1,0:T(8,128)} %get-tuple-element.28.att_hbm, f32[4,8,2048]{2,1,0:T(8,128)} %get-tuple-element.29.lse_hbm, bf16[4,64,2048]{2,1,0:T(8,128)(2,1)} %get-tuple-element.24.qt_ref.qt_hbm, ...), custom_call_target="tpu_custom_call" | custom-call | tf_op jit(solution)/shard_map/back/pallas_call | solution.py:830
  186.7 2.5 %publish.1 = (bf16[2,1024,256]{2,1,0:T(8,128)(2,1)}, bf16[2,1024,256]{2,1,0:T(8,128)(2,1)}, f32[96,256]{1,0:T(8,128)}, f32[8,128]{1,0:T(8,128)}) custom-call(bf16[2,1024,256]{2,1,0:T(8,128)(2,1)} %get-tuple-element.34.grad_ref, bf16[2,1024,256]{2,1,0:T(8,128)(2,1)} %get-tuple-element.35.out_ref, f32[96,256]{1,0:T(8,128)} %get-tuple-element.36.mats_ref, ...), custom_call_target="tpu_custom_call" | custom-call | tf_op jit(solution)/shard_map/publish/pallas_call | solution.py:892
  189.1 1.2 slice_bitcast_fusion
Async XLA Ops:
  7.2 64.0 %all-gather.2.cloned.1.call-start = ((), (), s32[]{:S(2)}) async-start(), calls=%async_computation | async-start | bytes 1622016 | tf_op jit(solution)/shard_map/all_gather | solution.py:911
  37.5 33.6 %collective-permute-start = (bf16[2,1024,256]{2,1,0:T(8,128)(2,1)}, bf16[2,1024,256]{2,1,0:T(8,128)(2,1)S(1)}, u32[]{:S(2)}, u32[]{:S(2)}) collective-permute-start(bf16[2,1024,256]{2,1,0:T(8,128)(2,1)} %near_hbm), channel_id=1, source_target_pairs={{0,2},{1,3},{2,0},{3,1},{4,6},{5,7},{6,4},{7,5},{8,10},{9,11},{10,... | collective-permute-start | bytes 3145736 | tf_op jit(solution)/shard_map/ppermute | solution.py:915
  71.1 1.0 copy-start
Sparse Core Ops, SparseCore 0:
  10.9 60.0 all-gather.1

commit v7 on v6

--- a/solution.py
+++ b/solution.py
@@ -232,6 +232,10 @@
                 copies.append(local(a.at[:, :, rows], b.at[:, :, rows], out_sem.at[i, index]))
         return copies
 
+    def query_copy(base, index):
+        rows = pl.ds(base, block)
+        return local(qt.at[:, :, rows], qt_out.at[:, :, rows], out_sem.at[4, index])
+
     def first_row(index):
         quarter = lax.div(index, per_quarter)
         order = lax.rem(quarter, 2) * 2 + lax.div(quarter, 2)
@@ -277,19 +281,21 @@
             queries = dot_nt(wt[0:width, :], low)
             for h in range(HEADS):
                 qt[h, :, rows] = queries[h * head : (h + 1) * head, :].astype(BF)
+            query_copy(base, index).start()
 
         for copy in out_copies(base, index):
             copy.start()
 
-    qt_copy = local(qt, qt_out, x_sem)
-    qt_copy.start()
-
     @pl.loop(0, 4 * per_quarter)
     def _(index):
-        for copy in out_copies(first_row(index), index):
+        base = first_row(index)
+        for copy in out_copies(base, index):
             copy.wait()
 
-    qt_copy.wait()
+        @pl.when(lax.rem(lax.div(index, per_quarter), 2) == 0)
+        def _():
+            query_copy(base, index).wait()
+
     rows_keep.wait()
 
     @pl.when(group == 0)
@@ -331,7 +337,7 @@
             dma, dma((chunks,)), dma((chunks,)), dma, dma, dma((chunks,)), dma((chunks,)), dma,
             dma((max(ctx_size // owners - 1, 1),)), dma, dma((2 * owners,)), dma((2 * owners,)), dma((2 * owners,)), dma((2 * owners,)),
             some, dma((ctx_size,)), dma, dma, dma((2,)), dma((2,)),
-            dma, dma((4, blocks)),
+            dma, dma((5, blocks)),
         ],
         compiler_params=params(collective_id=1, has_side_effects=True),
         name="start",
@@ -442,12 +448,12 @@
 
 def back_kernel(
     ctx_size, blk_size, per, entries,
-    att_hbm, lse_hbm, qt_hbm, kta_hbm, vta_hbm, kn_hbm, ln_hbm, x_hbm, near_hbm, far_hbm, w_hbm,
+    att_hbm, lse_hbm, qt_hbm, kta_hbm, vta_hbm, ln_hbm, x_hbm, near_hbm, far_hbm, w_hbm,
     vec_ref,
     grad_ref, out_ref, gw_ref, gvec_ref,
     w_ref, att, lse, cotangent, gwo, gup, gdown, late,
-    qa, doa, qt, dot_t, kta, vta, kn, ln, x, gmid, made,
-    dq_sum, dk_sum, dv_sum, gq, gk, gv, part, part_out, part_in, wqt,
+    qa_near, doa_near, dot_near, qa_far, doa_far, dot_far, qt, kta, vta, ln, x, gmid, made, turned,
+    dq_sum, dk_sum, dv_sum, gq, gk, gv, part, part_out, part_in,
     late_one, late_pass, late_two, late_sum, late_three,
     early, early_one, early_pass, early_two, early_sum, early_three,
     vec_own, vec_one, vec_pair, vec_two, vec_sum, vec_three,
@@ -476,7 +482,7 @@
     local = pltpu.make_async_copy
 
     def head_loads(h):
-        pairs = ((kta_hbm, kta), (vta_hbm, vta), (kn_hbm, kn))
+        pairs = ((kta_hbm, kta), (vta_hbm, vta))
         return [local(a.at[h], b.at[h], head_sem.at[i, h]) for i, (a, b) in enumerate(pairs)]
 
     middle_loads = [
@@ -556,11 +562,9 @@
     pieces = (w_ref.shape[0] - 4 * width) // (2 * width)
     down_bias = vec_ref[4 + pieces : 5 + pieces, :]
     from_log2 = math.sqrt(head) * LN2
-    count = min(512, length)
-
-    @pl.loop(0, own // count)
-    def _(index):
-        rows = pl.ds(pl.multiple_of(index * count, count), count)
+
+    def middle_rows(base, low, count, qa, doa, dot_t):
+        rows, local_rows = pl.ds(pl.multiple_of(base + low, count), count), pl.ds(pl.multiple_of(low, count), count)
         attended = att[:, :, rows].reshape(width, count)
         att_low = attended.astype(BF)
         grad = cotangent[rows, :]
@@ -570,6 +574,7 @@
         normed, inverse = normalize(middle)
         ln_mid = (normed * gain_mid + bias_mid).astype(BF)
         ln_mid_t = ln_mid.astype(F32).T.astype(BF)
+        yield
         result = middle + down_bias
         grad_ln = jnp.zeros((count, width), F32)
         for p in range(pieces):
@@ -585,6 +590,7 @@
             gdown[:, columns] += dot(grad_t, hidden)
             gup[:, columns] += dot(ln_mid_t, grad_low)
             vec_own[4 + p : 5 + p, :] += jnp.sum(grad_low.astype(F32), 0, keepdims=True)
+            yield
         made[rows, :] = result.astype(BF)
         vec_own[2:3, :] += jnp.sum(grad_ln * normed, 0, keepdims=True)
         vec_own[3:4, :] += jnp.sum(grad_ln, 0, keepdims=True)
@@ -595,27 +601,32 @@
         gwo[...] += dot(att_low, branch)
         grad_att = dot_nt(wo, branch).astype(BF)
         spare = jnp.zeros((128 - AUG, count), F32)
+        yield
         for h in range(HEADS):
             part_of = slice(h * head, (h + 1) * head)
             grad_head = grad_att[part_of, :]
-            dot_t[h, :, rows] = grad_head
+            dot_t[h, :, local_rows] = grad_head
             grad_head = grad_head.astype(F32)
             delta = jnp.sum(grad_head * attended[part_of, :], 0, keepdims=True)
             wide = jnp.concatenate([grad_head, split_rows(-delta, AUG - head), spare], 0)
-            doa[h, rows, :] = wide.T.astype(BF)
+            doa[h, local_rows, :] = wide.T.astype(BF)
             level = lse[h, 0:1, rows] * from_log2
             wide = jnp.concatenate([qt[h, :, rows].astype(F32), split_rows(-level, AUG - head), spare], 0)
-            qa[h, rows, :] = wide.T.astype(BF)
-
-    out_send.start()
+            qa[h, local_rows, :] = wide.T.astype(BF)
+            if h == 1:
+                yield
+
+    step_rows = min(512, length)
+
+    @pl.loop(0, length // step_rows)
+    def _(index):
+        for _ in middle_rows(0, index * step_rows, step_rows, qa_near, doa_near, dot_near):
+            pass
+
     out_keep.start()
-    into_slots(late, jnp.concatenate([gwo[...], gup[...].T, gdown[...].T], 0), per)
-    for copy in late_first:
-        copy.start()
-
     tk = min(256, length)
     inverse_root = 1.0 / math.sqrt(head)
-    wk, wv = w_ref[width : 2 * width, :], w_ref[2 * width : 3 * width, :]
+    wq, wk, wv = (w_ref[index * width : (index + 1) * width, :] for index in range(3))
     gain = vec_ref[0:1, :]
     size = min(512, length)
     chunks = length // size
@@ -631,79 +642,28 @@
                 part_out[half] = both.astype(BF)
                 part_send(half).start()
             else:
-                part[half] = both
+                dq = (dq_sum[:, :, rows] * inverse_root).astype(BF).reshape(width, length)
+                part[half] = both + dot(wq, dq)
+                gq[...] += dot(dq, ln[rows, :])
             gk[...] += dot(dk, ln[rows, :])
             gv[...] += dot(dv, ln[rows, :])
-        for c in range(chunks):
-            low = half * length + c * size
-            gq[...] += dot_tn(ln[low : low + size, :], query_grads(low))
-
-    def query_grads(low):
-        return jnp.concatenate([(dq_sum[h, low : low + size, :] * inverse_root).astype(BF) for h in range(HEADS)], 1)
 
     def rows_back(half):
         for c in range(chunks):
             rows = slice(half * length + c * size, half * length + (c + 1) * size)
             lanes = slice(c * size, (c + 1) * size)
-            grad_ln = dot(query_grads(half * length + c * size), wqt[...]) + (part[half, :, lanes] + part_in[half, :, lanes].astype(F32)).T
+            grad_ln = (part[half, :, lanes] + part_in[half, :, lanes].astype(F32)).T
             normed, inverse = normalize(x[rows, :].astype(F32))
             vec_own[0:1, :] += jnp.sum(grad_ln * normed, 0, keepdims=True)
             vec_own[1:2, :] += jnp.sum(grad_ln, 0, keepdims=True)
             made[rows, :] = (gmid[rows, :] + normalize_back(grad_ln * gain, normed, inverse)).astype(BF)
             (grad_send(half, c, size) if half else grad_keep(c, size)).start()
 
-    @pl.loop(0, 4 * HEADS)
-    def _(t):
-        block, h = lax.div(t, HEADS), lax.rem(t, HEADS)
-
-        @pl.when(block == 0)
-        def _():
-            for load in head_loads(h):
-                load.wait()
-
-        @pl.when(t < HEADS - 1)
-        def _():
-            for load in head_loads(t + 1):
-                load.start()
-
-        @pl.when(t == 2)
-        def _():
-            for y in range(2):
-                late_first[y].wait_recv()
-                late_pass[y] = (late[2 * y + core].astype(F32) + late_one[y].astype(F32)).astype(BF)
-            late_second.start()
-
-        @pl.when(t == 5)
-        def _():
-            late_second.wait_recv()
-            late_sum[...] = (late_pass[mine].astype(F32) + late_two[...].astype(F32)).astype(BF)
-            for step, other in enumerate(others):
-                @pl.when(other >= owners)
-                def _():
-                    late_third(step).start()
-
-        @pl.when(t == 3 * HEADS)
-        def _():
-            turned = w_ref[:width, :].astype(F32).T
-            for head_index in range(HEADS):
-                low = head_index * 128
-                wqt[low : low + head, :] = turned[head_index * head : (head_index + 1) * head, :].astype(BF)
-                wqt[low + head : low + 128, :] = jnp.zeros((128 - head, width), BF)
-            ln_load.wait()
-            out_keep.wait()
-            out_send.wait()
-            terms(1)
-
-        @pl.when(t == 3 * HEADS + 1)
-        def _():
-            part_send(1).wait_recv()
-            rows_back(1)
-
-        first_half = jnp.logical_or(block == 0, block == 3)
-        where = pl.ds(pl.multiple_of(jnp.where(first_half, 0, length), length), length)
-        base = jnp.where(block < 2, length, 0)
-        queries, grads = qa[h, where, :AUG], doa[h, where, :AUG]
-        queries_t, grads_t = qt[h, :, where], dot_t[h, :, where]
+    def attention(h, half, base, qa, doa, dot_t, beside=None):
+        beside = beside or iter(())
+        queries, grads = qa[h, :, :AUG], doa[h, :, :AUG]
+        where = slice(half * length, (half + 1) * length)
+        queries_t, grads_t = qt[h, :, where], dot_t[h]
         parts = []
         for offset in (0, own):
             for low in range(0, length, tk):
@@ -712,7 +672,7 @@
         def pair(part):
             return dot(queries, kta[h, :, part]), dot(grads, vta[h, :, part])
 
-        grad_query = jnp.zeros((length, 128), F32)
+        grad_query = jnp.zeros((head, length), F32)
         level, change = pair(parts[0])
         for j, part_now in enumerate(parts):
             probs = jnp.exp2(level * (LOG2E * inverse_root))
@@ -720,13 +680,71 @@
             grad_scores = (probs * change).astype(BF)
             if j + 1 < len(parts):
                 level, change = pair(parts[j + 1])
+            next(beside, None)
             dv_sum[h, :, part_now] += dot(grads_t, probs_low)
             dk_sum[h, :, part_now] += dot(queries_t, grad_scores)
-            grad_query = grad_query + dot(grad_scores, kn[h, part_now, :])
-        dq_sum[h, where, :] += grad_query
+            turned[j % 2] = grad_scores.T
+            grad_query = grad_query + dot(kta[h, :head, part_now], turned[j % 2])
+        for _ in beside:
+            pass
+        dq_sum[h, :, where] += grad_query
+
+    piece_rows = length // HEADS
+
+    @pl.loop(0, HEADS)
+    def _(h):
+        for load in head_loads(h):
+            load.wait()
+
+        @pl.when(h < HEADS - 1)
+        def _():
+            for load in head_loads(h + 1):
+                load.start()
+
+        beside = middle_rows(length, h * piece_rows, piece_rows, qa_far, doa_far, dot_far)
+        attention(h, 0, length, qa_near, doa_near, dot_near, beside)
+
+    out_send.start()
+    into_slots(late, jnp.concatenate([gwo[...], gup[...].T, gdown[...].T], 0), per)
+    for copy in late_first:
+        copy.start()
+
+    @pl.loop(0, 2 * HEADS)
+    def _(t):
+        @pl.when(t == 1)
+        def _():
+            for y in range(2):
+                late_first[y].wait_recv()
+                late_pass[y] = (late[2 * y + core].astype(F32) + late_one[y].astype(F32)).astype(BF)
+            late_second.start()
+
+        @pl.when(t == 4)
+        def _():
+            late_second.wait_recv()
+            late_sum[...] = (late_pass[mine].astype(F32) + late_two[...].astype(F32)).astype(BF)
+            for step, other in enumerate(others):
+                @pl.when(other >= owners)
+                def _():
+                    late_third(step).start()
+
+        attention(lax.rem(t, HEADS), 1, jnp.where(t < HEADS, length, 0), qa_far, doa_far, dot_far)
+
+    ln_load.wait()
+    out_keep.wait()
+    out_send.wait()
+    terms(1)
+
+    @pl.loop(0, HEADS)
+    def _(h):
+        @pl.when(h == 1)
+        def _():
+            part_send(1).wait_recv()
+            rows_back(1)
+
+        attention(h, 0, 0, qa_near, doa_near, dot_near)
 
     terms(0)
-    grads = jnp.concatenate([jnp.concatenate([gq[:, h * 128 : h * 128 + head] for h in range(HEADS)], 1), gk[...].T, gv[...].T], 0)
+    grads = jnp.concatenate([gq[...].T, gk[...].T, gv[...].T], 0)
     into_slots(early, grads, per)
     for copy in early_first:
         copy.start()
@@ -810,7 +828,7 @@
         grad_send(1, c, size).wait()
 
 
-def back(ctx_size, blk_size, per, entries, owners, att, lse, qt, kta, vta, kn, ln, rows, grad_near, grad_far, weights, vec):
+def back(ctx_size, blk_size, per, entries, owners, att, lse, qt, kta, vta, ln, rows, grad_near, grad_far, weights, vec):
     own, width = rows.shape
     head = width // HEADS
     total = 2 * own
@@ -829,7 +847,7 @@
     some = lambda count: dma((max(count, 1),))
     return pl.pallas_call(
         functools.partial(back_kernel, ctx_size, blk_size, per, entries),
-        in_specs=[place] * 11 + [vmem],
+        in_specs=[place] * 10 + [vmem],
         out_specs=[place, place, vmem, vmem],
         out_shape=[
             jax.ShapeDtypeStruct((2, length, width), BF),
@@ -840,26 +858,27 @@
         scratch_shapes=[
             low(*weights.shape), single(HEADS, head, own), single(HEADS, 8, own), low(own, width), single(width, width), single(width, hidden_width),
             single(width, hidden_width), low(blk_size, late_count, padded, width),
-            low(HEADS, own, 128), low(HEADS, own, 128), low(HEADS, head, own), low(HEADS, head, own),
-            low(HEADS, AUG, total), low(HEADS, AUG, total), low(HEADS, total, 128), low(total, width),
-            low(own, width), single(own, width), low(own, width),
-            single(HEADS, own, 128), single(HEADS, head, total), single(HEADS, head, total),
-            single(width, HEADS * 128), single(width, width), single(width, width),
-            single(2, width, length), low(2, width, length), low(2, width, length), low(HEADS * 128, width),
+            low(HEADS, length, 128), low(HEADS, length, 128), low(HEADS, head, length),
+            low(HEADS, length, 128), low(HEADS, length, 128), low(HEADS, head, length), low(HEADS, head, own),
+            low(HEADS, AUG, total), low(HEADS, AUG, total), low(total, width),
+            low(own, width), single(own, width), low(own, width), low(2, min(256, length), length),
+            single(HEADS, head, own), single(HEADS, head, total), single(HEADS, head, total),
+            single(width, width), single(width, width), single(width, width),
+            single(2, width, length), low(2, width, length), low(2, width, length),
             low(2, late_count, padded, width), low(2, late_count, padded, width),
             low(late_count, padded, width), low(late_count, padded, width), low(ctx_size, padded, width),
             low(blk_size, owners, padded, width), low(2, owners, padded, width), low(2, owners, padded, width),
             low(plane, padded, width), low(padded, width), low(max(groups - 1, 1), padded, width),
             single(16, width), single(16, width), single(16, width), single(plane, 16, width), single(16, width),
             single(groups, 16, width),
-            dma((3, HEADS)), dma((8,)), dma, dma, dma((1 + chunks,)), dma((chunks,)), dma((chunks,)), dma((2,)), dma((2,)),
+            dma((2, HEADS)), dma((8,)), dma, dma, dma((1 + chunks,)), dma((chunks,)), dma((chunks,)), dma((2,)), dma((2,)),
             dma((2,)), dma((2,)), dma, dma, some(ctx_size - 1), dma((ctx_size,)),
             dma((2,)), dma((2,)), some(plane - 1), dma((plane,)), dma, some(groups - 1),
             dma, dma, some(plane - 1), dma((plane,)), some(groups - 1), dma((groups,)),
         ],
         compiler_params=params(collective_id=2, has_side_effects=True),
         name="back",
-    )(att, lse, qt, kta, vta, kn, ln, rows, grad_near, grad_far, weights, vec)
+    )(att, lse, qt, kta, vta, ln, rows, grad_near, grad_far, weights, vec)
 
 
 def publish_kernel(grad_ref, out_ref, mats_ref, vec_ref, grad_to, out_to, mats_to, vec_to, grad, out, mats, vecs, sems):
@@ -915,7 +934,7 @@
     grad_far = lax.ppermute(out_grad, "blk", far)
     att, lse = attend(qt, kn, kta, vta)
     layer_grad, layer_out, matrices_grad, vecs = back(
-        ctx_size, blk_size, per, entries, owners, att, lse, qt, kta, vta, kn, ln, rows, out_grad, grad_far, weights, vec
+        ctx_size, blk_size, per, entries, owners, att, lse, qt, kta, vta, ln, rows, out_grad, grad_far, weights, vec
     )
     layer_grad, layer_out, matrices_grad, vecs = publish(layer_grad, layer_out, matrices_grad, vecs, per)
     return layer_out, layer_grad, matrices_grad[:per], vecs[0, :entries]

time: 197 us -> 189 us (0.959)
  Pallas kernels: 180 us -> 171 us
    pallas_call x1, Pallas kernels: 115 us -> 107 us  [back(): pl.pallas_call(functools.partial(back_kernel, ctx_size, blk_size, per, en...]
  transfers between devices with their start and end apart: 2 -> 2, of which waited for: 0 -> 0; matrix products, arithmetic and copies ran while one was open for 0% -> 0% of each run, Pallas kernels for 32% -> 33%
where the time goes in v7:
time: 189 us
  Pallas kernels  171 us (90%)
  between operations  14.1 us (7%)
  local copies, waits for them, and re-layouts  2.13 us (1%)
    pallas_call x1, Pallas kernels, back(): pl.pallas_call(functools.partial(back_kernel, ctx_size, blk_size, per, en...  107 us
    pallas_call x1, Pallas kernels, attend(): pl.pallas_call(attend_kernel, grid=(HEADS,), in_specs=[per_head(head, own...  33.1 us
    pallas_call x1, Pallas kernels, start(): pl.pallas_call(functools.partial(start_kernel, ctx_size, blk_size, per),...  29.3 us
  transfers between devices with their start and end apart: 2, of which 0 were waited for; matrix products, arithmetic and copies ran while one was open for 0% of the time, Pallas kernels for 33%

profile of v7, /device:TPU:0, one launch (start us, length us, event | category | flops | bytes accessed | tf_op | source)
XLA Modules:
  0.0 188.9 jit_solution(15190485503027343675)
XLA Ops:
  7.2 0.0 all-gather.2.cloned.1.call-start
  7.2 0.7 all-gather.2.cloned.1.call-update
  7.9 29.3 %start.1 = (bf16[2048,256]{1,0:T(8,128)(2,1)}, bf16[4096,256]{1,0:T(8,128)(2,1)}, bf16[4,64,2048]{2,1,0:T(8,128)(2,1)}, bf16[4,4096,128]{2,1,0:T(8,128)(2,1)}, b...) custom-call(bf16[2,1024,256]{2,1,0:T(8,128)(2,1)} %x_hbm.1, bf16[96,256]{1,0:T(8,128)(2,1)} %w_hbm.1, ...), custom_call_target="tpu_custom_call" | custom-call | tf_op jit(solution)/shard_map/start/pallas_call | solution.py:327
  37.2 0.6 collective-permute-start
  37.8 33.1 %attend.1 = (f32[4,64,2048]{2,1,0:T(8,128)}, f32[4,8,2048]{2,1,0:T(8,128)}) custom-call(bf16[4,64,2048]{2,1,0:T(8,128)(2,1)} %get-tuple-element.24.qt_ref.qt_hbm, bf16[4,4096,128]{2,1,0:T(8,128)(2,1)} %get-tuple-element.25.kn_ref, bf16[4,80,4096]{2,1,0:T(8,128)(2,1)} %get-tuple-element.26.kta_ref.kta_hbm, bf16[4,80,4096]{2,1,0:T(8,128)(2,1)} %get-tuple-element.27.vta_ref.vta_hbm), custom_call_target="tpu_custom_call" | custom-call | tf_op jit(solution)/shard_map/attend/pallas_call | solution.py:410
  70.9 0.0 collective-permute-done.far_hbm
  70.9 0.0 copy-start
  70.9 0.0 all-gather.2.cloned.1.call-done.w_hbm
  70.9 0.9 copy-done
  71.8 106.5 %back.1 = (bf16[2,1024,256]{2,1,0:T(8,128)(2,1)}, bf16[2,1024,256]{2,1,0:T(8,128)(2,1)}, f32[96,256]{1,0:T(8,128)}, f32[8,128]{1,0:T(8,128)}) custom-call(f32[4,64,2048]{2,1,0:T(8,128)} %get-tuple-element.28.att_hbm, f32[4,8,2048]{2,1,0:T(8,128)} %get-tuple-element.29.lse_hbm, bf16[4,64,2048]{2,1,0:T(8,128)(2,1)} %get-tuple-element.24.qt_ref.qt_hbm, ...), custom_call_target="tpu_custom_call" | custom-call | tf_op jit(solution)/shard_map/back/pallas_call | solution.py:848
  178.4 2.5 %publish.1 = (bf16[2,1024,256]{2,1,0:T(8,128)(2,1)}, bf16[2,1024,256]{2,1,0:T(8,128)(2,1)}, f32[96,256]{1,0:T(8,128)}, f32[8,128]{1,0:T(8,128)}) custom-call(bf16[2,1024,256]{2,1,0:T(8,128)(2,1)} %get-tuple-element.34.grad_ref, bf16[2,1024,256]{2,1,0:T(8,128)(2,1)} %get-tuple-element.35.out_ref, f32[96,256]{1,0:T(8,128)} %get-tuple-element.36.mats_ref, ...), custom_call_target="tpu_custom_call" | custom-call | tf_op jit(solution)/shard_map/publish/pallas_call | solution.py:911
  180.8 1.2 slice_bitcast_fusion
Async XLA Ops:
  7.2 63.7 %all-gather.2.cloned.1.call-start = ((), (), s32[]{:S(2)}) async-start(), calls=%async_computation | async-start | bytes 1622016 | tf_op jit(solution)/shard_map/all_gather | solution.py:930
  37.2 33.6 %collective-permute-start = (bf16[2,1024,256]{2,1,0:T(8,128)(2,1)}, bf16[2,1024,256]{2,1,0:T(8,128)(2,1)S(1)}, u32[]{:S(2)}, u32[]{:S(2)}) collective-permute-start(bf16[2,1024,256]{2,1,0:T(8,128)(2,1)} %near_hbm), channel_id=1, source_target_pairs={{0,2},{1,3},{2,0},{3,1},{4,6},{5,7},{6,4},{7,5},{8,10},{9,11},{10,... | collective-permute-start | bytes 3145736 | tf_op jit(solution)/shard_map/ppermute | solution.py:934
  70.9 1.0 copy-start
Sparse Core Ops, SparseCore 0:
  10.9 59.9 all-gather.1
